TPU v7x, 128 devices: a whole 4x4x4 slice. The times are simulated.
128 devices in a mesh: dp: 8 (over x, core), seq: 16 (over y, z).
Axes of the slice: x: 4, y: 4, z: 4, core: 2. Of those that a mesh axis runs over, the one named last changes fastest.
Arguments:
- inputs: bfloat16 [16, 3072, 1024], P('dp', 'seq'), may hold values from -6 to 6
- first_gain: float32 [1024], replicated, may hold values from 0.1 to 1.9
- first_shift: float32 [1024], replicated, may hold values from -3 to 3
- qkv_weight: bfloat16 [1024, 3072], replicated, may hold values from -0.1875 to 0.1875
- out_weight: bfloat16 [1024, 1024], replicated, may hold values from -4 to 4
- second_gain: float32 [1024], replicated, may hold values from 0.1 to 1.9
- second_shift: float32 [1024], replicated, may hold values from -3 to 3
- up_weight: bfloat16 [1024, 4096], replicated, may hold values from -0.1875 to 0.1875
- down_weight: bfloat16 [4096, 1024], replicated, may hold values from -0.09375 to 0.09375
- cotangent: bfloat16 [16, 3072, 1024], P('dp', 'seq'), may hold values from -6 to 6
Outputs:
- output: bfloat16 [16, 3072, 1024], P('dp', 'seq')
- grad_input: float32 [16, 3072, 1024], P('dp', 'seq')
- grad_qkv: float32 [1024, 3072], P(('dp', 'seq'))
- grad_out: float32 [1024, 1024], P(('dp', 'seq'))
- grad_up: float32 [1024, 4096], P(('dp', 'seq'))
- grad_down: float32 [4096, 1024], P(('dp', 'seq'))
- grad_first_gain: float32 [1024], P(('dp', 'seq'))
- grad_first_shift: float32 [1024], P(('dp', 'seq'))
- grad_second_gain: float32 [1024], P(('dp', 'seq'))
- grad_second_shift: float32 [1024], P(('dp', 'seq'))
All inputs are finite; a program needn't handle non-finite values.
Results may differ from a plain program's by a relative error of at most 0.0065.
Values sent between devices are 32-bit elements; how exact they have to be, the bound alone decides.
A program may use at most 192 MiB of HBM per device.

v0:
```python
import math

import jax
import jax.numpy as jnp
from jax import lax
from jax.sharding import PartitionSpec as P

HEADS = 16


highest = lax.Precision.HIGHEST


def carried_in(shard, axis, combine, identity, reverse):
    devices, place = (lax.axis_size(axis), lax.axis_index(axis))
    everything = jax.tree.map(lambda part: lax.all_gather(part, axis), shard)
    start = jax.tree.map(
        lambda part, zero: jnp.broadcast_to(jnp.asarray(zero, part.dtype), part.shape),
        shard,
        identity,
    )

    def lap(k, before):
        at = devices - 1 - k if reverse else k
        reached = at > place if reverse else at < place
        new = combine(before, jax.tree.map(lambda part: part[at], everything))
        return jax.tree.map(lambda a, b: jnp.where(reached, a, b), new, before)

    return lax.fori_loop(0, devices, lap, start)


def rounded(values):
    return lax.optimization_barrier(values.astype(jnp.bfloat16)).astype(jnp.float32)


def layer_norm(values, gain, shift):
    center = jnp.mean(values, axis=-1, keepdims=True)
    centered = values - center
    variance = jnp.mean(centered * centered, axis=-1, keepdims=True)
    inverse = lax.rsqrt(variance + 1e-05)
    scaled = centered * inverse
    return (scaled * gain + shift, scaled, inverse)


def norm_back(grad_out, gain, scaled, inverse):
    grad_scaled = grad_out * gain
    first_mean = jnp.mean(grad_scaled, axis=-1, keepdims=True)
    second_mean = jnp.mean(grad_scaled * scaled, axis=-1, keepdims=True)
    return inverse * (grad_scaled - first_mean - scaled * second_mean)


def rows_dot(left, right):
    return lax.dot_general(
        left, right, (((0,), (0,)), ((), ())), preferred_element_type=jnp.float32
    )


def back_dot(left, right):
    return lax.dot_general(
        left, right, (((1,), (1,)), ((), ())), preferred_element_type=jnp.float32
    )


def add_pair(earlier, later):
    return (earlier[0] + later[0], earlier[1] + later[1])


def body(
    inputs,
    first_gain,
    first_shift,
    qkv_weight,
    out_weight,
    second_gain,
    second_shift,
    up_weight,
    down_weight,
    cotangent,
):
    seq_count, block_len, width = inputs.shape
    head_size = width // HEADS
    row_count = seq_count * block_len
    flat_input = inputs.astype(jnp.float32).reshape(row_count, width)
    normed, scaled_one, inverse_one = layer_norm(flat_input, first_gain, first_shift)
    normed_low = normed.astype(jnp.bfloat16)
    qkv_low = jnp.dot(normed_low, qkv_weight, preferred_element_type=jnp.float32).astype(
        jnp.bfloat16
    )
    qkv_wide = qkv_low.astype(jnp.float32).reshape(seq_count, block_len, 3, HEADS, head_size)
    queries = qkv_wide[:, :, 0]
    keys = qkv_wide[:, :, 1]
    values = qkv_wide[:, :, 2]
    feat_query = rounded(jax.nn.elu(queries) + 1.0)
    feat_key = rounded(jax.nn.elu(keys) + 1.0)
    causal = (
        lax.broadcasted_iota(jnp.int32, (block_len, block_len), 0)
        >= lax.broadcasted_iota(jnp.int32, (block_len, block_len), 1)
    ).astype(jnp.float32)
    scores = jnp.einsum("nthe,nshe->nhts", feat_query, feat_key, precision=highest) * causal
    numer_local = jnp.einsum("nhts,nshf->nthf", scores, values, precision=highest)
    denom_local = jnp.transpose(jnp.sum(scores, axis=-1), (0, 2, 1))
    state_local = jnp.einsum("nshe,nshf->nhef", feat_key, values, precision=highest)
    total_local = jnp.sum(feat_key, axis=1)
    state_in, total_in = carried_in(
        (state_local, total_local),
        "seq",
        add_pair,
        (jnp.zeros_like(state_local), jnp.zeros_like(total_local)),
        False,
    )
    numer = numer_local + jnp.einsum("nthe,nhef->nthf", feat_query, state_in, precision=highest)
    denom = denom_local + jnp.einsum("nthe,nhe->nth", feat_query, total_in, precision=highest)
    attended = numer / denom[..., None]
    attended_low = attended.reshape(row_count, width).astype(jnp.bfloat16)
    mixed = flat_input + jnp.dot(attended_low, out_weight, preferred_element_type=jnp.float32)
    normed_two, scaled_two, inverse_two = layer_norm(mixed, second_gain, second_shift)
    normed_two_low = normed_two.astype(jnp.bfloat16)
    pre_act = jnp.dot(normed_two_low, up_weight, preferred_element_type=jnp.float32)
    hidden_low = jax.nn.gelu(pre_act, approximate=False).astype(jnp.bfloat16)
    result = mixed + jnp.dot(hidden_low, down_weight, preferred_element_type=jnp.float32)
    output = result.astype(jnp.bfloat16).reshape(seq_count, block_len, width)
    grad_result = cotangent.reshape(row_count, width)
    grad_down = rows_dot(hidden_low, grad_result)
    grad_hidden = back_dot(grad_result, down_weight)
    cumulative = 0.5 * (1.0 + lax.erf(pre_act * (1.0 / math.sqrt(2.0))))
    density = jnp.exp(-0.5 * pre_act * pre_act) * (1.0 / math.sqrt(2.0 * math.pi))
    grad_pre_low = (grad_hidden * (cumulative + pre_act * density)).astype(jnp.bfloat16)
    grad_up = rows_dot(normed_two_low, grad_pre_low)
    grad_normed_two = back_dot(grad_pre_low, up_weight)
    grad_second_gain = jnp.sum(grad_normed_two * scaled_two, axis=0)
    grad_second_shift = jnp.sum(grad_normed_two, axis=0)
    grad_mixed = grad_result.astype(jnp.float32) + norm_back(
        grad_normed_two, second_gain, scaled_two, inverse_two
    )
    grad_mixed_low = grad_mixed.astype(jnp.bfloat16)
    grad_out = rows_dot(attended_low, grad_mixed_low)
    grad_att = back_dot(grad_mixed_low, out_weight).reshape(seq_count, block_len, HEADS, head_size)
    grad_numer = grad_att / denom[..., None]
    grad_denom = -jnp.sum(grad_att * attended, axis=-1) / denom
    mixing = (
        jnp.einsum("nthf,nshf->nhts", grad_numer, values, precision=highest)
        + jnp.transpose(grad_denom, (0, 2, 1))[..., None]
    ) * causal
    grad_query = (
        jnp.einsum("nhts,nshe->nthe", mixing, feat_key, precision=highest)
        + jnp.einsum("nthf,nhef->nthe", grad_numer, state_in, precision=highest)
        + grad_denom[..., None] * total_in[:, None]
    )
    grad_state_in = jnp.einsum("nthe,nthf->nhef", feat_query, grad_numer, precision=highest)
    grad_total_in = jnp.einsum("nthe,nth->nhe", feat_query, grad_denom, precision=highest)
    grad_state, grad_total = carried_in(
        (grad_state_in, grad_total_in),
        "seq",
        add_pair,
        (jnp.zeros_like(grad_state_in), jnp.zeros_like(grad_total_in)),
        True,
    )
    grad_key = (
        jnp.einsum("nhts,nthe->nshe", mixing, feat_query, precision=highest)
        + jnp.einsum("nshf,nhef->nshe", values, grad_state, precision=highest)
        + grad_total[:, None]
    )
    grad_value = jnp.einsum("nhts,nthf->nshf", scores, grad_numer, precision=highest) + jnp.einsum(
        "nshe,nhef->nshf", feat_key, grad_state, precision=highest
    )
    grad_query = grad_query * jnp.where(queries > 0, 1.0, jnp.exp(jnp.minimum(queries, 0.0)))
    grad_key = grad_key * jnp.where(keys > 0, 1.0, jnp.exp(jnp.minimum(keys, 0.0)))
    grad_qkv_low = (
        jnp.stack([grad_query, grad_key, grad_value], axis=2)
        .reshape(row_count, 3 * width)
        .astype(jnp.bfloat16)
    )
    grad_qkv = rows_dot(normed_low, grad_qkv_low)
    grad_normed = back_dot(grad_qkv_low, qkv_weight)
    grad_first_gain = jnp.sum(grad_normed * scaled_one, axis=0)
    grad_first_shift = jnp.sum(grad_normed, axis=0)
    grad_input = (grad_mixed + norm_back(grad_normed, first_gain, scaled_one, inverse_one)).reshape(
        seq_count, block_len, width
    )
    summed = (
        lax.psum_scatter(grad_qkv, ("dp", "seq"), scatter_dimension=0, tiled=True),
        lax.psum_scatter(grad_out, ("dp", "seq"), scatter_dimension=0, tiled=True),
        lax.psum_scatter(grad_up, ("dp", "seq"), scatter_dimension=0, tiled=True),
        lax.psum_scatter(grad_down, ("dp", "seq"), scatter_dimension=0, tiled=True),
        lax.psum_scatter(grad_first_gain, ("dp", "seq"), scatter_dimension=0, tiled=True),
        lax.psum_scatter(grad_first_shift, ("dp", "seq"), scatter_dimension=0, tiled=True),
        lax.psum_scatter(grad_second_gain, ("dp", "seq"), scatter_dimension=0, tiled=True),
        lax.psum_scatter(grad_second_shift, ("dp", "seq"), scatter_dimension=0, tiled=True),
    )
    return (
        output,
        grad_input,
        summed[0],
        summed[1],
        summed[2],
        summed[3],
        summed[4],
        summed[5],
        summed[6],
        summed[7],
    )


def solution(mesh):
    return jax.shard_map(
        body,
        mesh=mesh,
        in_specs=(
            P("dp", "seq", None),
            P(),
            P(),
            P(),
            P(),
            P(),
            P(),
            P(),
            P(),
            P("dp", "seq", None),
        ),
        out_specs=(
            P("dp", "seq", None),
            P("dp", "seq", None),
            P(("dp", "seq"), None),
            P(("dp", "seq"), None),
            P(("dp", "seq"), None),
            P(("dp", "seq"), None),
            P(("dp", "seq")),
            P(("dp", "seq")),
            P(("dp", "seq")),
            P(("dp", "seq")),
        ),
        check_vma=False,
    )
```

profile of v0, /device:TPU:0, one launch (start us, length us, event | category | flops | bytes accessed | tf_op | source)
XLA Modules:
  0.0 2600.7 jit_solution(8741896087510281200)
XLA Ops:
  25.3 7.2 copy.45
  41.3 28.0 %all-gather.1 = f32[32,16,64]{2,1,0:T(8,128)} all-gather(f32[2,16,64]{2,1,0:T(8,128)S(1)} %convert_reduce_fusion), channel_id=3, replica_groups=mesh['dp'=8,'seq'=16] {'seq'}, dimensions={0}, use_global_device_ids=true | all-gather | bytes 139264 | tf_op jit(solution)/shard_map/all_gather | solution.py:16
  74.3 81.6 %all-gather.7.cloned.1.call-done = f32[32,16,64,64]{3,2,1,0:T(8,128)} async-done(((f32[2,16,64,64]{3,2,1,0:T(8,128)}), f32[32,16,64,64]{3,2,1,0:T(8,128)}) %all-gather.7.cloned.1.call-update) | async-done | bytes 8388624 | tf_op jit(solution)/shard_map/all_gather | solution.py:16
  155.9 56.8 %while.34 = (s32[]{:T(128)}, f32[2,16,64,64]{3,2,1,0:T(8,128)}, f32[2,16,64]{2,1,0:T(8,128)S(1)}, s32[]{:T(128)}, f32[16,2,16,64,64]{4,3,2,1,0:T(8,128)}, /*index=5*/f32[16,2,16,64]{3,2,1,0:T(8,128)}, s32[]{:T(128)}, s32[]{:T(128)}) while((s32[]{:T(128)}, f32[2,16,64,64]{3,2,1,0:T(8,128)}, f32[2,16,64]{2,1,0:T(8,128)S(1)}, ...), condition=%wide.region_4.5_spmd.clone, body=%wide.region_3.4_spmd.clone.sunk | while | flops 399364 | bytes 1597563 | solution.py:29
  217.1 7.3 fusion.75
  233.0 21.3 fusion.2
  254.4 8.4 fusion.8
  285.1 25.9 all-gather.3
  317.7 7.2 fusion.61
  325.0 8.5 fusion.32
  333.5 57.8 %all-gather.9.cloned.1.call-done = f32[32,16,64,64]{3,2,1,0:T(8,128)} async-done(((f32[2,16,64,64]{3,2,1,0:T(8,128)}), f32[32,16,64,64]{3,2,1,0:T(8,128)}) %all-gather.9.cloned.1.call-update) | async-done | bytes 8388624 | tf_op jit(solution)/shard_map/all_gather | solution.py:16
  391.3 37.5 %while.35 = (s32[]{:T(128)}, f32[2,16,64,64]{3,2,1,0:T(8,128)S(1)}, f32[2,16,64]{2,1,0:T(8,128)S(1)}, s32[]{:T(128)}, f32[16,2,16,64,64]{4,3,2,1,0:T(8,128)}, /*...) while((s32[]{:T(128)}, f32[2,16,64,64]{3,2,1,0:T(8,128)S(1)}, ...), condition=%wide.region_12.13_spmd.clone, body=%wide.region_11.12_spmd.clone.sunk | while | flops 399368 | bytes 1597625 | solution.py:29
  432.3 7.8 fusion.37
  452.6 7.5 convert_element_type.87
  460.0 8.0 fusion.80
  469.4 10.1 fusion.71
  480.7 10.3 fusion.81
  491.1 8.8 add_convert_fusion
  500.0 7.0 fusion.59
  507.0 65.7 %all-reduce.4 = (f32[1024]{0:T(1024)S(1)}, f32[1024]{0:T(1024)S(1)}, f32[1024]{0:T(1024)S(1)}, f32[1024]{0:T(1024)S(1)}) all-reduce(f32[1024]{0:T(1024)S(1)} %get-tuple-element.323, f32[1024]{0:T(1024)S(1)} %get-tuple-element.328, f32[1024]{0:T(1024)S(1)} %copy-done.30, ...), channel_id=10, replica_groups=mesh['dp'=8,'seq'=16] {'dp','seq'}, use_global_device_ids=true, to_apply=%region_20.21.clone | all-reduce | flops 4096 | bytes 32768
  578.8 458.7 %reduce-scatter.7.cloned.1.call-done = f32[8,1024]{1,0:T(8,128)} async-done(((f32[1024,1024]{1,0:T(8,128)}), f32[8,1024]{1,0:T(8,128)}) %reduce-scatter.7.cloned.1.call-update) | async-done | bytes 32784 | tf_op jit(solution)/shard_map/reduce_scatter | solution.py:182
  1037.5 222.2 %reduce-scatter.5.cloned.1.call-done = f32[8,3072]{1,0:T(8,128)} async-done(((f32[1024,3072]{1,0:T(8,128)}), f32[8,3072]{1,0:T(8,128)}) %reduce-scatter.5.cloned.1.call-update) | async-done | bytes 98320 | tf_op jit(solution)/shard_map/reduce_scatter | solution.py:181
  1259.7 668.8 %reduce-scatter.9.cloned.1.call-done = f32[8,4096]{1,0:T(8,128)} async-done(((f32[1024,4096]{1,0:T(8,128)}), f32[8,4096]{1,0:T(8,128)}) %reduce-scatter.9.cloned.1.call-update) | async-done | bytes 131088 | tf_op jit(solution)/shard_map/reduce_scatter | solution.py:183
  1928.5 665.1 %reduce-scatter.11.cloned.1.call-done = f32[32,1024]{1,0:T(8,128)} async-done(((f32[4096,1024]{1,0:T(8,128)}), f32[32,1024]{1,0:T(8,128)}) %reduce-scatter.11.cloned.1.call-update) | async-done | bytes 131088 | tf_op jit(solution)/shard_map/reduce_scatter | solution.py:184
  (203 shorter events, 192.0 us)
Async XLA Ops:
  7.2 222.8 %copy-start = (bf16[1024,1024]{1,0:T(8,128)(2,1)S(1)}, bf16[1024,1024]{1,0:T(8,128)(2,1)}, u32[]{:S(2)}) copy-start(bf16[1024,1024]{1,0:T(8,128)(2,1)} %param.18) | copy-start | bytes 6291460
  7.2 148.7 %all-gather.7.cloned.1.call-start = ((), (), s32[]{:S(2)}) async-start(), calls=%async_computation.8 | async-start | bytes 17825792 | tf_op jit(solution)/shard_map/all_gather | solution.py:16
  10.3 8.3 copy-start.25
  10.4 8.2 copy-start.27
  40.9 350.4 %all-gather.9.cloned.1.call-start = ((), (), s32[]{:S(2)}) async-start(), calls=%async_computation.9 | async-start | bytes 17825792 | tf_op jit(solution)/shard_map/all_gather | solution.py:16
  230.0 32.7 %slice-start.2 = ((s8[8388608]{0:T(1024)(128)(4,1)}), s8[4194304]{0:T(1024)(128)(4,1)S(1)}, s32[]{:S(2)}) async-start(s8[8388608]{0:T(1024)(128)(4,1)} %bitcast.158), calls=%async_computation.12 | async-start | bytes 8388608
  232.6 34.5 %copy-start.10 = (f32[384,1024]{1,0:T(8,128)}, f32[384,1024]{1,0:T(8,128)S(1)}, u32[]{:S(2)}) copy-start(f32[384,1024]{1,0:T(8,128)S(1)} %get-tuple-element.364) | copy-start | bytes 4718596
  233.0 21.4 copy-start.17
  233.0 29.7 %slice-start.3 = ((s8[8388608]{0:T(1024)(128)(4,1)}), s8[4194304]{0:T(1024)(128)(4,1)S(1)}, s32[]{:S(2)}) async-start(s8[8388608]{0:T(1024)(128)(4,1)} %bitcast.158), calls=%async_computation.13 | async-start | bytes 8388608
  278.9 758.6 %reduce-scatter.7.cloned.1.call-start = ((), (), s32[]{:S(2)}) async-start(), calls=%async_computation.5 | async-start | bytes 4227072 | tf_op jit(solution)/shard_map/reduce_scatter | solution.py:182
  281.4 29.7 %copy-start.2 = (f32[2,16,64,64]{3,2,1,0:T(8,128)S(1)}, f32[2,16,64,64]{3,2,1,0:T(8,128)}, u32[]{:S(2)}) copy-start(f32[2,16,64,64]{3,2,1,0:T(8,128)} %get-tuple-element.275) | copy-start | bytes 1572868
  281.4 29.7 %copy-start.5 = (f32[2,192,16,64]{1,0,3,2:T(2,128)S(1)}, f32[2,192,16,64]{1,0,3,2:T(2,128)}, u32[]{:S(2)}) copy-start(f32[2,192,16,64]{1,0,3,2:T(2,128)} %copy-done.4) | copy-start | bytes 4718596
  325.0 934.8 %reduce-scatter.5.cloned.1.call-start = ((), (), s32[]{:S(2)}) async-start(), calls=%async_computation.4 | async-start | bytes 12681216 | tf_op jit(solution)/shard_map/reduce_scatter | solution.py:181
  429.9 10.2 slice-start
  432.3 7.8 slice-start.1
  432.3 7.8 copy-start.6
  468.0 1460.5 %reduce-scatter.9.cloned.1.call-start = ((), (), s32[]{:S(2)}) async-start(), calls=%async_computation.6 | async-start | bytes 16908288 | tf_op jit(solution)/shard_map/reduce_scatter | solution.py:183
  479.6 2114.0 %reduce-scatter.11.cloned.1.call-start = ((), (), s32[]{:S(2)}) async-start(), calls=%async_computation.7 | async-start | bytes 16908288 | tf_op jit(solution)/shard_map/reduce_scatter | solution.py:184
  491.1 8.9 copy-start.7
  491.1 8.8 copy-start.15
  491.1 8.8 copy-start.24
  491.1 8.8 copy-start.26
  491.1 8.8 copy-start.28
  575.1 2018.6 %copy-start.1 = (bf16[1024,1024]{1,0:T(8,128)(2,1)S(1)}, bf16[1024,1024]{1,0:T(8,128)(2,1)}, u32[]{:S(2)}) copy-start(bf16[1024,1024]{1,0:T(8,128)(2,1)} %param.18) | copy-start | bytes 6291460
  (18 other events, 71.7 us)
Sparse Core Ops, SparseCore 0:
  41.0 114.7 all-gather.6
  279.0 112.2 all-gather.8
  394.2 643.2 reduce-scatter.6
  1043.7 216.0 reduce-scatter.4
  1262.7 665.8 reduce-scatter.8
  1931.5 662.1 reduce-scatter.10
where the time goes:
time: 2610 us; the launch traced here: 2600 us
  waiting for transfers between devices  2150 us (82%)
  matrix products  155 us (6%)
  blocking collectives  120 us (5%)
  other arithmetic  115 us (4%)
  local copies, waits for them, and re-layouts  41.4 us (2%)
    reduce_scatter x1, waiting for transfers between devices, body(): lax.psum_scatter(grad_up, ('dp', 'seq'), scatter_dimension=0, tiled=True)  669 us
    reduce_scatter x1, waiting for transfers between devices, body(): lax.psum_scatter(grad_down, ('dp', 'seq'), scatter_dimension=0, tiled=True)  665 us
    reduce_scatter x1, waiting for transfers between devices, body(): lax.psum_scatter(grad_out, ('dp', 'seq'), scatter_dimension=0, tiled=True)  459 us
    reduce_scatter x1, waiting for transfers between devices, body(): lax.psum_scatter(grad_qkv, ('dp', 'seq'), scatter_dimension=0, tiled=True)  222 us
    all_gather x2, waiting for transfers between devices, carried_in(): everything = jax.tree.map(lambda part: lax.all_gather(part, axis), shard)  139 us
    select_n x64, other arithmetic, lap(): return jax.tree.map(lambda a, b: jnp.where(reached, a, b), new, before)  93.9 us
    unnamed x1, blocking collectives  65.7 us
    all_gather x2, blocking collectives, carried_in(): everything = jax.tree.map(lambda part: lax.all_gather(part, axis), shard)  53.9 us
  transfers between devices with their start and end apart: 6, of which 6 were waited for; matrix products, arithmetic and copies ran while one was open for 6% of the time, Pallas kernels for 0%

commit v1 on v0

--- a/solution.py
+++ b/solution.py
@@ -3,14 +3,361 @@
 import jax
 import jax.numpy as jnp
 from jax import lax
+from jax.experimental import pallas as pl
+from jax.experimental.pallas import tpu as pltpu
 from jax.sharding import PartitionSpec as P
 
 HEADS = 16
-
+MESH = pl.DeviceIdType.MESH
+F32 = jnp.float32
+BF16 = jnp.bfloat16
+RING = 4
+MIB = 2**20
 
 highest = lax.Precision.HIGHEST
 
 
+class Place:
+    def __init__(self):
+        dp, seq = lax.axis_index("dp"), lax.axis_index("seq")
+        self.core = lax.rem(dp, 2)
+        self.at = (lax.div(dp, 2), lax.div(seq, RING), lax.rem(seq, RING))
+
+    def id_of(self, x, y, z, core):
+        return (x * 2 + core, y * RING + z)
+
+    def ring(self, axis, step):
+        return lax.rem(self.at[axis] + (step + RING), RING)
+
+    def neighbour(self, axis, step):
+        at = list(self.at)
+        at[axis] = self.ring(axis, step)
+        return self.id_of(*at, self.core)
+
+    def partner(self):
+        return self.id_of(*self.at, 1 - self.core)
+
+
+def greet(place):
+    barrier = pltpu.get_barrier_semaphore()
+    others = [place.neighbour(axis, step) for axis in range(3) for step in (1, -1)]
+    others.append(place.partner())
+    for other in others:
+        pl.semaphore_signal(barrier, inc=1, device_id=other, device_id_type=MESH)
+    pl.semaphore_wait(barrier, len(others))
+
+
+ORDERS = ((0, 1, 2), (1, 2, 0), (2, 0, 1))
+MESSAGES = 18
+
+
+def stream_scratch(length):
+    wide = (length // 256) * 128 + (128 if (length // 128) % 2 else 0)
+    return [
+        pltpu.VMEM((2, 4, 4, 8, length), F32),
+        pltpu.VMEM((2, 2, 4, 8, length), F32),
+        pltpu.VMEM((2, 4, 8, length), F32),
+        pltpu.VMEM((2, 2, 8, length), F32),
+        pltpu.VMEM((2, 8, length), F32),
+        pltpu.VMEM((2, 8, wide), F32),
+        pltpu.SemaphoreType.DMA((MESSAGES,)),
+        pltpu.SemaphoreType.DMA((MESSAGES,)),
+    ]
+
+
+class Stream:
+    def __init__(self, place, slab, order, scratch):
+        self.place, self.slab, self.order = place, slab, order
+        self.full = (scratch[0], scratch[2], scratch[4])
+        self.half = (scratch[1], scratch[3], scratch[5])
+        self.sent, self.came = scratch[6], scratch[7]
+        self.length = slab.shape[-1]
+        self.cut = scratch[5].shape[-1]
+        self.flying = []
+
+    def chunk(self, phase, target):
+        index = [slice(None)] * 3
+        for done in self.order[:phase]:
+            index[done] = self.place.at[done]
+        index[self.order[phase]] = target
+        return self.slab.at[tuple(index)]
+
+    def part(self, ref, phase, which):
+        if phase < 2:
+            return ref.at[pl.ds(2 * which, 2)]
+        if which == 0:
+            return ref.at[:, pl.ds(0, self.cut)]
+        return ref.at[:, pl.ds(self.cut, self.length - self.cut)]
+
+    def through(self, phase, way):
+        ref = self.half[phase].at[way]
+        if phase == 2 and way == 1:
+            return ref.at[:, pl.ds(0, self.length - self.cut)]
+        return ref
+
+    def send(self, phase, kind, way, source, target):
+        number = phase * 6 + kind * 2 + way
+        copy = pltpu.make_async_remote_copy(
+            src_ref=source,
+            dst_ref=target,
+            send_sem=self.sent.at[number],
+            recv_sem=self.came.at[number],
+            device_id=self.place.neighbour(self.order[phase], 1 - 2 * way),
+            device_id_type=MESH,
+        )
+        copy.start()
+        self.flying.append(copy)
+
+    def ring(self, phase, step):
+        return self.place.ring(self.order[phase], step)
+
+    def begin(self, phase):
+        opposite = self.chunk(phase, self.ring(phase, 2))
+        for way in range(2):
+            self.send(phase, 0, way, self.part(opposite, phase, way), self.through(phase, way))
+        for way in range(2):
+            beside = self.chunk(phase, self.ring(phase, 1 - 2 * way))
+            self.send(
+                phase,
+                1,
+                way,
+                self.part(beside, phase, 1 - way),
+                self.part(self.full[phase].at[way], phase, 1 - way),
+            )
+
+    def arrived(self, phase, kind, way, target):
+        number = phase * 6 + kind * 2 + way
+        pltpu.make_async_remote_copy(
+            src_ref=target,
+            dst_ref=target,
+            send_sem=self.sent.at[number],
+            recv_sem=self.came.at[number],
+            device_id=self.place.neighbour(self.order[phase], 2 * way - 1),
+            device_id_type=MESH,
+        ).wait_recv()
+
+    def forward(self, phase):
+        for way in range(2):
+            came = self.through(phase, way)
+            self.arrived(phase, 0, way, came)
+            own = self.part(self.chunk(phase, self.ring(phase, 1 - 2 * way)), phase, way)
+            add_into(own, came)
+            self.send(phase, 2, way, own, self.part(self.full[phase].at[way], phase, way))
+
+    def finish(self, phase):
+        own = self.chunk(phase, self.place.at[self.order[phase]])
+        for way in range(2):
+            for kind, which in ((1, 1 - way), (2, way)):
+                self.arrived(phase, kind, way, self.part(self.full[phase].at[way], phase, which))
+        add_into(own, self.full[phase].at[0], self.full[phase].at[1])
+
+    def result(self):
+        return self.slab.at[self.place.at]
+
+    def drain(self):
+        for copy in self.flying:
+            copy.wait_send()
+
+
+def add_into(own, *others):
+    if len(own.shape) > 2:
+
+        def row(index, carry):
+            add_into(own.at[index], *[other.at[index] for other in others])
+            return carry
+
+        if len(own.shape) == 4:
+            lax.fori_loop(0, own.shape[0], row, 0)
+        else:
+            for index in range(own.shape[0]):
+                row(index, 0)
+        return
+    total = own[...]
+    for other in others:
+        total = total + other[...]
+    own[...] = total
+
+
+def run_streams(streams):
+    for phase in range(3):
+        for stream in streams:
+            stream.begin(phase)
+        for stream in streams:
+            stream.forward(phase)
+        for stream in streams:
+            stream.finish(phase)
+
+
+def tn_dot(left, right):
+    return lax.dot_general(left, right, (((0,), (0,)), ((), ())), preferred_element_type=F32)
+
+
+class Exchange:
+    def __init__(self, place, sent, came):
+        self.place, self.sent, self.came, self.count, self.flying = place, sent, came, 0, []
+
+    def send(self, source, target):
+        copy = pltpu.make_async_remote_copy(
+            src_ref=source,
+            dst_ref=target,
+            send_sem=self.sent.at[self.count],
+            recv_sem=self.came.at[self.count],
+            device_id=self.place.partner(),
+            device_id_type=MESH,
+        )
+        copy.start()
+        self.count += 1
+        self.flying.append(copy)
+        return copy
+
+    def drain(self):
+        for copy in self.flying:
+            copy.wait_send()
+
+
+def half_columns(block, core, quarter):
+    half = quarter // 2
+    return pl.ds(pl.multiple_of(block * quarter + core * half, half), half)
+
+
+def stage_left(place, exchange, left, stage, land, pieces):
+    quarter = left.shape[1] // 4
+    copies = []
+    for block in range(4):
+        columns = pl.ds(block * quarter // 2, quarter // 2)
+        stage[:, columns] = left[:, half_columns(block, 1 - place.core, quarter)].astype(F32)
+        copies.append(exchange.send(stage.at[:, columns], land.at[:, columns]))
+    return copies
+
+
+def stage_right(exchange, right, stage, land, tile):
+    copies = []
+    for start in range(0, right.shape[1], tile):
+        columns = pl.ds(start, tile)
+        stage[:, columns] = right[:, columns].astype(F32)
+        copies.append(exchange.send(stage.at[:, columns], land.at[:, columns]))
+    return copies
+
+
+def gather_left(place, left, land, both, copies):
+    rows, quarter = left.shape[0], left.shape[1] // 4
+    for block in range(4):
+        columns = pl.ds(block * quarter // 2, quarter // 2)
+        both[pl.ds(0, rows), columns] = left[:, half_columns(block, place.core, quarter)]
+        copies[block].wait_recv()
+        both[pl.ds(rows, rows), columns] = land[:, columns].astype(BF16)
+
+
+def gather_right(right, land, both, copies, tile, index):
+    rows = right.shape[0]
+    columns = pl.ds(index * tile, tile)
+    both[pl.ds(0, rows), columns] = right[:, columns]
+    copies[index].wait_recv()
+    both[pl.ds(rows, rows), columns] = land[:, columns].astype(BF16)
+
+
+TILE = 512
+
+
+def down_kernel(left, right, out, stage_l, land_l, both_l, stage_r, land_r, both_r, sent, came, *rest):
+    place = Place()
+    greet(place)
+    slabs, scratch = rest[:3], rest[3:]
+    exchange = Exchange(place, sent, came)
+    right_copies = stage_right(exchange, right, stage_r, land_r, TILE)
+    left_copies = stage_left(place, exchange, left, stage_l, land_l, None)
+    for index in range(right.shape[1] // TILE):
+        gather_right(right, land_r, both_r, right_copies, TILE, index)
+    gather_left(place, left, land_l, both_l, left_copies)
+    cuts = ((0, 384), (384, 384), (768, 256))
+
+    def block_product(block, carry):
+        rows = both_l[:, pl.ds(pl.multiple_of(block * 512, 512), 512)]
+        for piece, (start, width) in enumerate(cuts):
+            product = tn_dot(rows, both_r[:, pl.ds(start, width)]).reshape(4, 4, 4, 8, width)
+            for stream in range(3):
+                slabs[stream][block, :, :, :, pl.ds(start, width)] = product[:, :, stream]
+            slabs[piece][block, :, :, :, pl.ds(1024, width)] = product[:, :, 3]
+        return carry
+
+    lax.fori_loop(0, 4, block_product, 0)
+    streams = [
+        Stream(place, slabs[k], ORDERS[k], scratch[8 * k : 8 * k + 8]) for k in range(3)
+    ]
+    run_streams(streams)
+    for stream in range(3):
+        result = streams[stream].result()
+        out[pl.ds(8 * stream, 8), :] = result[:, pl.ds(0, 1024)]
+        start, width = cuts[stream]
+        out[pl.ds(24, 8), pl.ds(start, width)] = result[:, pl.ds(1024, width)]
+    exchange.drain()
+    for stream in streams:
+        stream.drain()
+
+
+def wide_kernel(widths, left, right, out, stage_l, land_l, both_l, stage_r, land_r, both_r, sent, came, *rest):
+    place = Place()
+    greet(place)
+    slabs, scratch = rest[:3], rest[3:]
+    exchange = Exchange(place, sent, came)
+    left_copies = stage_left(place, exchange, left, stage_l, land_l, None)
+    right_copies = stage_right(exchange, right, stage_r, land_r, TILE)
+    gather_left(place, left, land_l, both_l, left_copies)
+    for index in range(right.shape[1] // TILE):
+        gather_right(right, land_r, both_r, right_copies, TILE, index)
+    starts = (0, widths[0], widths[0] + widths[1])
+    for stream in range(3):
+        for start in range(0, widths[stream], TILE):
+            width = min(TILE, widths[stream] - start)
+            product = tn_dot(both_l[...], both_r[:, pl.ds(starts[stream] + start, width)])
+            slabs[stream][:, :, :, :, pl.ds(start, width)] = product.reshape(4, 4, 4, 8, width)
+    streams = [
+        Stream(place, slabs[k], ORDERS[k], scratch[8 * k : 8 * k + 8]) for k in range(3)
+    ]
+    run_streams(streams)
+    for stream in range(3):
+        out[:, pl.ds(starts[stream], widths[stream])] = streams[stream].result()[...]
+    exchange.drain()
+    for stream in streams:
+        stream.drain()
+
+
+def grad_call(kernel, left, right, out_shape, widths, collective_id):
+    rows, half, columns = left.shape[0], left.shape[1] // 2, right.shape[1]
+    pieces = 4 + columns // TILE
+    vmem = pl.BlockSpec(memory_space=pltpu.VMEM)
+    return pl.pallas_call(
+        kernel,
+        out_shape=jax.ShapeDtypeStruct(out_shape, F32),
+        in_specs=[vmem, vmem],
+        out_specs=vmem,
+        scratch_shapes=[
+            pltpu.VMEM((rows, half), F32),
+            pltpu.VMEM((rows, half), F32),
+            pltpu.VMEM((2 * rows, half), BF16),
+            pltpu.VMEM((rows, columns), F32),
+            pltpu.VMEM((rows, columns), F32),
+            pltpu.VMEM((2 * rows, columns), BF16),
+            pltpu.SemaphoreType.DMA((pieces,)),
+            pltpu.SemaphoreType.DMA((pieces,)),
+            *[pltpu.VMEM((4, 4, 4, 8, width), F32) for width in widths],
+            *[item for width in widths for item in stream_scratch(width)],
+        ],
+        compiler_params=pltpu.CompilerParams(
+            collective_id=collective_id, has_side_effects=True, vmem_limit_bytes=62 * MIB
+        ),
+    )(left, right)
+
+
+def grad_down_sum(hidden, cotangent):
+    return grad_call(down_kernel, hidden, cotangent, (32, 1024), (1408, 1408, 1280), 1)
+
+
+def grad_wide_sum(left, right, widths, collective_id):
+    def kernel(*refs):
+        wide_kernel(widths, *refs)
+
+    return grad_call(kernel, left, right, (8, right.shape[1]), widths, collective_id)
 def carried_in(shard, axis, combine, identity, reverse):
     devices, place = (lax.axis_size(axis), lax.axis_index(axis))
     everything = jax.tree.map(lambda part: lax.all_gather(part, axis), shard)
@@ -120,12 +467,12 @@
     result = mixed + jnp.dot(hidden_low, down_weight, preferred_element_type=jnp.float32)
     output = result.astype(jnp.bfloat16).reshape(seq_count, block_len, width)
     grad_result = cotangent.reshape(row_count, width)
-    grad_down = rows_dot(hidden_low, grad_result)
+    grad_down = grad_down_sum(hidden_low, grad_result)
     grad_hidden = back_dot(grad_result, down_weight)
     cumulative = 0.5 * (1.0 + lax.erf(pre_act * (1.0 / math.sqrt(2.0))))
     density = jnp.exp(-0.5 * pre_act * pre_act) * (1.0 / math.sqrt(2.0 * math.pi))
     grad_pre_low = (grad_hidden * (cumulative + pre_act * density)).astype(jnp.bfloat16)
-    grad_up = rows_dot(normed_two_low, grad_pre_low)
+    grad_up = grad_wide_sum(normed_two_low, grad_pre_low, (1408, 1408, 1280), 2)
     grad_normed_two = back_dot(grad_pre_low, up_weight)
     grad_second_gain = jnp.sum(grad_normed_two * scaled_two, axis=0)
     grad_second_shift = jnp.sum(grad_normed_two, axis=0)
@@ -133,7 +480,7 @@
         grad_normed_two, second_gain, scaled_two, inverse_two
     )
     grad_mixed_low = grad_mixed.astype(jnp.bfloat16)
-    grad_out = rows_dot(attended_low, grad_mixed_low)
+    grad_out = grad_wide_sum(attended_low, grad_mixed_low, (384, 384, 256), 3)
     grad_att = back_dot(grad_mixed_low, out_weight).reshape(seq_count, block_len, HEADS, head_size)
     grad_numer = grad_att / denom[..., None]
     grad_denom = -jnp.sum(grad_att * attended, axis=-1) / denom
@@ -170,7 +517,7 @@
         .reshape(row_count, 3 * width)
         .astype(jnp.bfloat16)
     )
-    grad_qkv = rows_dot(normed_low, grad_qkv_low)
+    grad_qkv = grad_wide_sum(normed_low, grad_qkv_low, (1024, 1024, 1024), 4)
     grad_normed = back_dot(grad_qkv_low, qkv_weight)
     grad_first_gain = jnp.sum(grad_normed * scaled_one, axis=0)
     grad_first_shift = jnp.sum(grad_normed, axis=0)
@@ -178,10 +525,10 @@
         seq_count, block_len, width
     )
     summed = (
-        lax.psum_scatter(grad_qkv, ("dp", "seq"), scatter_dimension=0, tiled=True),
-        lax.psum_scatter(grad_out, ("dp", "seq"), scatter_dimension=0, tiled=True),
-        lax.psum_scatter(grad_up, ("dp", "seq"), scatter_dimension=0, tiled=True),
-        lax.psum_scatter(grad_down, ("dp", "seq"), scatter_dimension=0, tiled=True),
+        grad_qkv,
+        grad_out,
+        grad_up,
+        grad_down,
         lax.psum_scatter(grad_first_gain, ("dp", "seq"), scatter_dimension=0, tiled=True),
         lax.psum_scatter(grad_first_shift, ("dp", "seq"), scatter_dimension=0, tiled=True),
         lax.psum_scatter(grad_second_gain, ("dp", "seq"), scatter_dimension=0, tiled=True),

time: 2610 us -> 715 us (0.27)
  waiting for transfers between devices: 2150 us -> 82.9 us
  Pallas kernels: 0 us -> 250 us
  matrix products: 155 us -> 106 us
    reduce_scatter x4 -> x0, waiting for transfers between devices: 2010 us -> none  [the longest x1 669 us: body(): lax.psum_scatter(grad_up, ('dp', 'seq'), scatter_dimension=0, tiled=True)]
    pallas_call x0 -> x4, Pallas kernels: none -> 250 us  [grad_call(): pl.pallas_call(kernel, out_shape=jax.ShapeDtypeStruct(out_shape, F32), in...]
    all_gather x2, waiting for transfers between devices: 139 us -> 82.9 us  [carried_in(): everything = jax.tree.map(lambda part: lax.all_gather(part, axis), shard)]
    dot_general x4 -> x0, matrix products: 31.7 us -> none  [rows_dot(): lax.dot_general(left, right, (((0,), (0,)), ((), ())), preferred_element_...]
  transfers between devices with their start and end apart: 6 -> 2, of which waited for: 6 -> 1; matrix products, arithmetic and copies ran while one was open for 6% -> 4% of each run, Pallas kernels for 0% -> 28%
where the time goes in v1:
time: 715 us; the launch traced here: 706 us
  Pallas kernels  250 us (35%)
  blocking collectives  115 us (16%)
  matrix products  106 us (15%)
  other arithmetic  92.7 us (13%)
  waiting for transfers between devices  82.9 us (12%)
  local copies, waits for them, and re-layouts  43.8 us (6%)
  between operations  15 us (2%)
    pallas_call x4, Pallas kernels, grad_call(): pl.pallas_call(kernel, out_shape=jax.ShapeDtypeStruct(out_shape, F32), in...  250 us
    all_gather x2, waiting for transfers between devices, carried_in(): everything = jax.tree.map(lambda part: lax.all_gather(part, axis), shard)  82.9 us
    select_n x64, other arithmetic, lap(): return jax.tree.map(lambda a, b: jnp.where(reached, a, b), new, before)  74 us
    unnamed x1, blocking collectives  63 us
    all_gather x2, blocking collectives, carried_in(): everything = jax.tree.map(lambda part: lax.all_gather(part, axis), shard)  51.7 us
    dot_general x4, matrix products, back_dot(): lax.dot_general(left, right, (((1,), (1,)), ((), ())), preferred_element_...  20.4 us
    dot_general x1, matrix products, body(): jnp.dot(normed_two_low, up_weight, preferred_element_type=jnp.float32)  20.3 us
  transfers between devices with their start and end apart: 2, of which 1 were waited for; matrix products, arithmetic and copies ran while one was open for 4% of the time, Pallas kernels for 28%

profile of v1, /device:TPU:0, one launch (start us, length us, event | category | flops | bytes accessed | tf_op | source)
XLA Modules:
  0.0 705.9 jit_solution(8054035628774523877)
XLA Ops:
  11.7 5.9 convolution_convert_fusion
  17.6 4.7 reshape.137
  22.4 7.2 %copy.49 = bf16[2,192,3,16,64]{1,4,3,0,2:T(8,128)(2,1)} copy(bf16[2,192,3,16,64]{4,3,2,1,0:T(8,128)(2,1)} %reshape.137) | data formatting | bytes 4718592 | tf_op jit(solution)/shard_map/reshape | solution.py:436
  38.8 28.0 %all-gather.1 = f32[32,16,64]{2,1,0:T(8,128)} all-gather(f32[2,16,64]{2,1,0:T(8,128)S(1)} %convert_reduce_fusion), channel_id=3, replica_groups=mesh['dp'=8,'seq'=16] {'seq'}, dimensions={0}, use_global_device_ids=true | all-gather | bytes 139264 | tf_op jit(solution)/shard_map/all_gather | solution.py:363
  70.5 82.9 %all-gather.7.cloned.1.call-done = f32[32,16,64,64]{3,2,1,0:T(8,128)} async-done(((f32[2,16,64,64]{3,2,1,0:T(8,128)}), f32[32,16,64,64]{3,2,1,0:T(8,128)}) %all-gather.7.cloned.1.call-update) | async-done | bytes 8388624 | tf_op jit(solution)/shard_map/all_gather | solution.py:363
  153.4 37.4 %while.34 = (s32[]{:T(128)}, f32[2,16,64,64]{3,2,1,0:T(8,128)S(1)}, f32[2,16,64]{2,1,0:T(8,128)S(1)}, s32[]{:T(128)}, f32[16,2,16,64,64]{4,3,2,1,0:T(8,128)}, /*...) while((s32[]{:T(128)}, f32[2,16,64,64]{3,2,1,0:T(8,128)S(1)}, f32[2,16,64]{2,1,0:T(8,128)S(1)}, ...), condition=%wide.region_4.5_spmd.clone, body=%wide.region_3.4_spmd.clone.sunk | while | flops 399364 | bytes 1597563 | solution.py:376
  192.4 7.3 %fusion.71 = (bf16[2,192,16,64]{1,3,2,0:T(8,128)(2,1)S(1)}, f32[2,192,16,64]{1,3,2,0:T(8,128)}) fusion(f32[2,192,16]{1,2,0:T(8,128)S(1)} %fusion.67, f32[2,16,64,192]{3,2,1,0:T(8,128)S(1)} %fusion.73, f32[2,16,192,192]{2,3,1,0:T(8,128)} %get-tuple-element.362, f32[192,192]{0,1:T(8,128)S(1)} %fusion.64, bf16[2,192,3,16,64]{1,4,3,0,2:T(8,128)(2,1)} %copy.49), kind=kOutput, calls=%fused_computation.123 | convolution fusion | flops 908328960 | bytes 11444224 | tf_op jit(solution)/shard_map/nhts,nshf->nthf/dot_general | solution.py:447
  208.3 20.3 %fusion.2 = (bf16[384,4096]{1,0:T(8,128)(2,1)}, f32[384,4096]{1,0:T(8,128)S(1)}) fusion(bf16[384,1024]{1,0:T(8,128)(2,1)S(1)} %add_convert_fusion.2.refs_0_, bf16[1024,4096]{1,0:T(8,128)(2,1)} %param.21), kind=kOutput, calls=%fused_computation.8 | convolution fusion | flops 3323461632 | bytes 18612224 | tf_op jit(solution)/shard_map/dot_general | solution.py:465
  228.6 7.3 %fusion.8.refs_1_ = bf16[384,4096]{1,0:T(8,128)(2,1)S(1)} fusion(f32[384,4096]{1,0:T(8,128)S(1)} %get-tuple-element.368, bf16[384,1024]{1,0:T(8,128)(2,1)S(1)} %bitcast.152, bf16[4096,1024]{1,0:T(8,128)(2,1)} %param.22), kind=kOutput, calls=%fused_computation.14 | convolution fusion | flops 3236954112 | bytes 18612224 | tf_op jit(solution)/shard_map/dot_general | solution.py:406
  253.2 79.9 %shard_map.179 = f32[8,4096]{1,0:T(8,128)} custom-call(bf16[384,1024]{1,0:T(8,128)(2,1)} %copy-done.22, bf16[384,4096]{1,0:T(8,128)(2,1)} %copy-done.20), custom_call_target="tpu_custom_call" | custom-call | tf_op jit(solution)/shard_map/pallas_call | solution.py:329
  333.1 86.2 %shard_map.180 = f32[32,1024]{1,0:T(8,128)} custom-call(bf16[384,4096]{1,0:T(8,128)(2,1)} %get-tuple-element.367.left, bf16[384,1024]{1,0:T(8,128)(2,1)} %bitcast.151), custom_call_target="tpu_custom_call" | custom-call | tf_op jit(solution)/shard_map/pallas_call | solution.py:329
  419.3 32.2 %shard_map.178 = f32[8,1024]{1,0:T(8,128)} custom-call(bf16[384,1024]{1,0:T(8,128)(2,1)} %copy.64.refs_0_, bf16[384,1024]{1,0:T(8,128)(2,1)} %copy-done.21), custom_call_target="tpu_custom_call" | custom-call | tf_op jit(solution)/shard_map/pallas_call | solution.py:329
  455.3 23.7 %all-gather.3 = f32[32,16,64]{2,1,0:T(8,128)} all-gather(f32[2,16,64]{2,1,0:T(8,128)S(1)} %bitcast.160), channel_id=5, replica_groups=mesh['dp'=8,'seq'=16] {'seq'}, dimensions={0}, use_global_device_ids=true | all-gather | bytes 139264 | tf_op jit(solution)/shard_map/all_gather | solution.py:363
  481.1 4.3 fusion.62
  485.5 7.9 %fusion.60 = bf16[2,192,1,16,64]{1,4,3,0,2:T(8,128)(2,1)} fusion(f32[2,192,3,16,64]{1,4,3,0,2:T(8,128)} %copy-done.5, f32[2,16,64,192]{3,2,1,0:T(8,128)S(1)} %fusion.69, bf16[2,192,16,64]{1,3,2,0:T(8,128)(2,1)S(1)} %copy-done.2, f32[2,16,192,192]{2,3,1,0:T(8,128)S(1)} %fusion.62, f32[2,16,192]{2,1,0:T(8,128)S(1)} %bitcast_divide_fusion.1, ...), kind=kOutput, calls=%fused_computation.99 | convolution fusion | flops 911474688 | bytes 9641984 | tf_op jit(solution)/shard_map/nhts,nshe->nthe/dot_general | solution.py:492
  493.4 4.3 add_convert_fusion.1
  497.8 37.5 %while.35 = (s32[]{:T(128)}, f32[2,16,64,64]{3,2,1,0:T(8,128)S(1)}, f32[2,16,64]{2,1,0:T(8,128)S(1)}, s32[]{:T(128)}, f32[16,2,16,64,64]{4,3,2,1,0:T(8,128)}, /*...) while((s32[]{:T(128)}, f32[2,16,64,64]{3,2,1,0:T(8,128)S(1)}, ...), condition=%wide.region_12.13_spmd.clone, body=%wide.region_11.12_spmd.clone.sunk | while | flops 399368 | bytes 1597625 | solution.py:376
  538.8 9.4 %fusion.56 = bf16[2,192,1,16,64]{1,4,3,0,2:T(8,128)(2,1)S(1)} fusion(f32[2,16,64,192]{3,2,1,0:T(8,128)S(1)} %fusion.76, f32[2,16,192,192]{2,3,1,0:T(8,128)} %get-tuple-element.362, f32[192,192]{0,1:T(8,128)S(1)} %fusion.64, f32[2,192,16,64]{1,0,3,2:T(2,128)S(1)} %copy-done.8, f32[2,192,16]{1,2,0:T(8,128)S(1)} %fusion.67), kind=kOutput, calls=%fused_computation.97 | convolution fusion | flops 908328960 | bytes 8822784 | tf_op jit(solution)/shard_map/nhts,nthf->nshf/dot_general | solution.py:510
  548.2 6.0 fusion.59
  555.0 4.9 copy.62
  559.9 6.5 convert_element_type.70
  566.4 6.9 fusion.55
  576.1 51.2 %shard_map.177 = f32[8,3072]{1,0:T(8,128)} custom-call(bf16[384,1024]{1,0:T(8,128)(2,1)} %copy-done.18, bf16[384,3072]{1,0:T(8,128)(2,1)} %copy.63.refs_1_), custom_call_target="tpu_custom_call" | custom-call | tf_op jit(solution)/shard_map/pallas_call | solution.py:329
  627.3 63.0 %all-reduce.4 = (f32[1024]{0:T(1024)S(1)}, f32[1024]{0:T(1024)S(1)}, f32[1024]{0:T(1024)S(1)}, f32[1024]{0:T(1024)S(1)}) all-reduce(f32[1024]{0:T(1024)S(1)} %get-tuple-element.323, f32[1024]{0:T(1024)S(1)} %get-tuple-element.328, f32[1024]{0:T(1024)S(1)} %get-tuple-element.321, ...), channel_id=6, replica_groups=mesh['dp'=8,'seq'=16] {'dp','seq'}, use_global_device_ids=true, to_apply=%region_16.17.clone | all-reduce | flops 4096 | bytes 32768
  (202 shorter events, 139.9 us)
Async XLA Ops:
  7.2 146.2 %all-gather.7.cloned.1.call-start = ((), (), s32[]{:S(2)}) async-start(), calls=%async_computation | async-start | bytes 17825792 | tf_op jit(solution)/shard_map/all_gather | solution.py:363
  35.0 35.5 %copy-start.1 = (bf16[2,192,16,64]{1,3,2,0:T(8,128)(2,1)}, bf16[2,192,16,64]{1,3,2,0:T(8,128)(2,1)S(1)}, u32[]{:S(2)}) copy-start(bf16[2,192,16,64]{1,3,2,0:T(8,128)(2,1)S(1)} %get-tuple-element.360) | copy-start | bytes 2359300
  35.0 156.3 %copy-start.9 = (bf16[2,192,16,64]{1,3,2,0:T(8,128)(2,1)}, bf16[2,192,16,64]{1,3,2,0:T(8,128)(2,1)S(1)}, u32[]{:S(2)}) copy-start(bf16[2,192,16,64]{1,3,2,0:T(8,128)(2,1)S(1)} %get-tuple-element.359) | copy-start | bytes 2359300
  38.4 459.4 %all-gather.9.cloned.1.call-start = ((), (), s32[]{:S(2)}) async-start(), calls=%async_computation.1 | async-start | bytes 17825792 | tf_op jit(solution)/shard_map/all_gather | solution.py:363
  190.8 9.0 %copy-start.3 = (f32[2,16,64,64]{3,2,1,0:T(8,128)}, f32[2,16,64,64]{3,2,1,0:T(8,128)S(1)}, u32[]{:S(2)}) copy-start(f32[2,16,64,64]{3,2,1,0:T(8,128)S(1)} %get-tuple-element.275) | copy-start | bytes 1572868
  207.6 32.2 %copy-start.12 = (f32[384,1024]{1,0:T(8,128)}, f32[384,1024]{1,0:T(8,128)S(1)}, u32[]{:S(2)}) copy-start(f32[384,1024]{1,0:T(8,128)S(1)} %get-tuple-element.366) | copy-start | bytes 4718596
  207.6 28.3 %slice-start.2 = ((s8[8388608]{0:T(1024)(128)(4,1)}), s8[4194304]{0:T(1024)(128)(4,1)S(1)}, s32[]{:S(2)}) async-start(s8[8388608]{0:T(1024)(128)(4,1)} %bitcast.161), calls=%async_computation.4 | async-start | bytes 8388608
  208.3 20.3 %copy-start.22 = (bf16[384,1024]{1,0:T(8,128)(2,1)}, bf16[384,1024]{1,0:T(8,128)(2,1)S(1)}, u32[]{:S(2)}) copy-start(bf16[384,1024]{1,0:T(8,128)(2,1)S(1)} %add_convert_fusion.2.refs_0_) | copy-start | bytes 2359300
  208.3 20.3 %copy-start.23 = (bf16[2,192,1024]{2,1,0:T(8,128)(2,1)S(1)}, bf16[2,192,1024]{2,1,0:T(8,128)(2,1)}, u32[]{:S(2)}) copy-start(bf16[2,192,1024]{2,1,0:T(8,128)(2,1)} %param.23) | copy-start | bytes 2359300
  208.3 27.6 %slice-start.3 = ((s8[8388608]{0:T(1024)(128)(4,1)}), s8[4194304]{0:T(1024)(128)(4,1)S(1)}, s32[]{:S(2)}) async-start(s8[8388608]{0:T(1024)(128)(4,1)} %bitcast.161), calls=%async_computation.5 | async-start | bytes 8388608
  451.6 27.5 %copy-start.4 = (f32[2,16,64,64]{3,2,1,0:T(8,128)S(1)}, f32[2,16,64,64]{3,2,1,0:T(8,128)}, u32[]{:S(2)}) copy-start(f32[2,16,64,64]{3,2,1,0:T(8,128)} %copy-done.3) | copy-start | bytes 1572868
  451.6 27.5 %copy-start.7 = (f32[2,192,16,64]{1,0,3,2:T(2,128)S(1)}, f32[2,192,16,64]{1,0,3,2:T(2,128)}, u32[]{:S(2)}) copy-start(f32[2,192,16,64]{1,0,3,2:T(2,128)} %copy-done.6) | copy-start | bytes 4718596
  481.1 12.3 %slice-start.4 = ((s8[8388608]{0:T(1024)(128)(4,1)}), s8[4194304]{0:T(1024)(128)(4,1)S(1)}, s32[]{:S(2)}) async-start(s8[8388608]{0:T(1024)(128)(4,1)} %bitcast.163), calls=%async_computation.6 | async-start | bytes 8388608
  485.4 8.0 %copy-start = (f32[2,16,192,192]{2,3,1,0:T(8,128)}, f32[2,16,192,192]{2,3,1,0:T(8,128)S(1)}, u32[]{:S(2)}) copy-start(f32[2,16,192,192]{2,3,1,0:T(8,128)S(1)} %fusion.62) | copy-start | bytes 14155780
  485.4 8.0 %copy-start.13 = (f32[384,1024]{1,0:T(8,128)S(1)}, f32[384,1024]{1,0:T(8,128)}, u32[]{:S(2)}) copy-start(f32[384,1024]{1,0:T(8,128)} %copy-done.12) | copy-start | bytes 4718596
  485.4 8.0 %copy-start.19 = (bf16[384,4096]{1,0:T(8,128)(2,1)S(1)}, bf16[384,4096]{1,0:T(8,128)(2,1)}, u32[]{:S(2)}) copy-start(bf16[384,4096]{1,0:T(8,128)(2,1)} %get-tuple-element.367.left) | copy-start | bytes 9437188
  485.4 8.0 %slice-start.5 = ((s8[8388608]{0:T(1024)(128)(4,1)}), s8[4194304]{0:T(1024)(128)(4,1)S(1)}, s32[]{:S(2)}) async-start(s8[8388608]{0:T(1024)(128)(4,1)} %bitcast.163), calls=%async_computation.7 | async-start | bytes 8388608
  537.7 10.5 %slice-start = ((s8[6291456]{0:T(1024)(128)(4,1)}), s8[4194304]{0:T(1024)(128)(4,1)S(1)}, s32[]{:S(2)}) async-start(s8[6291456]{0:T(1024)(128)(4,1)} %bitcast.149), calls=%async_computation.2 | async-start | bytes 8388608
  538.7 9.4 %slice-start.1 = ((s8[6291456]{0:T(1024)(128)(4,1)}), s8[2097152]{0:T(1024)(128)(4,1)S(1)}, s32[]{:S(2)}) async-start(s8[6291456]{0:T(1024)(128)(4,1)} %bitcast.149), calls=%async_computation.3 | async-start | bytes 4194304
  559.9 6.5 copy-start.29
  627.3 69.0 %copy-start.27 = (f32[8,3072]{1,0:T(8,128)S(1)}, f32[8,3072]{1,0:T(8,128)}, u32[]{:S(2)}) copy-start(f32[8,3072]{1,0:T(8,128)} %shard_map.177) | copy-start | bytes 294916
  627.3 69.6 %copy-start.28 = (f32[8,1024]{1,0:T(8,128)S(1)}, f32[8,1024]{1,0:T(8,128)}, u32[]{:S(2)}) copy-start(f32[8,1024]{1,0:T(8,128)} %shard_map.178) | copy-start | bytes 98308
  627.3 70.2 %copy-start.25 = (f32[8,4096]{1,0:T(8,128)S(1)}, f32[8,4096]{1,0:T(8,128)}, u32[]{:S(2)}) copy-start(f32[8,4096]{1,0:T(8,128)} %shard_map.179) | copy-start | bytes 393220
  627.3 70.9 %copy-start.26 = (f32[32,1024]{1,0:T(8,128)S(1)}, f32[32,1024]{1,0:T(8,128)}, u32[]{:S(2)}) copy-start(f32[32,1024]{1,0:T(8,128)} %shard_map.180) | copy-start | bytes 393220
  (16 other events, 62.3 us)
Sparse Core Ops, SparseCore 0:
  38.5 114.8 all-gather.6
  251.0 152.4 all-gather.8

commit v2 on v1

--- a/solution.py
+++ b/solution.py
@@ -7,14 +7,11 @@
 from jax.experimental.pallas import tpu as pltpu
 from jax.sharding import PartitionSpec as P
 
-HEADS = 16
 MESH = pl.DeviceIdType.MESH
 F32 = jnp.float32
 BF16 = jnp.bfloat16
 RING = 4
 MIB = 2**20
-
-highest = lax.Precision.HIGHEST
 
 
 class Place:
@@ -358,26 +355,430 @@
         wide_kernel(widths, *refs)
 
     return grad_call(kernel, left, right, (8, right.shape[1]), widths, collective_id)
-def carried_in(shard, axis, combine, identity, reverse):
-    devices, place = (lax.axis_size(axis), lax.axis_index(axis))
-    everything = jax.tree.map(lambda part: lax.all_gather(part, axis), shard)
-    start = jax.tree.map(
-        lambda part, zero: jnp.broadcast_to(jnp.asarray(zero, part.dtype), part.shape),
-        shard,
-        identity,
+
+SEQ = 16
+PAIR = 128
+NT = (((1,), (1,)), ((), ()))
+TN = (((0,), (0,)), ((), ()))
+
+
+def dot_nt(left, right):
+    return lax.dot_general(left, right, NT, preferred_element_type=F32)
+
+
+def dot_nn(left, right):
+    return jnp.dot(left, right, preferred_element_type=F32)
+
+
+def split(values):
+    high = values.astype(BF16)
+    return high, (values - high.astype(F32)).astype(BF16)
+
+
+def features(raw):
+    return jnp.where(raw > 0, raw + 1.0, jnp.exp(jnp.minimum(raw, 0.0))).astype(BF16)
+
+
+def feature_slope(raw):
+    return jnp.where(raw > 0, 1.0, jnp.exp(jnp.minimum(raw, 0.0)))
+
+
+def head_masks():
+    lane = lax.broadcasted_iota(jnp.int32, (1, PAIR), 1)
+    first = jnp.where(lane < 64, 1.0, 0.0)
+    return first.astype(BF16), (1.0 - first).astype(BF16)
+
+
+def first_head(rows):
+    return lax.broadcasted_iota(jnp.int32, (rows, PAIR), 1) < 64
+
+
+def pack_state(square, total):
+    blocks = jnp.where(first_head(64), square[:64], square[64:])
+    return blocks, jnp.broadcast_to(total, (8, PAIR))
+
+
+def unpack_state(packed):
+    first = first_head(64)
+    square = jnp.concatenate(
+        [jnp.where(first, packed[:64], 0.0), jnp.where(first, 0.0, packed[:64])], axis=0
     )
-
-    def lap(k, before):
-        at = devices - 1 - k if reverse else k
-        reached = at > place if reverse else at < place
-        new = combine(before, jax.tree.map(lambda part: part[at], everything))
-        return jax.tree.map(lambda a, b: jnp.where(reached, a, b), new, before)
-
-    return lax.fori_loop(0, devices, lap, start)
-
-
-def rounded(values):
-    return lax.optimization_barrier(values.astype(jnp.bfloat16)).astype(jnp.float32)
+    return square, packed[64:65]
+
+
+def same_head():
+    row = lax.broadcasted_iota(jnp.int32, (PAIR, PAIR), 0)
+    lane = lax.broadcasted_iota(jnp.int32, (PAIR, PAIR), 1)
+    return (row < 64) == (lane < 64)
+
+
+class Scan:
+    def __init__(self, terms, landed, sums, result, sems, reverse):
+        self.terms, self.landed, self.sums, self.result = terms, landed, sums, result
+        self.sems, self.reverse = sems, reverse
+        self.dp, self.me = lax.axis_index("dp"), lax.axis_index("seq")
+
+    def greet(self):
+        barrier = pltpu.get_barrier_semaphore()
+        for step in range(1, SEQ):
+            pl.semaphore_signal(
+                barrier,
+                inc=1,
+                device_id=(self.dp, lax.rem(self.me + step, SEQ)),
+                device_id_type=MESH,
+            )
+
+    def send_all(self, source, target, sent, came):
+        def one(step, carry):
+            other = lax.rem(self.me + step, SEQ)
+            pltpu.make_async_remote_copy(
+                src_ref=source.at[other],
+                dst_ref=target.at[self.me],
+                send_sem=sent.at[step],
+                recv_sem=came.at[step],
+                device_id=(self.dp, other),
+                device_id_type=MESH,
+            ).start()
+            return carry
+
+        lax.fori_loop(1, SEQ, one, 0)
+        target[self.me] = source[self.me]
+
+    def wait_all(self, source, target, sent, came):
+        def one(step, carry):
+            other = lax.rem(self.me + (SEQ - step), SEQ)
+            pltpu.make_async_remote_copy(
+                src_ref=source.at[other],
+                dst_ref=target.at[other],
+                send_sem=sent.at[step],
+                recv_sem=came.at[step],
+                device_id=(self.dp, other),
+                device_id_type=MESH,
+            ).wait_recv()
+            return carry
+
+        lax.fori_loop(1, SEQ, one, 0)
+
+    def wait_sent(self, source, target, sent, came):
+        def one(step, carry):
+            other = lax.rem(self.me + step, SEQ)
+            pltpu.make_async_remote_copy(
+                src_ref=source.at[other],
+                dst_ref=target.at[self.me],
+                send_sem=sent.at[step],
+                recv_sem=came.at[step],
+                device_id=(self.dp, other),
+                device_id_type=MESH,
+            ).wait_send()
+            return carry
+
+        lax.fori_loop(1, SEQ, one, 0)
+
+    def start(self):
+        self.send_all(self.terms, self.landed, self.sems[0], self.sems[1])
+
+    def middle(self):
+        self.wait_all(self.terms, self.landed, self.sems[0], self.sems[1])
+        total = jnp.zeros(self.landed.shape[1:], F32)
+        for k in range(SEQ):
+            at = SEQ - 1 - k if self.reverse else k
+            self.sums[at] = total
+            total = total + self.landed[at]
+        self.send_all(self.sums, self.result, self.sems[2], self.sems[3])
+
+    def finish(self):
+        self.wait_all(self.sums, self.result, self.sems[2], self.sems[3])
+
+    def drain(self):
+        self.wait_sent(self.terms, self.landed, self.sems[0], self.sems[1])
+        self.wait_sent(self.sums, self.result, self.sems[2], self.sems[3])
+
+
+SCAN_SCRATCH = [
+    pltpu.VMEM((SEQ, 72, PAIR), F32),
+    pltpu.VMEM((SEQ, 72, PAIR), F32),
+    pltpu.VMEM((SEQ, 72, PAIR), F32),
+    *[pltpu.SemaphoreType.DMA((SEQ,)) for _ in range(4)],
+]
+
+
+def unit_slices(unit, block):
+    rows = pl.ds(pl.multiple_of(lax.div(unit, 8) * block, block), block)
+    columns = pl.ds(pl.multiple_of(lax.rem(unit, 8) * PAIR, PAIR), PAIR)
+    return rows, columns
+
+
+def for_units(step, together):
+    def several(index, carry):
+        for offset in range(together):
+            step(index * together + offset)
+        return carry
+
+    lax.fori_loop(0, SEQ // together, several, 0)
+
+
+def causal_mask(block, transposed=False):
+    row = lax.broadcasted_iota(jnp.int32, (block, block), 0)
+    column = lax.broadcasted_iota(jnp.int32, (block, block), 1)
+    return (row <= column) if transposed else (row >= column)
+
+
+def norm_rows(values):
+    center = jnp.mean(values, axis=-1, keepdims=True)
+    centered = values - center
+    variance = jnp.mean(centered * centered, axis=-1, keepdims=True)
+    inverse = lax.rsqrt(variance + 1e-05)
+    return centered * inverse, inverse
+
+
+ROWS = 64
+
+
+def for_rows(count, step):
+    def one(index, carry):
+        step(pl.ds(pl.multiple_of(index * ROWS, ROWS), ROWS))
+        return carry
+
+    lax.fori_loop(0, count // ROWS, one, 0)
+
+
+def for_columns(count, width, step):
+    def one(index, carry):
+        step(pl.ds(pl.multiple_of(index * width, width), width))
+        return carry
+
+    lax.fori_loop(0, count // width, one, 0)
+
+
+def attention_forward_kernel(
+    block, x, gain, shift, weight, normed, qkv, att, den, state,
+    w, fq, fk, terms, landed, sums, s0, s1, s2, s3, wsem,
+):
+    scan = Scan(terms, landed, sums, state, (s0, s1, s2, s3), False)
+    scan.greet()
+    loads = []
+    for slot, third in enumerate((1, 2, 0)):
+        load = pltpu.make_async_copy(
+            weight.at[:, pl.ds(third * 1024, 1024)], w.at[slot], wsem.at[slot]
+        )
+        load.start()
+        loads.append(load)
+
+    def norm_step(rows):
+        scaled, _ = norm_rows(x[rows, :].astype(F32))
+        normed[rows, :] = (scaled * gain[...] + shift[...]).astype(BF16)
+
+    for_rows(x.shape[0], norm_step)
+
+    def project(slot, third, feature):
+        loads[slot].wait()
+
+        def step(columns):
+            raw = dot_nn(normed[...], w[slot, :, columns]).astype(BF16)
+            qkv[third, :, columns] = raw
+            if feature is not None:
+                feature[:, columns] = features(raw.astype(F32))
+
+        for_columns(1024, 512, step)
+
+    project(0, 1, fk)
+    project(1, 2, None)
+
+    def local_state(unit):
+        rows, columns = unit_slices(unit, block)
+        keys = fk[rows, columns]
+        square = tn_dot(qkv[2, rows, columns], keys)
+        total = jnp.sum(keys.astype(F32), axis=0, keepdims=True)
+        blocks, row = pack_state(square, total)
+        terms[unit, pl.ds(0, 64)] = blocks
+        terms[unit, pl.ds(64, 8)] = row
+
+    for_units(local_state, 4)
+    pl.semaphore_wait(pltpu.get_barrier_semaphore(), SEQ - 1)
+    scan.start()
+    project(2, 0, fq)
+    first, second = head_masks()
+    causal = causal_mask(block)
+
+    def local_part(unit):
+        rows, columns = unit_slices(unit, block)
+        query, key, value = fq[rows, columns], fk[rows, columns], qkv[2, rows, columns]
+        scores = dot_nt(jnp.concatenate([query * first, query * second], axis=0), key)
+        both = 0.0
+        for head, mask in enumerate((first, second)):
+            own = jnp.where(causal, scores[head * block : (head + 1) * block], 0.0).astype(BF16)
+            right = jnp.concatenate([value * mask, jnp.broadcast_to(mask, value.shape)], axis=1)
+            both = both + dot_nn(own, right)
+        att[rows, columns] = both[:, :PAIR]
+        den[rows, columns] = both[:, PAIR:]
+
+    for_units(local_part, 2)
+    scan.middle()
+    scan.finish()
+    together = same_head()
+
+    def incoming(unit):
+        rows, columns = unit_slices(unit, block)
+        square, total = unpack_state(state[unit])
+        totals = jnp.where(together, jnp.broadcast_to(total, (PAIR, PAIR)), 0.0)
+        high, low = split(jnp.concatenate([square, totals], axis=0))
+        query = fq[rows, columns]
+        both = dot_nt(
+            jnp.concatenate([query, query], axis=1), jnp.concatenate([high, low], axis=1)
+        )
+        denom = den[rows, columns] + both[:, PAIR:]
+        den[rows, columns] = denom
+        att[rows, columns] = (att[rows, columns] + both[:, :PAIR]) / denom
+
+    for_units(incoming, 2)
+    scan.drain()
+
+
+def attention_forward(x, gain, shift, weight, block):
+    rows, width = x.shape
+    vmem = pl.BlockSpec(memory_space=pltpu.VMEM)
+
+    def kernel(*refs):
+        attention_forward_kernel(block, *refs)
+
+    return pl.pallas_call(
+        kernel,
+        out_shape=[
+            jax.ShapeDtypeStruct((rows, width), BF16),
+            jax.ShapeDtypeStruct((3, rows, width), BF16),
+            jax.ShapeDtypeStruct((rows, width), F32),
+            jax.ShapeDtypeStruct((rows, width), F32),
+            jax.ShapeDtypeStruct((SEQ, 72, PAIR), F32),
+        ],
+        in_specs=[vmem, vmem, vmem, pl.BlockSpec(memory_space=pl.ANY)],
+        out_specs=[vmem] * 5,
+        scratch_shapes=[
+            pltpu.VMEM((3, width, width), BF16),
+            pltpu.VMEM((rows, width), BF16),
+            pltpu.VMEM((rows, width), BF16),
+            *SCAN_SCRATCH,
+            pltpu.SemaphoreType.DMA((3,)),
+        ],
+        compiler_params=pltpu.CompilerParams(
+            collective_id=5, has_side_effects=True, vmem_limit_bytes=62 * MIB
+        ),
+    )(x, gain.reshape(1, width), shift.reshape(1, width), weight)
+
+
+def attention_backward_kernel(
+    block, qkv, att, den, state, gatt, gqkv,
+    fq, fk, gn, grads, terms, landed, sums, result, s0, s1, s2, s3,
+):
+    scan = Scan(terms, landed, sums, result, (s0, s1, s2, s3), True)
+    scan.greet()
+    first, second = head_masks()
+    first_wide = first_head(block)
+    fq[...] = features(qkv[0].astype(F32))
+    fk[...] = features(qkv[1].astype(F32))
+
+    def slopes(rows, columns):
+        numer = gn[rows, columns]
+        product = numer * att[rows, columns]
+        ours = jnp.sum(jnp.where(first_wide, product, 0.0), axis=1, keepdims=True)
+        theirs = jnp.sum(jnp.where(first_wide, 0.0, product), axis=1, keepdims=True)
+        return numer, -ours, -theirs
+
+    def local_state(unit):
+        rows, columns = unit_slices(unit, block)
+        gn[rows, columns] = gatt[rows, columns] / den[rows, columns]
+        numer, one, two = slopes(rows, columns)
+        query = fq[rows, columns]
+        high, low = split(numer)
+        wide = tn_dot(query, jnp.concatenate([high, low], axis=1))
+        spread = jnp.where(first_wide, one, two)
+        total = jnp.sum(query.astype(F32) * spread, axis=0, keepdims=True)
+        blocks, row = pack_state(wide[:, :PAIR] + wide[:, PAIR:], total)
+        terms[unit, pl.ds(0, 64)] = blocks
+        terms[unit, pl.ds(64, 8)] = row
+
+    for_units(local_state, 2)
+    pl.semaphore_wait(pltpu.get_barrier_semaphore(), SEQ - 1)
+    scan.start()
+    causal = causal_mask(block)
+    causal_t = causal_mask(block, True)
+
+    def local_part(unit):
+        rows, columns = unit_slices(unit, block)
+        query, key, value = fq[rows, columns], fk[rows, columns], qkv[2, rows, columns]
+        numer, one, two = slopes(rows, columns)
+        high, low = split(numer)
+        scores = dot_nt(jnp.concatenate([key * first, key * second], axis=0), query)
+        wide = jnp.concatenate([high, low], axis=1)
+        values = jnp.concatenate([value, value], axis=1)
+        grad_query, grad_key, grad_value = 0.0, 0.0, 0.0
+        for head, (mask, slope) in enumerate(((first, one), (second, two))):
+            mask_wide = jnp.concatenate([mask, mask], axis=1)
+            mixing = jnp.where(causal, dot_nt(wide * mask_wide, values) + slope, 0.0).astype(BF16)
+            turned = jnp.where(causal_t, scores[head * block : (head + 1) * block], 0.0)
+            grad_query = grad_query + dot_nn(mixing, key * mask)
+            grad_key = grad_key + tn_dot(mixing, query * mask)
+            grad_value = grad_value + dot_nn(turned.astype(BF16), high * mask)
+        square, total = unpack_state(state[unit])
+        state_high, state_low = split(square)
+        grad_query = grad_query + dot_nn(
+            jnp.concatenate([high, low], axis=1),
+            jnp.concatenate([state_high, state_high], axis=0),
+        )
+        grad_query = grad_query + dot_nn(high, state_low)
+        grad_query = grad_query + jnp.where(first_wide, one, two) * total
+        raw = qkv[0, rows, columns].astype(F32)
+        gqkv[0, rows, columns] = (grad_query * feature_slope(raw)).astype(BF16)
+        grads[0, rows, columns] = grad_key
+        grads[1, rows, columns] = grad_value
+
+    for_units(local_part, 1)
+    scan.middle()
+    scan.finish()
+
+    def incoming(unit):
+        rows, columns = unit_slices(unit, block)
+        square, total = unpack_state(result[unit])
+        high, low = split(square)
+        key, value = fk[rows, columns], qkv[2, rows, columns]
+        grad_key = grads[0, rows, columns] + total
+        grad_key = grad_key + dot_nt(
+            jnp.concatenate([value, value], axis=1), jnp.concatenate([high, low], axis=1)
+        )
+        grad_value = grads[1, rows, columns] + dot_nn(
+            jnp.concatenate([key, key], axis=1), jnp.concatenate([high, low], axis=0)
+        )
+        raw = qkv[1, rows, columns].astype(F32)
+        gqkv[1, rows, columns] = (grad_key * feature_slope(raw)).astype(BF16)
+        gqkv[2, rows, columns] = grad_value.astype(BF16)
+
+    for_units(incoming, 2)
+    scan.drain()
+
+
+def attention_backward(qkv, att, den, state, gatt, block):
+    _, rows, width = qkv.shape
+    vmem = pl.BlockSpec(memory_space=pltpu.VMEM)
+
+    def kernel(*refs):
+        attention_backward_kernel(block, *refs)
+
+    return pl.pallas_call(
+        kernel,
+        out_shape=jax.ShapeDtypeStruct((3, rows, width), BF16),
+        in_specs=[vmem] * 5,
+        out_specs=vmem,
+        scratch_shapes=[
+            pltpu.VMEM((rows, width), BF16),
+            pltpu.VMEM((rows, width), BF16),
+            pltpu.VMEM((rows, width), F32),
+            pltpu.VMEM((2, rows, width), F32),
+            SCAN_SCRATCH[0],
+            *SCAN_SCRATCH,
+        ],
+        compiler_params=pltpu.CompilerParams(
+            collective_id=6, has_side_effects=True, vmem_limit_bytes=62 * MIB
+        ),
+    )(qkv, att, den, state, gatt)
 
 
 def layer_norm(values, gain, shift):
@@ -406,10 +807,6 @@
     return lax.dot_general(
         left, right, (((1,), (1,)), ((), ())), preferred_element_type=jnp.float32
     )
-
-
-def add_pair(earlier, later):
-    return (earlier[0] + later[0], earlier[1] + later[1])
 
 
 def body(
@@ -425,40 +822,13 @@
     cotangent,
 ):
     seq_count, block_len, width = inputs.shape
-    head_size = width // HEADS
     row_count = seq_count * block_len
     flat_input = inputs.astype(jnp.float32).reshape(row_count, width)
-    normed, scaled_one, inverse_one = layer_norm(flat_input, first_gain, first_shift)
-    normed_low = normed.astype(jnp.bfloat16)
-    qkv_low = jnp.dot(normed_low, qkv_weight, preferred_element_type=jnp.float32).astype(
-        jnp.bfloat16
+    _, scaled_one, inverse_one = layer_norm(flat_input, first_gain, first_shift)
+    normed_low, qkv_low, attended, denom, state_in = attention_forward(
+        inputs.reshape(row_count, width), first_gain, first_shift, qkv_weight, block_len
     )
-    qkv_wide = qkv_low.astype(jnp.float32).reshape(seq_count, block_len, 3, HEADS, head_size)
-    queries = qkv_wide[:, :, 0]
-    keys = qkv_wide[:, :, 1]
-    values = qkv_wide[:, :, 2]
-    feat_query = rounded(jax.nn.elu(queries) + 1.0)
-    feat_key = rounded(jax.nn.elu(keys) + 1.0)
-    causal = (
-        lax.broadcasted_iota(jnp.int32, (block_len, block_len), 0)
-        >= lax.broadcasted_iota(jnp.int32, (block_len, block_len), 1)
-    ).astype(jnp.float32)
-    scores = jnp.einsum("nthe,nshe->nhts", feat_query, feat_key, precision=highest) * causal
-    numer_local = jnp.einsum("nhts,nshf->nthf", scores, values, precision=highest)
-    denom_local = jnp.transpose(jnp.sum(scores, axis=-1), (0, 2, 1))
-    state_local = jnp.einsum("nshe,nshf->nhef", feat_key, values, precision=highest)
-    total_local = jnp.sum(feat_key, axis=1)
-    state_in, total_in = carried_in(
-        (state_local, total_local),
-        "seq",
-        add_pair,
-        (jnp.zeros_like(state_local), jnp.zeros_like(total_local)),
-        False,
-    )
-    numer = numer_local + jnp.einsum("nthe,nhef->nthf", feat_query, state_in, precision=highest)
-    denom = denom_local + jnp.einsum("nthe,nhe->nth", feat_query, total_in, precision=highest)
-    attended = numer / denom[..., None]
-    attended_low = attended.reshape(row_count, width).astype(jnp.bfloat16)
+    attended_low = attended.astype(jnp.bfloat16)
     mixed = flat_input + jnp.dot(attended_low, out_weight, preferred_element_type=jnp.float32)
     normed_two, scaled_two, inverse_two = layer_norm(mixed, second_gain, second_shift)
     normed_two_low = normed_two.astype(jnp.bfloat16)
@@ -481,42 +851,9 @@
     )
     grad_mixed_low = grad_mixed.astype(jnp.bfloat16)
     grad_out = grad_wide_sum(attended_low, grad_mixed_low, (384, 384, 256), 3)
-    grad_att = back_dot(grad_mixed_low, out_weight).reshape(seq_count, block_len, HEADS, head_size)
-    grad_numer = grad_att / denom[..., None]
-    grad_denom = -jnp.sum(grad_att * attended, axis=-1) / denom
-    mixing = (
-        jnp.einsum("nthf,nshf->nhts", grad_numer, values, precision=highest)
-        + jnp.transpose(grad_denom, (0, 2, 1))[..., None]
-    ) * causal
-    grad_query = (
-        jnp.einsum("nhts,nshe->nthe", mixing, feat_key, precision=highest)
-        + jnp.einsum("nthf,nhef->nthe", grad_numer, state_in, precision=highest)
-        + grad_denom[..., None] * total_in[:, None]
-    )
-    grad_state_in = jnp.einsum("nthe,nthf->nhef", feat_query, grad_numer, precision=highest)
-    grad_total_in = jnp.einsum("nthe,nth->nhe", feat_query, grad_denom, precision=highest)
-    grad_state, grad_total = carried_in(
-        (grad_state_in, grad_total_in),
-        "seq",
-        add_pair,
-        (jnp.zeros_like(grad_state_in), jnp.zeros_like(grad_total_in)),
-        True,
-    )
-    grad_key = (
-        jnp.einsum("nhts,nthe->nshe", mixing, feat_query, precision=highest)
-        + jnp.einsum("nshf,nhef->nshe", values, grad_state, precision=highest)
-        + grad_total[:, None]
-    )
-    grad_value = jnp.einsum("nhts,nthf->nshf", scores, grad_numer, precision=highest) + jnp.einsum(
-        "nshe,nhef->nshf", feat_key, grad_state, precision=highest
-    )
-    grad_query = grad_query * jnp.where(queries > 0, 1.0, jnp.exp(jnp.minimum(queries, 0.0)))
-    grad_key = grad_key * jnp.where(keys > 0, 1.0, jnp.exp(jnp.minimum(keys, 0.0)))
-    grad_qkv_low = (
-        jnp.stack([grad_query, grad_key, grad_value], axis=2)
-        .reshape(row_count, 3 * width)
-        .astype(jnp.bfloat16)
-    )
+    grad_att = back_dot(grad_mixed_low, out_weight)
+    grad_qkv_three = attention_backward(qkv_low, attended, denom, state_in, grad_att, block_len)
+    grad_qkv_low = jnp.concatenate([grad_qkv_three[0], grad_qkv_three[1], grad_qkv_three[2]], axis=1)
     grad_qkv = grad_wide_sum(normed_low, grad_qkv_low, (1024, 1024, 1024), 4)
     grad_normed = back_dot(grad_qkv_low, qkv_weight)
     grad_first_gain = jnp.sum(grad_normed * scaled_one, axis=0)

time: 715 us -> 420 us (0.59)
  waiting for transfers between devices: 82.9 us -> 0 us
  other arithmetic: 92.7 us -> 13.6 us
  matrix products: 106 us -> 51.8 us
  blocking collectives: 115 us -> 65.4 us
  local copies, waits for them, and re-layouts: 43.8 us -> 10.9 us
  Pallas kernels: 250 us -> 270 us
  between operations: 15 us -> 1.39 us
    all_gather x2 -> x0, waiting for transfers between devices: 82.9 us -> none  [carried_in(): everything = jax.tree.map(lambda part: lax.all_gather(part, axis), shard)]
    select_n x64 -> x0, other arithmetic: 74 us -> none  [lap(): return jax.tree.map(lambda a, b: jnp.where(reached, a, b), new, before)]
    pallas_call x0 -> x2, Pallas kernels: none -> 64.5 us  [the longest x1 33.7 us: attention_forward(): pl.pallas_call(kernel, out_shape=[jax.ShapeDtypeStruct((rows, width), BF1...]
    dot_general x15 -> x0, matrix products: 58.2 us -> none  [the longest x1 9.42 us: body(): jnp.einsum('nhts,nthf->nshf', scores, grad_numer, precision=highest)]
    all_gather x2 -> x0, blocking collectives: 51.7 us -> none  [carried_in(): everything = jax.tree.map(lambda part: lax.all_gather(part, axis), shard)]
    pallas_call x4, Pallas kernels: 250 us -> 205 us  [grad_call(): pl.pallas_call(kernel, out_shape=jax.ShapeDtypeStruct(out_shape, F32), in...]
    convert_element_type x5 -> x0, local copies, waits for them, and re-layouts: 16.4 us -> none  [the longest x2 9.25 us: body(): grad_qkv_low = jnp.stack([grad_query, grad_key, grad_value], axis=2).resh...]
    reshape x3 -> x0, local copies, waits for them, and re-layouts: 15.4 us -> none  [the longest x2 11.9 us: body(): qkv_low.astype(jnp.float32)]
  transfers between devices with their start and end apart: 2 -> 0, of which waited for: 1 -> 0; matrix products, arithmetic and copies ran while one was open for 4% -> 0% of each run, Pallas kernels for 28% -> 0%
where the time goes in v2:
time: 420 us; the launch traced here: 413 us
  Pallas kernels  270 us (64%)
  blocking collectives  65.4 us (16%)
  matrix products  51.8 us (12%)
  other arithmetic  13.6 us (3%)
  local copies, waits for them, and re-layouts  10.9 us (3%)
    pallas_call x4, Pallas kernels, grad_call(): pl.pallas_call(kernel, out_shape=jax.ShapeDtypeStruct(out_shape, F32), in...  205 us
    unnamed x1, blocking collectives  65.4 us
    pallas_call x1, Pallas kernels, attention_forward(): pl.pallas_call(kernel, out_shape=[jax.ShapeDtypeStruct((rows, width), BF1...  33.7 us
    pallas_call x1, Pallas kernels, attention_backward(): pl.pallas_call(kernel, out_shape=jax.ShapeDtypeStruct((3, rows, width), B...  30.8 us
    dot_general x4, matrix products, back_dot(): lax.dot_general(left, right, (((1,), (1,)), ((), ())), preferred_element_...  20.6 us
    dot_general x1, matrix products, body(): jnp.dot(normed_two_low, up_weight, preferred_element_type=jnp.float32)  19.8 us
    dot_general x1, matrix products, body(): jnp.dot(hidden_low, down_weight, preferred_element_type=jnp.float32)  8.66 us

profile of v2, /device:TPU:0, one launch (start us, length us, event | category | flops | bytes accessed | tf_op | source)
XLA Modules:
  0.0 412.9 jit_solution(10121336378898969867)
XLA Ops:
  0.6 33.7 %shard_map.177 = (bf16[384,1024]{1,0:T(8,128)(2,1)}, bf16[3,384,1024]{2,1,0:T(8,128)(2,1)}, f32[384,1024]{1,0:T(8,128)}, f32[384,1024]{1,0:T(8,128)}, f32[16,72,128]{2,1,0:T(8,128)}) custom-call(bf16[384,1024]{1,0:T(8,128)(2,1)} %bitcast.48, f32[1,1024]{1,0:T(1,128)} %bitcast.52, f32[1,1024]{1,0:T(1,128)} %bitcast.53, bf16[1024,3072]{1,0:T(8,128)(2,1)} %refs_3_.1), custom_call_target="tpu_custom_call" | custom-call | tf_op jit(solution)/shard_map/pallas_call | solution.py:644
  34.4 1.5 convert_element_type.25.refs_0_
  36.0 0.9 copy-done.1
  36.8 2.8 fusion.29
  40.4 19.8 %fusion.2 = (bf16[384,4096]{1,0:T(8,128)(2,1)}, f32[384,4096]{1,0:T(8,128)}) fusion(bf16[384,1024]{1,0:T(8,128)(2,1)S(1)} %add_convert_fusion.1.refs_0_, bf16[1024,4096]{1,0:T(8,128)(2,1)} %param.17), kind=kOutput, calls=%fused_computation.4 | convolution fusion | flops 3323461632 | bytes 18612224 | tf_op jit(solution)/shard_map/dot_general | solution.py:835
  60.2 7.1 %fusion.8.refs_1_ = bf16[384,4096]{1,0:T(8,128)(2,1)S(1)} fusion(f32[384,4096]{1,0:T(8,128)} %get-tuple-element.40, bf16[384,1024]{1,0:T(8,128)(2,1)S(1)} %bitcast.50, bf16[4096,1024]{1,0:T(8,128)(2,1)S(1)} %bitcast.57), kind=kOutput, calls=%fused_computation.10 | convolution fusion | flops 3236954112 | bytes 18612224 | tf_op jit(solution)/shard_map/dot_general | solution.py:807
  67.4 3.8 multiply_reduce_fusion
  71.3 1.8 fusion.28
  73.1 0.9 copy-done.3
  74.0 2.2 fusion.30.refs_4_
  76.2 30.8 %shard_map.178 = bf16[3,384,1024]{2,1,0:T(8,128)(2,1)} custom-call(bf16[3,384,1024]{2,1,0:T(8,128)(2,1)} %get-tuple-element.16.refs_0_, f32[384,1024]{1,0:T(8,128)} %get-tuple-element.15.refs_1_, f32[384,1024]{1,0:T(8,128)} %get-tuple-element.17.refs_2_, f32[16,72,128]{2,1,0:T(8,128)} %get-tuple-element.18.refs_3_, f32[384,1024]{1,0:T(8,128)} %fusion.30.refs_4_), custom_call_target="tpu_custom_call" | custom-call | tf_op jit(solution)/shard_map/pallas_call | solution.py:765
  107.0 3.0 slice_bitcast_fusion.2
  110.1 1.3 convert_reduce_fusion
  111.4 1.5 fusion.17
  113.1 7.4 %fusion.26 = (f32[1024]{0:T(1024)S(1)}, f32[384]{0:T(512)S(1)}, f32[384]{0:T(512)S(1)}, f32[1024]{0:T(1024)S(1)}, f32[384,1024]{1,0:T(8,128)}) fusion(bf16[2,192,1024]{2,1,0:T(8,128)(2,1)S(1)} %copy-done, f32[384]{0:T(512)S(1)} %div.33, f32[384]{0:T(512)S(1)} %rsqrt.21, f32[1024]{0:T(1024)S(1)} %copy-done.9, bf16[1024,3072]{1,0:T(8,128)(2,1)} %refs_3_.1, ...), kind=kOutput, calls=%fused_computation.41 | convolution fusion | flops 2426926080 | bytes 11028480 | tf_op jit(solution)/shard_map/dot_general | solution.py:807
  120.4 65.4 %all-reduce.4 = (f32[1024]{0:T(1024)S(1)}, f32[1024]{0:T(1024)S(1)}, f32[1024]{0:T(1024)S(1)}, f32[1024]{0:T(1024)S(1)}) all-reduce(f32[1024]{0:T(1024)S(1)} %get-tuple-element.22, f32[1024]{0:T(1024)S(1)} %get-tuple-element.27, f32[1024]{0:T(1024)S(1)} %get-tuple-element.20, ...), channel_id=2, replica_groups=mesh['dp'=8,'seq'=16] {'dp','seq'}, use_global_device_ids=true, to_apply=%region_9.0.clone | all-reduce | flops 4096 | bytes 32768
  188.2 3.0 pad_maximum_fusion.refs_1_
  191.2 51.3 %shard_map.179 = f32[8,3072]{1,0:T(8,128)} custom-call(bf16[384,1024]{1,0:T(8,128)(2,1)} %get-tuple-element.19.refs_0_, bf16[384,3072]{1,0:T(8,128)(2,1)} %pad_maximum_fusion.refs_1_), custom_call_target="tpu_custom_call" | custom-call | tf_op jit(solution)/shard_map/pallas_call | solution.py:326
  242.5 3.8 fusion.25
  246.3 32.3 %shard_map.180 = f32[8,1024]{1,0:T(8,128)} custom-call(bf16[384,1024]{1,0:T(8,128)(2,1)} %copy-done.1, bf16[384,1024]{1,0:T(8,128)(2,1)} %copy-done.3), custom_call_target="tpu_custom_call" | custom-call | tf_op jit(solution)/shard_map/pallas_call | solution.py:326
  278.6 61.1 %shard_map.181 = f32[8,4096]{1,0:T(8,128)} custom-call(bf16[384,1024]{1,0:T(8,128)(2,1)} %copy-done.4, bf16[384,4096]{1,0:T(8,128)(2,1)} %copy-done.2), custom_call_target="tpu_custom_call" | custom-call | tf_op jit(solution)/shard_map/pallas_call | solution.py:326
  339.7 8.7 %add_convert_fusion = bf16[384,1024]{1,0:T(8,128)(2,1)} fusion(f32[384,1024]{1,0:T(8,128)S(1)} %get-tuple-element.38, bf16[384,4096]{1,0:T(8,128)(2,1)} %get-tuple-element.39.left, bf16[4096,1024]{1,0:T(8,128)(2,1)} %param.18), kind=kOutput, calls=%fused_computation.45 | convolution fusion | flops 3222011904 | bytes 13893632 | tf_op jit(solution)/shard_map/dot_general | solution.py:837
  348.4 60.6 %shard_map.182 = f32[32,1024]{1,0:T(8,128)} custom-call(bf16[384,4096]{1,0:T(8,128)(2,1)} %get-tuple-element.39.left, bf16[384,1024]{1,0:T(8,128)(2,1)} %bitcast.49), custom_call_target="tpu_custom_call" | custom-call | tf_op jit(solution)/shard_map/pallas_call | solution.py:326
  410.9 1.6 copy.27
  (52 shorter events, 5.2 us)
Async XLA Ops:
  34.4 5.6 %copy-start.10 = (f32[1024]{0:T(1024)S(1)}, f32[1024]{0:T(1024)}, u32[]{:S(2)}) copy-start(f32[1024]{0:T(1024)} %param.15) | copy-start | bytes 12292
  34.4 5.6 %copy-start.11 = (f32[1024]{0:T(1024)S(1)}, f32[1024]{0:T(1024)}, u32[]{:S(2)}) copy-start(f32[1024]{0:T(1024)} %param.16) | copy-start | bytes 12292
  35.9 0.9 copy-start.1
  40.0 27.4 %slice-start = ((s8[8388608]{0:T(1024)(128)(4,1)}), s8[4194304]{0:T(1024)(128)(4,1)S(1)}, s32[]{:S(2)}) async-start(s8[8388608]{0:T(1024)(128)(4,1)} %bitcast.54), calls=%async_computation | async-start | bytes 8388608
  40.0 20.2 %slice-start.2 = ((s8[8388608]{0:T(1024)(128)(4,1)}), s8[4194304]{0:T(1024)(128)(4,1)S(1)}, s32[]{:S(2)}) async-start(s8[8388608]{0:T(1024)(128)(4,1)} %bitcast.56), calls=%async_computation.2 | async-start | bytes 8388608
  40.4 19.9 %copy-start.4 = (bf16[384,1024]{1,0:T(8,128)(2,1)}, bf16[384,1024]{1,0:T(8,128)(2,1)S(1)}, u32[]{:S(2)}) copy-start(bf16[384,1024]{1,0:T(8,128)(2,1)S(1)} %add_convert_fusion.1.refs_0_) | copy-start | bytes 2359300
  40.4 19.8 %copy-start.5 = (bf16[2,192,1024]{2,1,0:T(8,128)(2,1)S(1)}, bf16[2,192,1024]{2,1,0:T(8,128)(2,1)}, u32[]{:S(2)}) copy-start(bf16[2,192,1024]{2,1,0:T(8,128)(2,1)} %param.19) | copy-start | bytes 2359300
  40.4 19.8 %slice-start.3 = ((s8[8388608]{0:T(1024)(128)(4,1)}), s8[4194304]{0:T(1024)(128)(4,1)S(1)}, s32[]{:S(2)}) async-start(s8[8388608]{0:T(1024)(128)(4,1)} %bitcast.56), calls=%async_computation.3 | async-start | bytes 8388608
  40.4 27.0 %slice-start.1 = ((s8[8388608]{0:T(1024)(128)(4,1)}), s8[4194304]{0:T(1024)(128)(4,1)S(1)}, s32[]{:S(2)}) async-start(s8[8388608]{0:T(1024)(128)(4,1)} %bitcast.54), calls=%async_computation.1 | async-start | bytes 8388608
  67.4 3.9 copy-start.2
  71.3 2.7 copy-start.12
  73.1 0.9 copy-start.3
  76.2 36.8 %copy-start.9 = (f32[1024]{0:T(1024)S(1)}, f32[1024]{0:T(1024)}, u32[]{:S(2)}) copy-start(f32[1024]{0:T(1024)} %param.11) | copy-start | bytes 12292
  107.0 6.0 %copy-start = (bf16[2,192,1024]{2,1,0:T(8,128)(2,1)S(1)}, bf16[2,192,1024]{2,1,0:T(8,128)(2,1)}, u32[]{:S(2)}) copy-start(bf16[2,192,1024]{2,1,0:T(8,128)(2,1)} %param.10) | copy-start | bytes 2359300
  339.7 69.3 %copy-start.7 = (f32[8,3072]{1,0:T(8,128)S(1)}, f32[8,3072]{1,0:T(8,128)}, u32[]{:S(2)}) copy-start(f32[8,3072]{1,0:T(8,128)} %shard_map.179) | copy-start | bytes 294916
  339.7 69.9 %copy-start.8 = (f32[8,1024]{1,0:T(8,128)S(1)}, f32[8,1024]{1,0:T(8,128)}, u32[]{:S(2)}) copy-start(f32[8,1024]{1,0:T(8,128)} %shard_map.180) | copy-start | bytes 98308
  339.7 70.5 %copy-start.6 = (f32[8,4096]{1,0:T(8,128)S(1)}, f32[8,4096]{1,0:T(8,128)}, u32[]{:S(2)}) copy-start(f32[8,4096]{1,0:T(8,128)} %shard_map.181) | copy-start | bytes 393220

commit v3 on v2

v3 whole, which is shorter than its diff:
```python
import math

import jax
import jax.numpy as jnp
from jax import lax
from jax.experimental import pallas as pl
from jax.experimental.pallas import tpu as pltpu
from jax.sharding import PartitionSpec as P

MESH = pl.DeviceIdType.MESH
F32 = jnp.float32
BF16 = jnp.bfloat16
RING = 4
MIB = 2**20


class Place:
    def __init__(self):
        dp, seq = lax.axis_index("dp"), lax.axis_index("seq")
        self.core = lax.rem(dp, 2)
        self.at = (lax.div(dp, 2), lax.div(seq, RING), lax.rem(seq, RING))

    def id_of(self, x, y, z, core):
        return (x * 2 + core, y * RING + z)

    def ring(self, axis, step):
        return lax.rem(self.at[axis] + (step + RING), RING)

    def neighbour(self, axis, step):
        at = list(self.at)
        at[axis] = self.ring(axis, step)
        return self.id_of(*at, self.core)

    def partner(self):
        return self.id_of(*self.at, 1 - self.core)


def greet(others):
    barrier = pltpu.get_barrier_semaphore()
    for other in others:
        pl.semaphore_signal(barrier, inc=1, device_id=other, device_id_type=MESH)


def met(count):
    pl.semaphore_wait(pltpu.get_barrier_semaphore(), count)


def link_neighbours(place):
    others = [place.neighbour(axis, step) for axis in range(3) for step in (1, -1)]
    return [*others, place.partner()]


ORDERS = ((0, 1, 2), (1, 2, 0), (2, 0, 1))


def phase_scratch(remaining, length):
    if remaining:
        half = (2, 2, *[4] * (remaining - 1), 8, length)
    else:
        half = (2, 8, (length // 128 + 1) // 2 * 128)
    return [
        pltpu.VMEM((2, *[4] * remaining, 8, length), F32),
        pltpu.VMEM(half, F32),
        pltpu.SemaphoreType.DMA((6,)),
        pltpu.SemaphoreType.DMA((6,)),
    ]


class Phase:
    def __init__(self, place, data, axes, axis, scratch):
        self.place, self.data, self.axis = place, data, axis
        self.where = axes.index(axis)
        self.full, self.half, self.sent, self.came = scratch
        self.flying = []
        self.flat = len(axes) == 1
        self.length = data.shape[-1]
        self.cut = (self.length // 128 + 1) // 2 * 128
        self.whole = self.flat and self.cut == self.length

    def empty(self, which):
        return self.whole and which == 1

    def chunk(self, target):
        index = [slice(None)] * self.where + [target]
        return self.data.at[tuple(index)]

    def part(self, ref, which):
        if not self.flat:
            return ref.at[pl.ds(2 * which, 2)]
        if which == 0:
            return ref.at[:, pl.ds(0, self.cut)]
        return ref.at[:, pl.ds(self.cut, self.length - self.cut)]

    def through(self, way):
        ref = self.half.at[way]
        if self.flat and way == 1:
            return ref.at[:, pl.ds(0, self.length - self.cut)]
        return ref

    def copy(self, kind, way, source, target):
        number = kind * 2 + way
        return pltpu.make_async_remote_copy(
            src_ref=source,
            dst_ref=target,
            send_sem=self.sent.at[number],
            recv_sem=self.came.at[number],
            device_id=self.place.neighbour(self.axis, 1 - 2 * way),
            device_id_type=MESH,
        )

    def send(self, kind, way, source, target):
        copy = self.copy(kind, way, source, target)
        copy.start()
        self.flying.append(copy)

    def beside(self, way):
        return self.chunk(self.place.ring(self.axis, 1 - 2 * way))

    def begin(self):
        opposite = self.chunk(self.place.ring(self.axis, 2))
        for way in range(2):
            if not self.empty(way):
                self.send(0, way, self.part(opposite, way), self.through(way))
        for way in range(2):
            if self.empty(1 - way):
                continue
            target = self.part(self.full.at[way], 1 - way)
            self.send(1, way, self.part(self.beside(way), 1 - way), target)

    def forward(self):
        for way in range(2):
            if self.empty(way):
                continue
            came = self.through(way)
            self.copy(0, way, came, came).wait_recv()
            own = self.part(self.beside(way), way)
            add_into(own, own, came)
            self.send(2, way, own, self.part(self.full.at[way], way))

    def finish(self, out=None):
        own = self.chunk(self.place.at[self.axis])
        for way in range(2):
            for kind, which in ((1, 1 - way), (2, way)):
                if self.empty(which):
                    continue
                target = self.part(self.full.at[way], which)
                self.copy(kind, way, target, target).wait_recv()
        add_into(own if out is None else out, own, self.full.at[0], self.full.at[1])
        return own

    def drain(self):
        for copy in self.flying:
            copy.wait_send()


class Sum:
    def __init__(self, place, pieces, scratch, first=0, last=2):
        self.place, self.pieces, self.scratch = place, list(pieces), scratch
        self.at, self.last, self.old = first, last, []
        self.now = None
        self.axes = [sorted(order[first:]) for order in ORDERS[: len(self.pieces)]]

    def begin(self):
        self.now = []
        for k, piece in enumerate(self.pieces):
            axis = ORDERS[k][self.at]
            scratch = self.scratch[self.at][k]
            self.now.append(Phase(self.place, piece, self.axes[k], axis, scratch))
        for phase in self.now:
            phase.begin()

    def forward(self):
        for phase in self.now:
            phase.forward()

    def finish(self, outs=None):
        for k, phase in enumerate(self.now):
            self.pieces[k] = phase.finish(None if outs is None else outs[k])
            self.axes[k] = [axis for axis in self.axes[k] if axis != phase.axis]
        self.old += self.now
        self.at += 1
        if self.at <= self.last:
            self.begin()

    def drain(self):
        for phase in self.old:
            phase.drain()


def sum_scratch(widths, first=0, last=2):
    return {
        at: [phase_scratch(2 - at, width) for width in widths] for at in range(first, last + 1)
    }


def add_into(out, *terms):
    if len(out.shape) > 2:

        def row(index, carry):
            add_into(out.at[index], *[term.at[index] for term in terms])
            return carry

        if len(out.shape) == 4:
            lax.fori_loop(0, out.shape[0], row, 0)
        else:
            for index in range(out.shape[0]):
                row(index, 0)
        return
    total = terms[0][...]
    for term in terms[1:]:
        total = total + term[...]
    out[...] = total


def tn_dot(left, right):
    return lax.dot_general(left, right, (((0,), (0,)), ((), ())), preferred_element_type=F32)


TILE = 512


class Swap:
    def __init__(self, place, stage, sent, came):
        self.place, self.stage, self.sent, self.came = place, stage, sent, came

    def copy(self, number, slot, target):
        return pltpu.make_async_remote_copy(
            src_ref=self.stage.at[slot],
            dst_ref=target,
            send_sem=self.sent.at[number],
            recv_sem=self.came.at[number],
            device_id=self.place.partner(),
            device_id_type=MESH,
        )

    def put(self, number, slot, values, target, before=None):
        if before is not None:
            self.copy(before, slot, target).wait_send()
        self.stage[slot] = values.astype(F32)
        self.copy(number, slot, target).start()

    def get(self, number, target):
        self.copy(number, 0, target).wait_recv()
        return target[...].astype(BF16)

    def drain(self, numbers, target):
        for number in numbers:
            self.copy(number, number % 4, target).wait_send()


def half_columns(block, core, quarter):
    half = quarter // 2
    return pl.ds(pl.multiple_of(block * quarter + core * half, half), half)


def half_tile(index, core):
    return pl.ds(pl.multiple_of((2 * index + core) * TILE, TILE), TILE)


def shared_widths(columns):
    tiles = columns // 128
    main = (2 * tiles + 2) // 3
    return main * 128, main * 128, (2 * tiles - 2 * main) * 128


def shared_product(left, right, slabs, columns):
    main, _, tail = shared_widths(columns)
    rest = tail // 2
    start = 0
    while start < columns:
        width = min(TILE, main - start) if start < main else rest
        product = tn_dot(left[...], right[:, pl.ds(start, width)]).reshape(4, 2, 4, 4, 8, width)
        for core in range(2):
            if start < main:
                slabs[core][:, :, :, :, pl.ds(start, width)] = product[:, core]
            else:
                slabs[2][:, :, :, :, pl.ds(core * rest, rest)] = product[:, core]
        start += width


def shared_rows(pieces, columns, rows):
    main, _, tail = shared_widths(columns)
    rest = tail // 2
    for core in range(2):
        rows[core, :, pl.ds(0, main)] = pieces[core][...]
        rows[core, :, pl.ds(main, rest)] = pieces[2][:, pl.ds(core * rest, rest)]


def row_swap(place, rows, land, sems):
    return pltpu.make_async_remote_copy(
        src_ref=rows.at[1 - place.core],
        dst_ref=land,
        send_sem=sems.at[0],
        recv_sem=sems.at[1],
        device_id=place.partner(),
        device_id_type=MESH,
    )


def lay_rows(place, rows, land, out):
    for tile in range(land.shape[1] // TILE):
        columns = pl.ds(tile * TILE, TILE)
        out[:, half_tile(tile, place.core)] = rows[place.core, :, columns]
        out[:, half_tile(tile, 1 - place.core)] = land[:, columns]


DOWN_CUTS = ((0, 384), (384, 384), (768, 256))
DOWN_WIDTHS = (1408, 1408, 1280)


SEQ = 16
PAIR = 128
NT = (((1,), (1,)), ((), ()))
TN = (((0,), (0,)), ((), ()))


def dot_nt(left, right):
    return lax.dot_general(left, right, NT, preferred_element_type=F32)


def dot_nn(left, right):
    return jnp.dot(left, right, preferred_element_type=F32)


def split(values):
    high = values.astype(BF16)
    return high, (values - high.astype(F32)).astype(BF16)


def features(raw):
    return jnp.where(raw > 0, raw + 1.0, jnp.exp(jnp.minimum(raw, 0.0))).astype(BF16)


def feature_slope(raw):
    return jnp.where(raw > 0, 1.0, jnp.exp(jnp.minimum(raw, 0.0)))


def head_masks():
    lane = lax.broadcasted_iota(jnp.int32, (1, PAIR), 1)
    first = jnp.where(lane < 64, 1.0, 0.0)
    return first.astype(BF16), (1.0 - first).astype(BF16)


def first_head(rows):
    return lax.broadcasted_iota(jnp.int32, (rows, PAIR), 1) < 64


def pack_state(square, total):
    blocks = jnp.where(first_head(64), square[:64], square[64:])
    return blocks, jnp.broadcast_to(total, (8, PAIR))


def unpack_state(packed):
    first = first_head(64)
    square = jnp.concatenate(
        [jnp.where(first, packed[:64], 0.0), jnp.where(first, 0.0, packed[:64])], axis=0
    )
    return square, packed[64:65]


def same_head():
    row = lax.broadcasted_iota(jnp.int32, (PAIR, PAIR), 0)
    lane = lax.broadcasted_iota(jnp.int32, (PAIR, PAIR), 1)
    return (row < 64) == (lane < 64)


class Scan:
    def __init__(self, terms, landed, sums, result, sems, reverse):
        self.terms, self.landed, self.sums, self.result = terms, landed, sums, result
        self.sems, self.reverse = sems, reverse
        self.dp, self.me = lax.axis_index("dp"), lax.axis_index("seq")

    def others(self):
        return [(self.dp, lax.rem(self.me + step, SEQ)) for step in range(1, SEQ)]

    def send_all(self, source, target, sent, came):
        def one(step, carry):
            other = lax.rem(self.me + step, SEQ)
            pltpu.make_async_remote_copy(
                src_ref=source.at[other],
                dst_ref=target.at[self.me],
                send_sem=sent.at[step],
                recv_sem=came.at[step],
                device_id=(self.dp, other),
                device_id_type=MESH,
            ).start()
            return carry

        lax.fori_loop(1, SEQ, one, 0)
        target[self.me] = source[self.me]

    def wait_all(self, source, target, sent, came):
        def one(step, carry):
            other = lax.rem(self.me + (SEQ - step), SEQ)
            pltpu.make_async_remote_copy(
                src_ref=source.at[other],
                dst_ref=target.at[other],
                send_sem=sent.at[step],
                recv_sem=came.at[step],
                device_id=(self.dp, other),
                device_id_type=MESH,
            ).wait_recv()
            return carry

        lax.fori_loop(1, SEQ, one, 0)

    def wait_sent(self, source, target, sent, came):
        def one(step, carry):
            other = lax.rem(self.me + step, SEQ)
            pltpu.make_async_remote_copy(
                src_ref=source.at[other],
                dst_ref=target.at[self.me],
                send_sem=sent.at[step],
                recv_sem=came.at[step],
                device_id=(self.dp, other),
                device_id_type=MESH,
            ).wait_send()
            return carry

        lax.fori_loop(1, SEQ, one, 0)

    def start(self):
        self.send_all(self.terms, self.landed, self.sems[0], self.sems[1])

    def middle(self):
        self.wait_all(self.terms, self.landed, self.sems[0], self.sems[1])
        total = jnp.zeros(self.landed.shape[1:], F32)
        for k in range(SEQ):
            at = SEQ - 1 - k if self.reverse else k
            self.sums[at] = total
            total = total + self.landed[at]
        self.send_all(self.sums, self.result, self.sems[2], self.sems[3])

    def finish(self):
        self.wait_all(self.sums, self.result, self.sems[2], self.sems[3])

    def drain(self):
        self.wait_sent(self.terms, self.landed, self.sems[0], self.sems[1])
        self.wait_sent(self.sums, self.result, self.sems[2], self.sems[3])


SCAN_SCRATCH = [
    pltpu.VMEM((SEQ, 72, PAIR), F32),
    pltpu.VMEM((SEQ, 72, PAIR), F32),
    pltpu.VMEM((SEQ, 72, PAIR), F32),
    *[pltpu.SemaphoreType.DMA((SEQ,)) for _ in range(4)],
]


def unit_slices(unit, block):
    rows = pl.ds(pl.multiple_of(lax.div(unit, 8) * block, block), block)
    columns = pl.ds(pl.multiple_of(lax.rem(unit, 8) * PAIR, PAIR), PAIR)
    return rows, columns


def for_units(step, together):
    def several(index, carry):
        for offset in range(together):
            step(index * together + offset)
        return carry

    lax.fori_loop(0, SEQ // together, several, 0)


def causal_mask(block, transposed=False):
    row = lax.broadcasted_iota(jnp.int32, (block, block), 0)
    column = lax.broadcasted_iota(jnp.int32, (block, block), 1)
    return (row <= column) if transposed else (row >= column)


def norm_rows(values):
    center = jnp.mean(values, axis=-1, keepdims=True)
    centered = values - center
    variance = jnp.mean(centered * centered, axis=-1, keepdims=True)
    inverse = lax.rsqrt(variance + 1e-05)
    return centered * inverse, inverse


ROWS = 64


def for_rows(count, step):
    def one(index, carry):
        step(pl.ds(pl.multiple_of(index * ROWS, ROWS), ROWS))
        return carry

    lax.fori_loop(0, count // ROWS, one, 0)


def for_columns(count, width, step):
    def one(index, carry):
        step(pl.ds(pl.multiple_of(index * width, width), width))
        return carry

    lax.fori_loop(0, count // width, one, 0)


def attention_forward_kernel(
    block, x, gain, shift, weight, normed, qkv, att, att_low, den, state,
    w, fq, fk, terms, landed, sums, s0, s1, s2, s3, wsem,
):
    scan = Scan(terms, landed, sums, state, (s0, s1, s2, s3), False)
    greet(scan.others())
    loads = []
    for slot, third in enumerate((1, 2, 0)):
        load = pltpu.make_async_copy(
            weight.at[:, pl.ds(third * 1024, 1024)], w.at[slot], wsem.at[slot]
        )
        load.start()
        loads.append(load)

    def norm_step(rows):
        scaled, _ = norm_rows(x[rows, :].astype(F32))
        normed[rows, :] = (scaled * gain[...] + shift[...]).astype(BF16)

    for_rows(x.shape[0], norm_step)

    def project(slot, third, feature):
        loads[slot].wait()

        def step(columns):
            raw = dot_nn(normed[...], w[slot, :, columns]).astype(BF16)
            qkv[third, :, columns] = raw
            if feature is not None:
                feature[:, columns] = features(raw.astype(F32))

        for_columns(1024, 512, step)

    project(0, 1, fk)
    project(1, 2, None)

    def local_state(unit):
        rows, columns = unit_slices(unit, block)
        keys = fk[rows, columns]
        square = tn_dot(qkv[2, rows, columns], keys)
        total = jnp.sum(keys.astype(F32), axis=0, keepdims=True)
        blocks, row = pack_state(square, total)
        terms[unit, pl.ds(0, 64)] = blocks
        terms[unit, pl.ds(64, 8)] = row

    for_units(local_state, 4)
    met(SEQ - 1)
    scan.start()
    project(2, 0, fq)
    first, second = head_masks()
    causal = causal_mask(block)

    def local_part(unit):
        rows, columns = unit_slices(unit, block)
        query, key, value = fq[rows, columns], fk[rows, columns], qkv[2, rows, columns]
        scores = dot_nt(jnp.concatenate([query * first, query * second], axis=0), key)
        both = 0.0
        for head, mask in enumerate((first, second)):
            own = jnp.where(causal, scores[head * block : (head + 1) * block], 0.0).astype(BF16)
            right = jnp.concatenate([value * mask, jnp.broadcast_to(mask, value.shape)], axis=1)
            both = both + dot_nn(own, right)
        att[rows, columns] = both[:, :PAIR]
        den[rows, columns] = both[:, PAIR:]

    for_units(local_part, 2)
    scan.middle()
    scan.finish()
    together = same_head()

    def incoming(unit):
        rows, columns = unit_slices(unit, block)
        square, total = unpack_state(state[unit])
        totals = jnp.where(together, jnp.broadcast_to(total, (PAIR, PAIR)), 0.0)
        high, low = split(jnp.concatenate([square, totals], axis=0))
        query = fq[rows, columns]
        both = dot_nt(
            jnp.concatenate([query, query], axis=1), jnp.concatenate([high, low], axis=1)
        )
        denom = den[rows, columns] + both[:, PAIR:]
        den[rows, columns] = denom
        attended = (att[rows, columns] + both[:, :PAIR]) / denom
        att[rows, columns] = attended
        att_low[rows, columns] = attended.astype(BF16)

    for_units(incoming, 2)
    scan.drain()


def attention_forward(x, gain, shift, weight, block):
    rows, width = x.shape
    vmem = pl.BlockSpec(memory_space=pltpu.VMEM)

    def kernel(*refs):
        attention_forward_kernel(block, *refs)

    return pl.pallas_call(
        kernel,
        out_shape=[
            jax.ShapeDtypeStruct((rows, width), BF16),
            jax.ShapeDtypeStruct((3, rows, width), BF16),
            jax.ShapeDtypeStruct((rows, width), F32),
            jax.ShapeDtypeStruct((rows, width), BF16),
            jax.ShapeDtypeStruct((rows, width), F32),
            jax.ShapeDtypeStruct((SEQ, 72, PAIR), F32),
        ],
        in_specs=[vmem, vmem, vmem, pl.BlockSpec(memory_space=pl.ANY)],
        out_specs=[vmem] * 6,
        scratch_shapes=[
            pltpu.VMEM((3, width, width), BF16),
            pltpu.VMEM((rows, width), BF16),
            pltpu.VMEM((rows, width), BF16),
            *SCAN_SCRATCH,
            pltpu.SemaphoreType.DMA((3,)),
        ],
        compiler_params=pltpu.CompilerParams(
            collective_id=5, has_side_effects=True, vmem_limit_bytes=62 * MIB
        ),
    )(x, gain.reshape(1, width), shift.reshape(1, width), weight)


def gelu_both(pre):
    cumulative = 0.5 * (1.0 + lax.erf(pre * (1.0 / math.sqrt(2.0))))
    density = jnp.exp(-0.5 * pre * pre) * (1.0 / math.sqrt(2.0 * math.pi))
    return (pre * cumulative).astype(BF16), (cumulative + pre * density).astype(BF16)


def norm_back(grad, gain, scaled, inverse):
    spread = grad * gain
    first_mean = jnp.mean(spread, axis=-1, keepdims=True)
    second_mean = jnp.mean(spread * scaled, axis=-1, keepdims=True)
    return inverse * (spread - first_mean - scaled * second_mean)


def norm_back_rows(values, grad, base, gain, sums, store):
    sums[...] = jnp.zeros_like(sums)

    def step(rows):
        scaled, inverse = norm_rows(values[rows, :].astype(F32))
        part = grad[rows, :]
        sums[0:1, :] += jnp.sum(part * scaled, axis=0, keepdims=True)
        sums[1:2, :] += jnp.sum(part, axis=0, keepdims=True)
        store(rows, base[rows, :].astype(F32) + norm_back(part, gain[...], scaled, inverse))

    for_rows(grad.shape[0], step)


def feed_forward_kernel(
    x, att_low, gain, shift, cot_in, w_out, w_up, w_down,
    output, gmixed, gatt, sums, norm_cat, pre_cat, down_a, down_b, down_c,
    wo, wu, wd, wsem, hidden, slope, cot_cat, stage, land, land_cot, land_norm,
    slab_a, slab_b, slab_c, swap_sent, swap_came, free, *scratch,
):
    place = Place()
    core = place.core
    rows = x.shape[0]
    others = link_neighbours(place)
    greet(others)
    own, other = pl.ds(0, rows), pl.ds(rows, rows)
    mixed = gatt
    loads = []
    moves = ((w_out, wo), (w_up, wu), (w_down, wd), (cot_in, cot_cat.at[own]))
    for slot in (3, 0, 1, 2):
        loads.append(pltpu.make_async_copy(*moves[slot], wsem.at[slot]))
        loads[-1].start()
    loads.append(loads.pop(0))
    cot = cot_cat.at[own]
    swap = Swap(place, stage, swap_sent, swap_came)
    met(len(others))
    loads[3].wait()
    for tile in range(2):
        columns = pl.ds(tile * TILE, TILE)
        swap.put(tile, tile, cot[:, columns], land_cot.at[tile])
    loads[0].wait()

    def mix(columns):
        mixed[:, columns] = x[:, columns].astype(F32) + dot_nn(att_low[...], wo[:, columns])

    for_columns(1024, TILE, mix)

    def norm_step(index):
        scaled, _ = norm_rows(mixed[index, :])
        norm_cat[index, :] = (scaled * gain[...] + shift[...]).astype(BF16)

    for_rows(rows, norm_step)
    for tile in range(2):
        columns = pl.ds(tile * TILE, TILE)
        swap.put(2 + tile, 2 + tile, norm_cat[own, columns], land_norm.at[tile])
    loads[1].wait()

    def up(columns):
        ours, ours_slope = gelu_both(dot_nn(norm_cat[own, :], wu[:, columns]))
        hidden[:, columns] = ours
        slope[:, columns] = ours_slope
        return ours

    def give(block, carry):
        theirs = up(half_columns(block, 1 - core, 1024))
        swap.put(4 + block, block, theirs, land.at[block], before=block)
        return carry

    lax.fori_loop(0, 4, give, 0)
    for tile in range(2):
        cot_cat[other, pl.ds(tile * TILE, TILE)] = swap.get(tile, land_cot.at[tile])
    slabs = (slab_a, slab_b, slab_c)

    def take(block, carry):
        ours = up(half_columns(block, core, 1024))
        both = jnp.concatenate([ours, swap.get(4 + block, land.at[block])], axis=0)
        for piece, (start, width) in enumerate(DOWN_CUTS):
            product = tn_dot(both, cot_cat[:, pl.ds(start, width)]).reshape(4, 4, 4, 8, width)
            for stream in range(3):
                slabs[stream][block, :, :, :, pl.ds(start, width)] = product[:, :, stream]
            slabs[piece][block, :, :, :, pl.ds(1024, width)] = product[:, :, 3]
        return carry

    lax.fori_loop(0, 4, take, 0)
    pl.semaphore_signal(free, inc=1, device_id=place.partner(), device_id_type=MESH)
    down = Sum(place, slabs, {0: [scratch[4 * k : 4 * k + 4] for k in range(3)]}, 0, 0)
    down.begin()
    loads[2].wait()

    def finish_forward(columns):
        output[:, columns] = (mixed[:, columns] + dot_nn(hidden[...], wd[:, columns])).astype(BF16)

    for_columns(1024, 256, finish_forward)

    def back(columns):
        grad = dot_nt(cot[...], wd[columns, :]) * slope[:, columns].astype(F32)
        low = grad.astype(BF16)
        hidden[:, columns] = low
        return low

    pl.semaphore_wait(free, 1)

    def give_back(block, carry):
        theirs = back(half_columns(block, 1 - core, 1024))
        swap.put(8 + block, block, theirs, land.at[block], before=4 + block)
        return carry

    lax.fori_loop(0, 4, give_back, 0)

    def take_back(block, carry):
        columns = pl.ds(pl.multiple_of(block * TILE, TILE), TILE)
        pre_cat[own, columns] = back(half_columns(block, core, 1024))
        pre_cat[other, columns] = swap.get(8 + block, land.at[block])
        return carry

    lax.fori_loop(0, 4, take_back, 0)
    down.forward()
    for tile in range(2):
        norm_cat[other, pl.ds(tile * TILE, TILE)] = swap.get(2 + tile, land_norm.at[tile])

    def back_up(columns):
        gmixed[:, columns] = dot_nt(hidden[...], wu[columns, :])

    for_columns(1024, 256, back_up)

    def store(index, values):
        gmixed[index, :] = values
        hidden[index, pl.ds(0, 1024)] = values.astype(BF16)

    norm_back_rows(mixed, gmixed, cot, gain, sums, store)

    def back_out(columns):
        gatt[:, columns] = dot_nt(hidden[:, pl.ds(0, 1024)], wo[columns, :])

    for_columns(1024, TILE, back_out)
    down.finish((down_a, down_b, down_c))
    swap.drain(range(8, 12), land.at[0])
    down.drain()


def slab_shapes(widths):
    return [pltpu.VMEM((4, 4, 4, 8, width), F32) for width in widths]


def flat_scratch(by_phase):
    return [item for at in sorted(by_phase) for stream in by_phase[at] for item in stream]


def nest(flat, phases, streams=3):
    nested = {}
    for at in phases:
        nested[at] = [[flat.pop(0) for _ in range(4)] for _ in range(streams)]
    return nested


def struct(shape, dtype=F32):
    return jax.ShapeDtypeStruct(shape, dtype)


VMEM_SPEC = pl.BlockSpec(memory_space=pltpu.VMEM)
ANY_SPEC = pl.BlockSpec(memory_space=pl.ANY)


def call(kernel, outs, operands, in_specs, scratch, collective_id):
    return pl.pallas_call(
        kernel,
        out_shape=outs,
        in_specs=in_specs,
        out_specs=[VMEM_SPEC] * len(outs),
        scratch_shapes=scratch,
        compiler_params=pltpu.CompilerParams(
            collective_id=collective_id, has_side_effects=True, vmem_limit_bytes=63 * MIB
        ),
    )(*operands)


def feed_forward(x, att_low, gain, shift, cot, w_out, w_up, w_down):
    rows, width = x.shape
    wide = w_up.shape[1]
    outs = [
        struct((rows, width), BF16),
        struct((rows, width)),
        struct((rows, width)),
        struct((8, width)),
        struct((2 * rows, width), BF16),
        struct((2 * rows, wide // 2), BF16),
        *[struct((4, 4, 8, length)) for length in DOWN_WIDTHS],
    ]
    scratch = [
        pltpu.VMEM((width, width), BF16),
        pltpu.VMEM((width, wide), BF16),
        pltpu.VMEM((wide, width), BF16),
        pltpu.SemaphoreType.DMA((4,)),
        pltpu.VMEM((rows, wide), BF16),
        pltpu.VMEM((rows, wide), BF16),
        pltpu.VMEM((2 * rows, width), BF16),
        pltpu.VMEM((4, rows, TILE), F32),
        pltpu.VMEM((4, rows, TILE), F32),
        pltpu.VMEM((2, rows, TILE), F32),
        pltpu.VMEM((2, rows, TILE), F32),
        *slab_shapes(DOWN_WIDTHS),
        pltpu.SemaphoreType.DMA((12,)),
        pltpu.SemaphoreType.DMA((12,)),
        pltpu.SemaphoreType.REGULAR,
        *flat_scratch(sum_scratch(DOWN_WIDTHS, 0, 0)),
    ]
    specs = [VMEM_SPEC] * 4 + [ANY_SPEC] * 4
    operands = (x, att_low, gain, shift, cot, w_out, w_up, w_down)
    return call(feed_forward_kernel, outs, operands, specs, scratch, 1)


UP_WIDTHS = shared_widths(2048)
OUT_WIDTHS = shared_widths(512)
QKV_WIDTHS = shared_widths(1536)


def attention_backward_kernel(
    block, qkv, att, den, state, gatt, gmixed, normed, norm_cat, pre_cat, down_in_a, down_in_b, down_in_c,
    gqkv, norm_one_cat, gqkv_cat, grad_down, up_a, up_b, up_c, out_a, out_b, out_c,
    grads, terms, landed, sums, result, s0, s1, s2, s3,
    att_cat, mixed_cat, stage, land_att, land_mixed, land_norm, land_gqkv, swap_sent, swap_came,
    slab_a, slab_b, slab_c, down_a, down_b, down_c, *scratch,
):
    place = Place()
    core = place.core
    rows = gatt.shape[0]
    scratch = list(scratch)
    scan = Scan(terms, landed, sums, result, (s0, s1, s2, s3), True)
    others = link_neighbours(place) + scan.others()
    greet(others)
    down_work = (down_a, down_b, down_c)
    for source, target in zip((down_in_a, down_in_b, down_in_c), down_work):
        add_into(target, source)
    down = Sum(place, down_work, nest(scratch, (1, 2)), 1, 2)
    slabs = (slab_a, slab_b, slab_c)
    up = Sum(place, slabs, nest(scratch, (0,)), 0, 0)
    swap = Swap(place, stage, swap_sent, swap_came)
    met(len(others))
    down.begin()
    own, other = pl.ds(0, rows), pl.ds(rows, rows)
    att_cat[own, :] = att[...].astype(BF16)
    norm_one_cat[own, :] = normed[...]
    for tile in range(2):
        columns = pl.ds(tile * TILE, TILE)
        swap.put(tile, tile, att_cat[own, columns], land_att.at[tile])
        swap.put(2 + tile, 2 + tile, normed[:, columns], land_norm.at[tile])
    shared_product(norm_cat, pre_cat, slabs, 2048)
    up.begin()
    mixed_cat[own, :] = gmixed[:, half_tile(0, core)].astype(BF16)
    swap.put(4, 0, gmixed[:, half_tile(0, 1 - core)].astype(BF16), land_mixed, before=0)
    first, second = head_masks()
    first_wide = first_head(block)

    def slopes(index, columns):
        numer = gatt[index, columns] / den[index, columns]
        product = numer * att[index, columns]
        ours = jnp.sum(jnp.where(first_wide, product, 0.0), axis=1, keepdims=True)
        theirs = jnp.sum(jnp.where(first_wide, 0.0, product), axis=1, keepdims=True)
        return numer, -ours, -theirs

    def local_state(unit):
        index, columns = unit_slices(unit, block)
        numer, one, two = slopes(index, columns)
        query = features(qkv[0, index, columns].astype(F32))
        high, low = split(numer)
        wide = tn_dot(query, jnp.concatenate([high, low], axis=1))
        spread = jnp.where(first_wide, one, two)
        total = jnp.sum(query.astype(F32) * spread, axis=0, keepdims=True)
        blocks, row = pack_state(wide[:, :PAIR] + wide[:, PAIR:], total)
        terms[unit, pl.ds(0, 64)] = blocks
        terms[unit, pl.ds(64, 8)] = row

    for_units(local_state, 2)
    scan.start()
    down.forward()
    causal = causal_mask(block)
    causal_t = causal_mask(block, True)

    def local_part(unit):
        index, columns = unit_slices(unit, block)
        raw_query = qkv[0, index, columns].astype(F32)
        query, value = features(raw_query), qkv[2, index, columns]
        key = features(qkv[1, index, columns].astype(F32))
        numer, one, two = slopes(index, columns)
        high, low = split(numer)
        scores = dot_nt(jnp.concatenate([key * first, key * second], axis=0), query)
        wide = jnp.concatenate([high, low], axis=1)
        values = jnp.concatenate([value, value], axis=1)
        grad_query, grad_key, grad_value = 0.0, 0.0, 0.0
        for head, (mask, slope) in enumerate(((first, one), (second, two))):
            mask_wide = jnp.concatenate([mask, mask], axis=1)
            mixing = jnp.where(causal, dot_nt(wide * mask_wide, values) + slope, 0.0).astype(BF16)
            turned = jnp.where(causal_t, scores[head * block : (head + 1) * block], 0.0)
            grad_query = grad_query + dot_nn(mixing, key * mask)
            grad_key = grad_key + tn_dot(mixing, query * mask)
            grad_value = grad_value + dot_nn(turned.astype(BF16), high * mask)
        square, total = unpack_state(state[unit])
        state_high, state_low = split(square)
        grad_query = grad_query + dot_nn(
            jnp.concatenate([high, low], axis=1),
            jnp.concatenate([state_high, state_high], axis=0),
        )
        grad_query = grad_query + dot_nn(high, state_low)
        grad_query = grad_query + jnp.where(first_wide, one, two) * total
        gqkv[0, index, columns] = (grad_query * feature_slope(raw_query)).astype(BF16)
        grads[0, index, columns] = grad_key
        grads[1, index, columns] = grad_value

    def local_parts(start, count):
        def one(index, carry):
            local_part(start + index)
            return carry

        lax.fori_loop(0, count, one, 0)

    local_parts(0, 4)
    down.finish()
    local_parts(4, 3)
    down.forward()
    scan.middle()
    local_parts(7, 4)
    down.finish()
    up.forward()
    for stream in range(3):
        piece = down.pieces[stream]
        grad_down[pl.ds(8 * stream, 8), :] = piece[:, pl.ds(0, 1024)]
        start, width = DOWN_CUTS[stream]
        grad_down[pl.ds(24, 8), pl.ds(start, width)] = piece[:, pl.ds(1024, width)]
    local_parts(11, 5)
    for tile in range(2):
        columns = pl.ds(tile * TILE, TILE)
        att_cat[other, columns] = swap.get(tile, land_att.at[tile])
        norm_one_cat[other, columns] = swap.get(2 + tile, land_norm.at[tile])
    mixed_cat[other, :] = swap.get(4, land_mixed)
    shared_product(att_cat, mixed_cat, (out_a, out_b, out_c), 512)
    scan.finish()

    def incoming(unit):
        index, columns = unit_slices(unit, block)
        square, total = unpack_state(result[unit])
        high, low = split(square)
        raw_key = qkv[1, index, columns].astype(F32)
        key, value = features(raw_key), qkv[2, index, columns]
        grad_key = grads[0, index, columns] + total
        grad_key = grad_key + dot_nt(
            jnp.concatenate([value, value], axis=1), jnp.concatenate([high, low], axis=1)
        )
        grad_value = grads[1, index, columns] + dot_nn(
            jnp.concatenate([key, key], axis=1), jnp.concatenate([high, low], axis=0)
        )
        gqkv[1, index, columns] = (grad_key * feature_slope(raw_key)).astype(BF16)
        gqkv[2, index, columns] = grad_value.astype(BF16)

    for_units(incoming, 2)
    before = (1, 2, 3)
    for third in range(3):
        theirs = gqkv[third, :, half_tile(0, 1 - core)]
        swap.put(5 + third, 1 + third, theirs, land_gqkv.at[third], before=before[third])
    for third in range(3):
        columns = pl.ds(third * TILE, TILE)
        gqkv_cat[own, columns] = gqkv[third, :, half_tile(0, core)]
        gqkv_cat[other, columns] = swap.get(5 + third, land_gqkv.at[third])
    up.finish((up_a, up_b, up_c))
    swap.copy(4, 0, land_mixed).wait_send()
    for third in range(3):
        swap.copy(5 + third, 1 + third, land_gqkv.at[third]).wait_send()
    scan.drain()
    up.drain()
    down.drain()


def attention_backward(qkv, att, den, state, gatt, gmixed, normed, norm_cat, pre_cat, down, block):
    _, rows, width = qkv.shape

    def kernel(*refs):
        attention_backward_kernel(block, *refs)

    outs = [
        struct((3, rows, width), BF16),
        struct((2 * rows, width), BF16),
        struct((2 * rows, 3 * TILE), BF16),
        struct((32, width)),
        *[struct((4, 4, 8, length)) for length in UP_WIDTHS],
        *[struct((4, 4, 4, 8, length)) for length in OUT_WIDTHS],
    ]
    scratch = [
        pltpu.VMEM((2, rows, width), F32),
        SCAN_SCRATCH[0],
        *SCAN_SCRATCH,
        pltpu.VMEM((2 * rows, width), BF16),
        pltpu.VMEM((2 * rows, TILE), BF16),
        pltpu.VMEM((4, rows, TILE), F32),
        pltpu.VMEM((2, rows, TILE), F32),
        pltpu.VMEM((rows, TILE), F32),
        pltpu.VMEM((2, rows, TILE), F32),
        pltpu.VMEM((3, rows, TILE), F32),
        pltpu.SemaphoreType.DMA((8,)),
        pltpu.SemaphoreType.DMA((8,)),
        *slab_shapes(UP_WIDTHS),
        *[pltpu.VMEM((4, 4, 8, length), F32) for length in DOWN_WIDTHS],
        *flat_scratch(sum_scratch(DOWN_WIDTHS, 1, 2)),
        *flat_scratch(sum_scratch(UP_WIDTHS, 0, 0)),
    ]
    operands = (qkv, att, den, state, gatt, gmixed, normed, norm_cat, pre_cat, *down)
    return call(kernel, outs, operands, [VMEM_SPEC] * len(operands), scratch, 2)


def last_kernel(
    x, gain, norm_one_cat, gqkv, gqkv_cat, gmixed, sums_two, weight,
    up_in_a, up_in_b, up_in_c, out_in_a, out_in_b, out_in_c,
    grad_input, grad_up, grad_out, grad_qkv, grad_gains,
    w, wsem, sums, up_rows, up_land, out_rows, out_land, qkv_rows, qkv_land, row_sems,
    vec_slab, vec_land, vec_sems,
    up_a, up_b, up_c, out_a, out_b, out_c, qkv_a, qkv_b, qkv_c, *scratch,
):
    place = Place()
    scratch = list(scratch)
    others = link_neighbours(place)
    greet(others)
    load = pltpu.make_async_copy(weight, w, wsem.at[0])
    load.start()
    up_work, out_work, qkv_work = (up_a, up_b, up_c), (out_a, out_b, out_c), (qkv_a, qkv_b, qkv_c)
    for source, target in zip((up_in_a, up_in_b, up_in_c), up_work):
        add_into(target, source)
    for source, target in zip((out_in_a, out_in_b, out_in_c), out_work):
        for index in range(4):
            add_into(target.at[index], source.at[index])
    up = Sum(place, up_work, nest(scratch, (1, 2)), 1, 2)
    out = Sum(place, out_work, nest(scratch, (0, 1, 2)))
    qkv = Sum(place, qkv_work, nest(scratch, (0, 1, 2)))
    vec = Sum(place, (vec_slab,), nest(scratch, (0, 1, 2), 1))
    met(len(others))
    up.begin()
    out.begin()
    shared_product(norm_one_cat, gqkv_cat, qkv_work, 3 * TILE)
    qkv.begin()
    load.wait()

    def back_norm(columns):
        total = 0.0
        for third in range(3):
            total = total + dot_nt(gqkv[third], w[columns, pl.ds(third * 1024, 1024)])
        grad_input[:, columns] = total

    for_columns(1024, 256, back_norm)
    up.forward()

    def store(index, values):
        grad_input[index, :] = values

    norm_back_rows(x, grad_input, gmixed, gain, sums, store)
    row = lax.broadcasted_iota(jnp.int32, (8, 1), 0)
    four = jnp.concatenate([sums[0:2, :], sums_two[0:2, :]], axis=0)
    eight = jnp.concatenate([four, four], axis=0)
    turned = jnp.transpose(jnp.concatenate([eight, jnp.zeros((120, 1024), F32)], axis=0))
    turned = turned.reshape(4, 2, 4, 4, 8, 128)
    lane = lax.broadcasted_iota(jnp.int32, (8, 128), 1)
    vec_slab[...] = jnp.where(lane < 4, turned[:, 0], jnp.where(lane < 8, turned[:, 1], 0.0))
    vec.begin()
    up.finish()
    out.forward()
    vec.forward()
    up.forward()
    out.finish()
    vec.finish()
    out.forward()
    up.finish()
    vec.forward()
    qkv.forward()
    out.finish()
    vec.finish()
    out.forward()
    vec.forward()
    out.finish()
    vec.finish()
    swaps = []

    def swap_rows(pieces, columns, rows, land, slot):
        shared_rows(pieces, columns, rows)
        copy = row_swap(place, rows, land, row_sems.at[slot])
        copy.start()
        swaps.append(copy)

    swap_rows(up.pieces, 2048, up_rows, up_land, 0)
    swap_rows(out.pieces, 512, out_rows, out_land, 1)
    vec_tile = vec.pieces[0]
    vec_copy = pltpu.make_async_remote_copy(
        src_ref=vec_tile,
        dst_ref=vec_land,
        send_sem=vec_sems.at[0],
        recv_sem=vec_sems.at[1],
        device_id=place.partner(),
        device_id_type=MESH,
    )
    vec_copy.start()
    swaps[0].wait()
    lay_rows(place, up_rows, up_land, grad_up)
    swaps[1].wait()
    lay_rows(place, out_rows, out_land, grad_out)
    vec_copy.wait()
    grad_gains[...] = vec_tile[...] + vec_land[...]
    qkv.finish()
    qkv.forward()
    qkv.finish()
    qkv.forward()
    qkv.finish()
    swap_rows(qkv.pieces, 3 * TILE, qkv_rows, qkv_land, 2)
    swaps[2].wait()
    lay_rows(place, qkv_rows, qkv_land, grad_qkv)
    for each in (up, out, qkv, vec):
        each.drain()


def last_part(x, gain, norm_one_cat, gqkv, gqkv_cat, gmixed, sums_two, weight, up, out):
    rows, width = x.shape
    outs = [
        struct((rows, width)),
        struct((8, 4096)),
        struct((8, width)),
        struct((8, 3 * width)),
        struct((8, 128)),
    ]
    scratch = [
        pltpu.VMEM((width, 3 * width), BF16),
        pltpu.SemaphoreType.DMA((1,)),
        pltpu.VMEM((8, width), F32),
        pltpu.VMEM((2, 8, 2048), F32),
        pltpu.VMEM((8, 2048), F32),
        pltpu.VMEM((2, 8, 512), F32),
        pltpu.VMEM((8, 512), F32),
        pltpu.VMEM((2, 8, 1536), F32),
        pltpu.VMEM((8, 1536), F32),
        pltpu.SemaphoreType.DMA((3, 2)),
        pltpu.VMEM((4, 4, 4, 8, 128), F32),
        pltpu.VMEM((8, 128), F32),
        pltpu.SemaphoreType.DMA((2,)),
        *[pltpu.VMEM((4, 4, 8, length), F32) for length in UP_WIDTHS],
        *slab_shapes(OUT_WIDTHS),
        *slab_shapes(QKV_WIDTHS),
        *flat_scratch(sum_scratch(UP_WIDTHS, 1, 2)),
        *flat_scratch(sum_scratch(OUT_WIDTHS)),
        *flat_scratch(sum_scratch(QKV_WIDTHS)),
        *flat_scratch(sum_scratch((128,))),
    ]
    operands = (x, gain, norm_one_cat, gqkv, gqkv_cat, gmixed, sums_two, weight, *up, *out)
    specs = [VMEM_SPEC] * len(operands)
    specs[7] = ANY_SPEC
    return call(last_kernel, outs, operands, specs, scratch, 3)


def body(
    inputs,
    first_gain,
    first_shift,
    qkv_weight,
    out_weight,
    second_gain,
    second_shift,
    up_weight,
    down_weight,
    cotangent,
):
    sequences, block, width = inputs.shape
    rows = sequences * block
    x = inputs.reshape(rows, width)
    cot = cotangent.reshape(rows, width)
    gain_one, gain_two = first_gain.reshape(1, width), second_gain.reshape(1, width)
    shift_two = second_shift.reshape(1, width)
    normed, qkv, att, att_low, den, state = attention_forward(
        x, first_gain, first_shift, qkv_weight, block
    )
    output, gmixed, gatt, sums_two, norm_cat, pre_cat, *down = feed_forward(
        x, att_low, gain_two, shift_two, cot, out_weight, up_weight, down_weight
    )
    gqkv, norm_one_cat, gqkv_cat, grad_down, *rest = attention_backward(
        qkv, att, den, state, gatt, gmixed, normed, norm_cat, pre_cat, down, block
    )
    grad_input, grad_up, grad_out, grad_qkv, gains = last_part(
        x, gain_one, norm_one_cat, gqkv, gqkv_cat, gmixed, sums_two, qkv_weight, rest[:3], rest[3:]
    )
    core = lax.rem(lax.axis_index("dp"), 2)
    gains = lax.dynamic_slice(gains, (0, 4 * core), (8, 4))
    return (
        output.reshape(inputs.shape),
        grad_input.reshape(inputs.shape),
        grad_qkv,
        grad_out,
        grad_up,
        grad_down,
        *[gains[:, k] for k in range(4)],
    )


def solution(mesh):
    return jax.shard_map(
        body,
        mesh=mesh,
        in_specs=(
            P("dp", "seq", None),
            P(),
            P(),
            P(),
            P(),
            P(),
            P(),
            P(),
            P(),
            P("dp", "seq", None),
        ),
        out_specs=(
            P("dp", "seq", None),
            P("dp", "seq", None),
            P(("dp", "seq"), None),
            P(("dp", "seq"), None),
            P(("dp", "seq"), None),
            P(("dp", "seq"), None),
            P(("dp", "seq")),
            P(("dp", "seq")),
            P(("dp", "seq")),
            P(("dp", "seq")),
        ),
        check_vma=False,
    )
```

time: 420 us -> 232 us (0.55); the launches traced: 413 us -> 231 us
  blocking collectives: 65.4 us -> 0 us
  matrix products: 51.8 us -> 0 us
  Pallas kernels: 270 us -> 224 us
  other arithmetic: 13.6 us -> 0 us
  local copies, waits for them, and re-layouts: 10.9 us -> 6.22 us
    unnamed x1 -> x0, blocking collectives: 65.4 us -> none
    dot_general x7 -> x0, matrix products: 51.8 us -> none  [the longest x4 20.6 us: back_dot(): lax.dot_general(left, right, (((1,), (1,)), ((), ())), preferred_element_...]
    pallas_call x5 -> x3, Pallas kernels: 236 us -> 190 us  [call(): pl.pallas_call(kernel, out_shape=outs, in_specs=in_specs, out_specs=[VMEM...]
where the time goes in v3:
time: 232 us; the launch traced here: 231 us
  Pallas kernels  224 us (97%)
  local copies, waits for them, and re-layouts  6.22 us (3%)
    pallas_call x3, Pallas kernels, call(): pl.pallas_call(kernel, out_shape=outs, in_specs=in_specs, out_specs=[VMEM...  190 us
    pallas_call x1, Pallas kernels, attention_forward(): pl.pallas_call(kernel, out_shape=[jax.ShapeDtypeStruct((rows, width), BF1...  34.1 us

profile of v3, /device:TPU:0, one launch (start us, length us, event | category | flops | bytes accessed | tf_op | source)
XLA Modules:
  0.0 230.5 jit_solution(7729321766393570289)
XLA Ops:
  0.6 34.1 %shard_map.177 = (bf16[384,1024]{1,0:T(8,128)(2,1)}, bf16[3,384,1024]{2,1,0:T(8,128)(2,1)}, f32[384,1024]{1,0:T(8,128)}, bf16[384,1024]{1,0:T(8,128)(2,1)}, f32[384,1024]{1,0:T(8,128)}, /*index=5*/f32[16,72,128]{2,1,0:T(8,128)}) custom-call(bf16[384,1024]{1,0:T(8,128)(2,1)} %bitcast.8, f32[1,1024]{1,0:T(1,128)} %bitcast.14, f32[1,1024]{1,0:T(1,128)} %bitcast.16, ...), custom_call_target="tpu_custom_call" | custom-call | tf_op jit(solution)/shard_map/pallas_call | solution.py:591
  34.7 50.9 %shard_map.178 = (bf16[384,1024]{1,0:T(8,128)(2,1)}, f32[384,1024]{1,0:T(8,128)}, f32[384,1024]{1,0:T(8,128)}, f32[8,1024]{1,0:T(8,128)}, bf16[768,1024]{1,0:T(8...) custom-call(bf16[384,1024]{1,0:T(8,128)(2,1)} %bitcast.9, ...), custom_call_target="tpu_custom_call" | custom-call | tf_op jit(solution)/shard_map/pallas_call | solution.py:792
  85.6 64.3 %shard_map.179 = (bf16[3,384,1024]{2,1,0:T(8,128)(2,1)}, bf16[768,1024]{1,0:T(8,128)(2,1)}, bf16[768,1536]{1,0:T(8,128)(2,1)}, f32[32,1024]{1,0:T(8,128)}, f32[4...) custom-call(bf16[3,384,1024]{2,1,0:T(8,128)(2,1)} %get-tuple-element, ...), custom_call_target="tpu_custom_call" | custom-call | tf_op jit(solution)/shard_map/pallas_call | solution.py:792
  149.9 0.0 copy-start.1
  149.9 74.4 %shard_map.180 = (f32[384,1024]{1,0:T(8,128)}, f32[8,4096]{1,0:T(8,128)}, f32[8,1024]{1,0:T(8,128)}, f32[8,3072]{1,0:T(8,128)}, f32[8,128]{1,0:T(8,128)}) custom-call(bf16[384,1024]{1,0:T(8,128)(2,1)} %bitcast.10, f32[1,1024]{1,0:T(1,128)} %bitcast.15, bf16[768,1024]{1,0:T(8,128)(2,1)} %get-tuple-element.54.norm_one_cat, ...), custom_call_target="tpu_custom_call" | custom-call | tf_op jit(solution)/shard_map/pallas_call | solution.py:792
  224.3 0.0 copy-start
  224.3 0.9 constant_dynamic-slice_fusion
  225.2 0.7 slice_reduce_fusion
  225.9 0.0 copy-done.1
  225.9 0.0 copy-start.4
  225.9 0.0 copy-start.5
  225.9 0.0 copy-start.3
  225.9 0.9 copy.26
  226.8 0.0 copy-done
  226.8 0.0 copy-start.2
  226.8 1.1 copy.27
  228.0 0.0 copy-done.4
  228.0 0.6 copy.28
  228.6 0.0 copy-done.5
  228.6 0.6 copy.29
  229.2 0.0 copy-done.3
  229.2 0.7 copy.30
  229.9 0.0 copy-done.2
  229.9 0.7 copy.31
Async XLA Ops:
  149.9 76.0 %copy-start.1 = (bf16[384,1024]{1,0:T(8,128)(2,1)S(1)}, bf16[384,1024]{1,0:T(8,128)(2,1)}, u32[]{:S(2)}) copy-start(bf16[384,1024]{1,0:T(8,128)(2,1)} %get-tuple-element.41) | copy-start | bytes 2359300
  224.3 2.5 %copy-start = (f32[384,1024]{1,0:T(8,128)S(1)}, f32[384,1024]{1,0:T(8,128)}, u32[]{:S(2)}) copy-start(f32[384,1024]{1,0:T(8,128)} %get-tuple-element.64) | copy-start | bytes 4718596
  225.9 2.0 copy-start.4
  225.9 2.7 %copy-start.5 = (f32[8,1024]{1,0:T(8,128)S(1)}, f32[8,1024]{1,0:T(8,128)}, u32[]{:S(2)}) copy-start(f32[8,1024]{1,0:T(8,128)} %get-tuple-element.87) | copy-start | bytes 98308
  225.9 3.3 %copy-start.3 = (f32[8,4096]{1,0:T(8,128)S(1)}, f32[8,4096]{1,0:T(8,128)}, u32[]{:S(2)}) copy-start(f32[8,4096]{1,0:T(8,128)} %get-tuple-element.88) | copy-start | bytes 393220
  226.8 3.1 %copy-start.2 = (f32[32,1024]{1,0:T(8,128)S(1)}, f32[32,1024]{1,0:T(8,128)}, u32[]{:S(2)}) copy-start(f32[32,1024]{1,0:T(8,128)} %get-tuple-element.89) | copy-start | bytes 393220

commit v4 on v3

v4 whole, which is shorter than its diff:
```python
import math

import jax
import jax.numpy as jnp
from jax import lax
from jax.experimental import pallas as pl
from jax.experimental.pallas import tpu as pltpu
from jax.sharding import PartitionSpec as P

MESH = pl.DeviceIdType.MESH
F32 = jnp.float32
BF16 = jnp.bfloat16
RING = 4
MIB = 2**20


class Place:
    def __init__(self):
        dp, seq = lax.axis_index("dp"), lax.axis_index("seq")
        self.core = lax.rem(dp, 2)
        self.at = (lax.div(dp, 2), lax.div(seq, RING), lax.rem(seq, RING))

    def id_of(self, x, y, z, core):
        return (x * 2 + core, y * RING + z)

    def ring(self, axis, step):
        return lax.rem(self.at[axis] + (step + RING), RING)

    def neighbour(self, axis, step):
        at = list(self.at)
        at[axis] = self.ring(axis, step)
        return self.id_of(*at, self.core)

    def partner(self):
        return self.id_of(*self.at, 1 - self.core)


def greet(others):
    barrier = pltpu.get_barrier_semaphore()
    for other in others:
        pl.semaphore_signal(barrier, inc=1, device_id=other, device_id_type=MESH)


def met(count):
    pl.semaphore_wait(pltpu.get_barrier_semaphore(), count)


def link_neighbours(place):
    others = [place.neighbour(axis, step) for axis in range(3) for step in (1, -1)]
    return [*others, place.partner()]


ORDERS = ((0, 1, 2), (1, 2, 0), (2, 0, 1))


def phase_scratch(remaining, length):
    if remaining:
        half = (2, 2, *[4] * (remaining - 1), 8, length)
    else:
        half = (2, 8, (length // 128 + 1) // 2 * 128)
    return [
        pltpu.VMEM((2, *[4] * remaining, 8, length), F32),
        pltpu.VMEM(half, F32),
        pltpu.SemaphoreType.DMA((6,)),
        pltpu.SemaphoreType.DMA((6,)),
    ]


class Phase:
    def __init__(self, place, data, axes, axis, scratch):
        self.place, self.data, self.axis = place, data, axis
        self.where = axes.index(axis)
        self.full, self.half, self.sent, self.came = scratch
        self.flying = []
        self.flat = len(axes) == 1
        self.length = data.shape[-1]
        self.cut = (self.length // 128 + 1) // 2 * 128
        self.whole = self.flat and self.cut == self.length

    def empty(self, which):
        return self.whole and which == 1

    def chunk(self, target):
        index = [slice(None)] * self.where + [target]
        return self.data.at[tuple(index)]

    def part(self, ref, which):
        if not self.flat:
            return ref.at[pl.ds(2 * which, 2)]
        if which == 0:
            return ref.at[:, pl.ds(0, self.cut)]
        return ref.at[:, pl.ds(self.cut, self.length - self.cut)]

    def through(self, way):
        ref = self.half.at[way]
        if self.flat and way == 1:
            return ref.at[:, pl.ds(0, self.length - self.cut)]
        return ref

    def copy(self, kind, way, source, target):
        number = kind * 2 + way
        return pltpu.make_async_remote_copy(
            src_ref=source,
            dst_ref=target,
            send_sem=self.sent.at[number],
            recv_sem=self.came.at[number],
            device_id=self.place.neighbour(self.axis, 1 - 2 * way),
            device_id_type=MESH,
        )

    def send(self, kind, way, source, target):
        copy = self.copy(kind, way, source, target)
        copy.start()
        self.flying.append(copy)

    def beside(self, way):
        return self.chunk(self.place.ring(self.axis, 1 - 2 * way))

    def begin_far(self):
        opposite = self.chunk(self.place.ring(self.axis, 2))
        for way in range(2):
            if not self.empty(way):
                self.send(0, way, self.part(opposite, way), self.through(way))

    def begin_near(self):
        for way in range(2):
            if self.empty(1 - way):
                continue
            target = self.part(self.full.at[way], 1 - way)
            self.send(1, way, self.part(self.beside(way), 1 - way), target)

    def begin(self):
        self.begin_far()
        self.begin_near()

    def forward(self):
        for way in range(2):
            if self.empty(way):
                continue
            came = self.through(way)
            self.copy(0, way, came, came).wait_recv()
            own = self.part(self.beside(way), way)
            add_into(own, own, came)
            self.send(2, way, own, self.part(self.full.at[way], way))

    def finish(self, out=None):
        own = self.chunk(self.place.at[self.axis])
        for way in range(2):
            for kind, which in ((1, 1 - way), (2, way)):
                if self.empty(which):
                    continue
                target = self.part(self.full.at[way], which)
                self.copy(kind, way, target, target).wait_recv()
        add_into(own if out is None else out, own, self.full.at[0], self.full.at[1])
        return own

    def drain(self):
        for copy in self.flying:
            copy.wait_send()


class Direct:
    def __init__(self, place, data, axes, axis, scratch):
        self.place, self.data, self.axis = place, data, axis
        self.where = axes.index(axis)
        self.full, self.sent, self.came = scratch
        self.flying = []

    def chunk(self, target):
        index = [slice(None)] * self.where + [target]
        return self.data.at[tuple(index)]

    def copy(self, step, source):
        return pltpu.make_async_remote_copy(
            src_ref=source,
            dst_ref=self.full.at[step - 1],
            send_sem=self.sent.at[step - 1],
            recv_sem=self.came.at[step - 1],
            device_id=self.place.neighbour(self.axis, step),
            device_id_type=MESH,
        )

    def begin(self):
        for step in (2, 1, 3):
            copy = self.copy(step, self.chunk(self.place.ring(self.axis, step)))
            copy.start()
            self.flying.append(copy)

    def forward(self):
        pass

    def finish(self, out=None):
        own = self.chunk(self.place.at[self.axis])
        for step in (1, 2, 3):
            self.copy(step, self.full.at[step - 1]).wait_recv()
        add_into(own if out is None else out, own, *[self.full.at[k] for k in range(3)])
        return own

    def drain(self):
        for copy in self.flying:
            copy.wait_send()


class Stream:
    def __init__(self, place, data, order, scratch):
        self.place, self.data, self.scratch = place, data, scratch
        self.todo, self.old = [axis for axis in order], []
        self.axes = sorted(order)
        self.phase = None

    def prepare(self):
        scratch = self.scratch.pop(0)
        kind = Phase if len(scratch) == 4 else Direct
        self.phase = kind(self.place, self.data, self.axes, self.todo[0], scratch)
        return self.phase

    def begin(self):
        self.prepare().begin()

    def forward(self):
        self.phase.forward()

    def finish(self, out=None):
        own = self.phase.finish(out)
        self.data = own if out is None else out
        self.axes.remove(self.todo.pop(0))
        self.old.append(self.phase)

    def proceed(self):
        self.finish()
        self.begin()

    def drain(self):
        for phase in self.old:
            phase.drain()
        self.old = []


def direct_scratch(remaining, length):
    return [
        pltpu.VMEM((3, *[4] * remaining, 8, length), F32),
        pltpu.SemaphoreType.DMA((3,)),
        pltpu.SemaphoreType.DMA((3,)),
    ]


def stream_scratch(length, phases, direct=()):
    return [
        (direct_scratch if phase in direct else phase_scratch)(2 - phase, length)
        for phase in phases
    ]


class Taker:
    def __init__(self, refs):
        self.refs = list(refs)

    def __call__(self, like):
        if isinstance(like, list):
            return [self(item) for item in like]
        return self.refs.pop(0)


def flatten(items):
    if isinstance(items, list):
        return [leaf for item in items for leaf in flatten(item)]
    return [items]


def add_into(out, *terms):
    if len(out.shape) > 2:

        def row(index, carry):
            add_into(out.at[index], *[term.at[index] for term in terms])
            return carry

        if len(out.shape) == 4:
            lax.fori_loop(0, out.shape[0], row, 0)
        else:
            for index in range(out.shape[0]):
                row(index, 0)
        return
    total = terms[0][...]
    for term in terms[1:]:
        total = total + term[...]
    out[...] = total


def tn_dot(left, right):
    return lax.dot_general(left, right, (((0,), (0,)), ((), ())), preferred_element_type=F32)


TILE = 512


class Swap:
    def __init__(self, place, stage, sent, came):
        self.place, self.stage, self.sent, self.came = place, stage, sent, came

    def copy(self, number, slot, target):
        return pltpu.make_async_remote_copy(
            src_ref=self.stage.at[slot],
            dst_ref=target,
            send_sem=self.sent.at[number],
            recv_sem=self.came.at[number],
            device_id=self.place.partner(),
            device_id_type=MESH,
        )

    def put(self, number, slot, values, target, before=None):
        if before is not None:
            self.copy(before, slot, target).wait_send()
        self.stage[slot] = values.astype(F32)
        self.copy(number, slot, target).start()

    def get(self, number, target):
        self.copy(number, 0, target).wait_recv()
        return target[...].astype(BF16)

    def drain(self, numbers, target):
        for number in numbers:
            self.copy(number, number % 4, target).wait_send()


def half_columns(block, core, quarter):
    half = quarter // 2
    return pl.ds(pl.multiple_of(block * quarter + core * half, half), half)


def half_tile(index, core):
    return pl.ds(pl.multiple_of((2 * index + core) * TILE, TILE), TILE)


def core_product(left, core, right, start, width, slab, at):
    done = 0
    while done < width:
        step = min(TILE, width - done)
        product = tn_dot(left[core], right[:, pl.ds(start + done, step)])
        slab[:, :, :, :, pl.ds(at + done, step)] = product.reshape(4, 4, 4, 8, step)
        done += step


UP_WIDTHS = (1536, 1280, 1280)
OUT_WIDTHS = (512, 256, 256)
QKV_WIDTHS = (1152, 896, 1024)


def stream_pieces(stream, widths, columns):
    if stream < 2:
        return [(stream, 0, widths[stream], 0)]
    pieces, at = [], 0
    for core in range(2):
        width = columns - widths[core]
        if width:
            pieces.append((core, widths[core], width, at))
        at += width
    return pieces


def stream_product(stream, left, right, slab, widths, columns):
    for core, start, width, at in stream_pieces(stream, widths, columns):
        core_product(left, core, right, start, width, slab, at)


def shared_rows(streams, widths, columns, rows):
    for stream in range(3):
        for core, start, width, at in stream_pieces(stream, widths, columns):
            rows[core, :, pl.ds(start, width)] = streams[stream].data[:, pl.ds(at, width)]


def row_swap(place, rows, land, sems):
    return pltpu.make_async_remote_copy(
        src_ref=rows.at[1 - place.core],
        dst_ref=land,
        send_sem=sems.at[0],
        recv_sem=sems.at[1],
        device_id=place.partner(),
        device_id_type=MESH,
    )


def lay_rows(place, rows, land, out):
    for tile in range(land.shape[1] // TILE):
        columns = pl.ds(tile * TILE, TILE)
        out[:, half_tile(tile, place.core)] = rows[place.core, :, columns]
        out[:, half_tile(tile, 1 - place.core)] = land[:, columns]


DOWN_CUTS = ((0, 384), (384, 384), (768, 256))
DOWN_WIDTHS = (1408, 1408, 1280)


SEQ = 16
PAIR = 128
NT = (((1,), (1,)), ((), ()))
TN = (((0,), (0,)), ((), ()))


def dot_nt(left, right):
    return lax.dot_general(left, right, NT, preferred_element_type=F32)


def dot_nn(left, right):
    return jnp.dot(left, right, preferred_element_type=F32)


def split(values):
    high = values.astype(BF16)
    return high, (values - high.astype(F32)).astype(BF16)


def features(raw):
    return jnp.where(raw > 0, raw + 1.0, jnp.exp(jnp.minimum(raw, 0.0))).astype(BF16)


def feature_slope(raw):
    return jnp.where(raw > 0, 1.0, jnp.exp(jnp.minimum(raw, 0.0)))


def head_masks():
    lane = lax.broadcasted_iota(jnp.int32, (1, PAIR), 1)
    first = jnp.where(lane < 64, 1.0, 0.0)
    return first.astype(BF16), (1.0 - first).astype(BF16)


def first_head(rows):
    return lax.broadcasted_iota(jnp.int32, (rows, PAIR), 1) < 64


def pack_state(square, total):
    blocks = jnp.where(first_head(64), square[:64], square[64:])
    return blocks, jnp.broadcast_to(total, (8, PAIR))


def unpack_state(packed):
    first = first_head(64)
    square = jnp.concatenate(
        [jnp.where(first, packed[:64], 0.0), jnp.where(first, 0.0, packed[:64])], axis=0
    )
    return square, packed[64:65]


def same_head():
    row = lax.broadcasted_iota(jnp.int32, (PAIR, PAIR), 0)
    lane = lax.broadcasted_iota(jnp.int32, (PAIR, PAIR), 1)
    return (row < 64) == (lane < 64)


class Scan:
    def __init__(self, terms, landed, sums, result, sems, reverse):
        self.terms, self.landed, self.sums, self.result = terms, landed, sums, result
        self.sems, self.reverse = sems, reverse
        self.dp, self.me = lax.axis_index("dp"), lax.axis_index("seq")

    def others(self):
        return [(self.dp, lax.rem(self.me + step, SEQ)) for step in range(1, SEQ)]

    def send_all(self, source, target, sent, came):
        def one(step, carry):
            other = lax.rem(self.me + step, SEQ)
            pltpu.make_async_remote_copy(
                src_ref=source.at[other],
                dst_ref=target.at[self.me],
                send_sem=sent.at[step],
                recv_sem=came.at[step],
                device_id=(self.dp, other),
                device_id_type=MESH,
            ).start()
            return carry

        lax.fori_loop(1, SEQ, one, 0)
        target[self.me] = source[self.me]

    def wait_all(self, source, target, sent, came):
        def one(step, carry):
            other = lax.rem(self.me + (SEQ - step), SEQ)
            pltpu.make_async_remote_copy(
                src_ref=source.at[other],
                dst_ref=target.at[other],
                send_sem=sent.at[step],
                recv_sem=came.at[step],
                device_id=(self.dp, other),
                device_id_type=MESH,
            ).wait_recv()
            return carry

        lax.fori_loop(1, SEQ, one, 0)

    def wait_sent(self, source, target, sent, came):
        def one(step, carry):
            other = lax.rem(self.me + step, SEQ)
            pltpu.make_async_remote_copy(
                src_ref=source.at[other],
                dst_ref=target.at[self.me],
                send_sem=sent.at[step],
                recv_sem=came.at[step],
                device_id=(self.dp, other),
                device_id_type=MESH,
            ).wait_send()
            return carry

        lax.fori_loop(1, SEQ, one, 0)

    def start(self):
        self.send_all(self.terms, self.landed, self.sems[0], self.sems[1])

    def middle(self):
        total = jnp.zeros(self.landed.shape[1:], F32)
        for k in range(SEQ):
            at = SEQ - 1 - k if self.reverse else k
            mine = self.me == at
            ahead = lax.rem(at - self.me + SEQ, SEQ)
            behind = lax.rem(self.me - at + SEQ, SEQ)
            self.sums[at] = total

            @pl.when(mine)
            def _():
                self.result[at] = self.sums[at]

            @pl.when(jnp.logical_not(mine))
            def _():
                pltpu.make_async_remote_copy(
                    src_ref=self.sums.at[at],
                    dst_ref=self.result.at[self.me],
                    send_sem=self.sems[2].at[ahead],
                    recv_sem=self.sems[3].at[ahead],
                    device_id=(self.dp, at),
                    device_id_type=MESH,
                ).start()
                pltpu.make_async_remote_copy(
                    src_ref=self.terms.at[at],
                    dst_ref=self.landed.at[at],
                    send_sem=self.sems[0].at[behind],
                    recv_sem=self.sems[1].at[behind],
                    device_id=(self.dp, at),
                    device_id_type=MESH,
                ).wait_recv()

            total = total + self.landed[at]

    def finish(self):
        self.wait_all(self.sums, self.result, self.sems[2], self.sems[3])

    def drain(self):
        self.wait_sent(self.terms, self.landed, self.sems[0], self.sems[1])
        self.wait_sent(self.sums, self.result, self.sems[2], self.sems[3])


SCAN_SCRATCH = [
    pltpu.VMEM((SEQ, 72, PAIR), F32),
    pltpu.VMEM((SEQ, 72, PAIR), F32),
    pltpu.VMEM((SEQ, 72, PAIR), F32),
    *[pltpu.SemaphoreType.DMA((SEQ,)) for _ in range(4)],
]


def unit_slices(unit, block):
    rows = pl.ds(pl.multiple_of(lax.div(unit, 8) * block, block), block)
    columns = pl.ds(pl.multiple_of(lax.rem(unit, 8) * PAIR, PAIR), PAIR)
    return rows, columns


def for_units(step, together):
    def several(index, carry):
        for offset in range(together):
            step(index * together + offset)
        return carry

    lax.fori_loop(0, SEQ // together, several, 0)


def causal_mask(block, transposed=False):
    row = lax.broadcasted_iota(jnp.int32, (block, block), 0)
    column = lax.broadcasted_iota(jnp.int32, (block, block), 1)
    return (row <= column) if transposed else (row >= column)


def norm_rows(values):
    center = jnp.mean(values, axis=-1, keepdims=True)
    centered = values - center
    variance = jnp.mean(centered * centered, axis=-1, keepdims=True)
    inverse = lax.rsqrt(variance + 1e-05)
    return centered * inverse, inverse


ROWS = 64


def for_rows(count, step):
    def one(index, carry):
        step(pl.ds(pl.multiple_of(index * ROWS, ROWS), ROWS))
        return carry

    lax.fori_loop(0, count // ROWS, one, 0)


def for_columns(count, width, step):
    def one(index, carry):
        step(pl.ds(pl.multiple_of(index * width, width), width))
        return carry

    lax.fori_loop(0, count // width, one, 0)


def attention_forward_kernel(
    block, x, gain, shift, weight, cot_in, cat_out, cot_out, qkv_out, att_out, att_low_out, den_out, state,
    w, cot, normed, qkv, att, att_low, den, cat, fq, fk, stage, land, terms, landed, sums, s0, s1, s2, s3,
    wsem, osem, swap_sent, swap_came,
):
    place = Place()
    rows_all = x.shape[0]
    own, other = pl.ds(0, rows_all), pl.ds(rows_all, rows_all)
    outs = []

    def leave(source, target):
        outs.append(pltpu.make_async_copy(source, target, osem.at[len(outs)]))
        outs[-1].start()

    scan = Scan(terms, landed, sums, state, (s0, s1, s2, s3), False)
    others = [*scan.others(), place.partner()]
    greet(others)
    loads = []
    cot_load = pltpu.make_async_copy(cot_in, cot.at[own], wsem.at[3])
    for slot, third in enumerate((1, 2, 0)):
        load = pltpu.make_async_copy(
            weight.at[:, pl.ds(third * 1024, 1024)], w.at[slot], wsem.at[slot]
        )
        load.start()
        loads.append(load)
    cot_load.start()

    def norm_step(rows):
        scaled, _ = norm_rows(x[rows, :].astype(F32))
        normed[rows, :] = (scaled * gain[...] + shift[...]).astype(BF16)

    for_rows(x.shape[0], norm_step)

    def project(slot, third, feature):
        loads[slot].wait()

        def step(columns):
            raw = dot_nn(normed[...], w[slot, :, columns]).astype(BF16)
            qkv[third, :, columns] = raw
            if feature is not None:
                feature[:, columns] = features(raw.astype(F32))

        for_columns(1024, 512, step)

    project(0, 1, fk)
    project(1, 2, None)

    def local_state(unit):
        rows, columns = unit_slices(unit, block)
        keys = fk[rows, columns]
        square = tn_dot(qkv[2, rows, columns], keys)
        total = jnp.sum(keys.astype(F32), axis=0, keepdims=True)
        blocks, row = pack_state(square, total)
        terms[unit, pl.ds(0, 64)] = blocks
        terms[unit, pl.ds(64, 8)] = row

    for_units(local_state, 4)
    met(len(others))
    scan.start()
    swap = Swap(place, stage, swap_sent, swap_came)
    for core in range(2):
        for block_x in range(4):
            columns = pl.ds(block_x * 256 + core * 128, 128)
            cat[core, own, pl.ds(block_x * 128, 128)] = normed[:, columns]
        swap.put(core, core, cat[core, own, :], land.at[core])
    cot_load.wait()
    for tile in range(2):
        swap.put(2 + tile, 2 + tile, cot[own, pl.ds(tile * TILE, TILE)], land.at[2 + tile])
    leave(qkv.at[pl.ds(1, 2)], qkv_out.at[pl.ds(1, 2)])
    project(2, 0, fq)
    leave(qkv.at[0], qkv_out.at[0])
    first, second = head_masks()
    causal = causal_mask(block)

    def local_part(unit):
        rows, columns = unit_slices(unit, block)
        query, key, value = fq[rows, columns], fk[rows, columns], qkv[2, rows, columns]
        scores = dot_nt(jnp.concatenate([query * first, query * second], axis=0), key)
        both = 0.0
        for head, mask in enumerate((first, second)):
            own = jnp.where(causal, scores[head * block : (head + 1) * block], 0.0).astype(BF16)
            right = jnp.concatenate([value * mask, jnp.broadcast_to(mask, value.shape)], axis=1)
            both = both + dot_nn(own, right)
        att[rows, columns] = both[:, :PAIR]
        den[rows, columns] = both[:, PAIR:]

    for_units(local_part, 2)
    for core in range(2):
        cat[core, other, :] = swap.get(core, land.at[core])
        cot[other, pl.ds(core * TILE, TILE)] = swap.get(2 + core, land.at[2 + core])
    leave(cat, cat_out)
    leave(cot, cot_out)
    scan.middle()
    scan.finish()
    together = same_head()

    def incoming(unit):
        rows, columns = unit_slices(unit, block)
        square, total = unpack_state(state[unit])
        totals = jnp.where(together, jnp.broadcast_to(total, (PAIR, PAIR)), 0.0)
        high, low = split(jnp.concatenate([square, totals], axis=0))
        query = fq[rows, columns]
        both = dot_nt(
            jnp.concatenate([query, query], axis=1), jnp.concatenate([high, low], axis=1)
        )
        denom = den[rows, columns] + both[:, PAIR:]
        den[rows, columns] = denom
        attended = (att[rows, columns] + both[:, :PAIR]) / denom
        att[rows, columns] = attended
        att_low[rows, columns] = attended.astype(BF16)

    for half in range(2):

        def several(index, carry):
            incoming(half * 8 + 2 * index)
            incoming(half * 8 + 2 * index + 1)
            return carry

        lax.fori_loop(0, 4, several, 0)
        part = pl.ds(half * block, block)
        leave(att.at[part], att_out.at[part])
        leave(den.at[part], den_out.at[part])
        leave(att_low.at[part], att_low_out.at[part])
    scan.drain()
    swap.drain(range(4), land.at[0])
    for copy in outs:
        copy.wait()


def attention_forward(x, gain, shift, weight, cot, block):
    rows, width = x.shape
    vmem = pl.BlockSpec(memory_space=pltpu.VMEM)

    def kernel(*refs):
        attention_forward_kernel(block, *refs)

    return pl.pallas_call(
        kernel,
        out_shape=[
            struct((2, 2 * rows, width // 2), BF16),
            struct((2 * rows, width), BF16),
            struct((3, rows, width), BF16),
            struct((rows, width)),
            struct((rows, width), BF16),
            struct((rows, width)),
            struct((SEQ, 72, PAIR)),
        ],
        in_specs=[vmem, vmem, vmem, ANY_SPEC, ANY_SPEC],
        out_specs=[ANY_SPEC] * 6 + [vmem],
        scratch_shapes=[
            pltpu.VMEM((3, width, width), BF16),
            pltpu.VMEM((2 * rows, width), BF16),
            pltpu.VMEM((rows, width), BF16),
            pltpu.VMEM((3, rows, width), BF16),
            pltpu.VMEM((rows, width), F32),
            pltpu.VMEM((rows, width), BF16),
            pltpu.VMEM((rows, width), F32),
            pltpu.VMEM((2, 2 * rows, width // 2), BF16),
            pltpu.VMEM((rows, width), BF16),
            pltpu.VMEM((rows, width), BF16),
            pltpu.VMEM((4, rows, TILE), F32),
            pltpu.VMEM((4, rows, TILE), F32),
            *SCAN_SCRATCH,
            pltpu.SemaphoreType.DMA((4,)),
            pltpu.SemaphoreType.DMA((10,)),
            pltpu.SemaphoreType.DMA((4,)),
            pltpu.SemaphoreType.DMA((4,)),
        ],
        compiler_params=pltpu.CompilerParams(
            collective_id=5, has_side_effects=True, vmem_limit_bytes=62 * MIB
        ),
    )(x, gain.reshape(1, width), shift.reshape(1, width), weight, cot)


def gelu_both(pre):
    cumulative = 0.5 * (1.0 + lax.erf(pre * (1.0 / math.sqrt(2.0))))
    density = jnp.exp(-0.5 * pre * pre) * (1.0 / math.sqrt(2.0 * math.pi))
    return (pre * cumulative).astype(BF16), (cumulative + pre * density).astype(BF16)


def norm_back(grad, gain, scaled, inverse):
    spread = grad * gain
    first_mean = jnp.mean(spread, axis=-1, keepdims=True)
    second_mean = jnp.mean(spread * scaled, axis=-1, keepdims=True)
    return inverse * (spread - first_mean - scaled * second_mean)


def norm_back_rows(values, grad, base, gain, sums, store):
    sums[...] = jnp.zeros_like(sums)

    def step(rows):
        scaled, inverse = norm_rows(values[rows, :].astype(F32))
        part = grad[rows, :]
        sums[0:1, :] += jnp.sum(part * scaled, axis=0, keepdims=True)
        sums[1:2, :] += jnp.sum(part, axis=0, keepdims=True)
        store(rows, base[rows, :].astype(F32) + norm_back(part, gain[...], scaled, inverse))

    for_rows(grad.shape[0], step)


def feed_forward_kernel(
    x, att_low, gain, shift, cot_in, w_out, w_up, w_down,
    output_out, gmixed_out, gatt_out, sums, norm_out, pre_out, out_out, down_a, down_b, down_c,
    wo, wu, wd, wsem, osem, output, gmixed, gatt, norm_cat, pre_cat, hidden, slope, cot_cat,
    stage, land, land_att, land_norm, swap_sent, swap_came, free, *scratch,
):
    take_scratch = Taker(scratch)
    slabs = take_scratch(slab_shapes(DOWN_WIDTHS))
    slab_a, slab_b, slab_c = slabs
    phases = take_scratch([stream_scratch(length, (0,)) for length in DOWN_WIDTHS])
    place = Place()
    core = place.core
    rows = x.shape[0]
    others = link_neighbours(place)
    greet(others)
    own, other = pl.ds(0, rows), pl.ds(rows, rows)
    mixed = gatt
    loads = []
    moves = ((w_out, wo), (w_up, wu), (w_down, wd), (cot_in, cot_cat))
    for slot in (0, 1, 3, 2):
        loads.append(pltpu.make_async_copy(*moves[slot], wsem.at[slot]))
        loads[-1].start()
    outs = []

    def leave(source, target):
        outs.append(pltpu.make_async_copy(source, target, osem.at[len(outs)]))
        outs[-1].start()

    cot = cot_cat.at[own]
    swap = Swap(place, stage, swap_sent, swap_came)
    loads[0].wait()

    def mix(columns):
        mixed[:, columns] = x[:, columns].astype(F32) + dot_nn(att_low[...], wo[:, columns])

    for_columns(1024, TILE, mix)

    def norm_step(index):
        scaled, _ = norm_rows(mixed[index, :])
        norm_cat[index, :] = (scaled * gain[...] + shift[...]).astype(BF16)

    for_rows(rows, norm_step)
    met(len(others))
    loads[1].wait()

    def up(columns):
        ours, ours_slope = gelu_both(dot_nn(norm_cat[own, :], wu[:, columns]))
        hidden[:, columns] = ours
        slope[:, columns] = ours_slope
        return ours

    def give(block, carry):
        theirs = up(half_columns(block, 1 - core, 1024))
        swap.put(block, block, theirs, land.at[block])
        return carry

    lax.fori_loop(0, 4, give, 0)
    loads[2].wait()

    def take(block, carry):
        ours = up(half_columns(block, core, 1024))
        both = jnp.concatenate([ours, swap.get(block, land.at[block])], axis=0)
        for half in range(2):
            columns = pl.ds(half * TILE, TILE)
            product = tn_dot(both, cot_cat[:, columns]).reshape(4, 4, 4, 8, TILE)
            for stream in range(3):
                slabs[stream][block, :, :, :, columns] = product[:, :, stream]
            last = product[:, :, 3]
            if half == 0:
                slab_a[block, :, :, :, pl.ds(1024, 384)] = last[..., :384]
                slab_b[block, :, :, :, pl.ds(1024, 128)] = last[..., 384:]
            else:
                slab_b[block, :, :, :, pl.ds(1152, 256)] = last[..., :256]
                slab_c[block, :, :, :, pl.ds(1024, 256)] = last[..., 256:]
        return carry

    lax.fori_loop(0, 4, take, 0)
    pl.semaphore_signal(free, inc=1, device_id=place.partner(), device_id_type=MESH)
    down = [Stream(place, slabs[k], ORDERS[k], phases[k]) for k in range(3)]
    for stream in down:
        stream.prepare().begin_far()
    for stream in down:
        stream.phase.begin_near()
    for tile in range(2):
        columns = pl.ds(tile * TILE, TILE)
        swap.put(4 + tile, tile, norm_cat[own, columns], land_norm.at[tile], before=tile)
    loads[3].wait()

    def finish_forward(columns):
        output[:, columns] = (mixed[:, columns] + dot_nn(hidden[...], wd[:, columns])).astype(BF16)

    for_columns(1024, 256, finish_forward)
    leave(output, output_out)

    def back(columns):
        grad = dot_nt(cot[...], wd[columns, :]) * slope[:, columns].astype(F32)
        low = grad.astype(BF16)
        hidden[:, columns] = low
        return low

    pl.semaphore_wait(free, 1)

    def give_back(block, carry):
        theirs = back(half_columns(block, 1 - core, 1024))
        before = jnp.where(block < 2, 4 + block, block)
        swap.put(6 + block, block, theirs, land.at[block], before=before)
        return carry

    lax.fori_loop(0, 4, give_back, 0)

    def take_back(block, carry):
        columns = pl.ds(pl.multiple_of(block * TILE, TILE), TILE)
        pre_cat[own, columns] = back(half_columns(block, core, 1024))
        pre_cat[other, columns] = swap.get(6 + block, land.at[block])
        return carry

    lax.fori_loop(0, 4, take_back, 0)
    leave(pre_cat, pre_out)
    for tile in range(2):
        columns = pl.ds(tile * TILE, TILE)
        norm_cat[other, columns] = swap.get(4 + tile, land_norm.at[tile])
        swap.put(10 + tile, tile, att_low[:, columns], land_att.at[tile], before=6 + tile)
    leave(norm_cat, norm_out)
    pl.semaphore_signal(free, inc=1, device_id=place.partner(), device_id_type=MESH)
    for stream in down:
        stream.forward()

    def back_up(columns):
        gmixed[:, columns] = dot_nt(hidden[...], wu[columns, :])

    for_columns(1024, 256, back_up)

    def store(index, values):
        gmixed[index, :] = values
        hidden[index, pl.ds(0, 1024)] = values.astype(BF16)

    norm_back_rows(mixed, gmixed, cot, gain, sums, store)
    leave(gmixed, gmixed_out)
    pl.semaphore_wait(free, 1)
    swap.put(12, 2, hidden[:, half_tile(0, 1 - core)], land_norm.at[0], before=8)

    def back_out(columns):
        gatt[:, columns] = dot_nt(hidden[:, pl.ds(0, 1024)], wo[columns, :])

    for_columns(1024, TILE, back_out)
    leave(gatt, gatt_out)
    ours = hidden[:, half_tile(0, core)]
    theirs = swap.get(12, land_norm.at[0])
    for tile in range(2):
        swap.copy(10 + tile, tile, land_att.at[tile]).wait_recv()
        for part, (start, width) in enumerate(((0, 384), (384, 128))):
            product = tn_dot(att_low[:, pl.ds(tile * TILE + start, width)], ours)
            theirs_att = land_att[tile, :, pl.ds(start, width)].astype(BF16)
            land[2 * tile + part, pl.ds(0, width), :] = product + tn_dot(theirs_att, theirs)
            leave(land.at[2 * tile + part, pl.ds(0, width)], out_out.at[pl.ds(tile * TILE + start, width)])
    for stream, out in zip(down, (down_a, down_b, down_c)):
        stream.finish(out)
    for number, slot in ((9, 3), (10, 0), (11, 1), (12, 2)):
        swap.copy(number, slot, land_norm.at[0]).wait_send()
    for stream in down:
        stream.drain()
    for copy in outs:
        copy.wait()


def slab_shapes(widths):
    return [pltpu.VMEM((4, 4, 4, 8, width), F32) for width in widths]


def struct(shape, dtype=F32):
    return jax.ShapeDtypeStruct(shape, dtype)


VMEM_SPEC = pl.BlockSpec(memory_space=pltpu.VMEM)
ANY_SPEC = pl.BlockSpec(memory_space=pl.ANY)


def call(kernel, outs, out_specs, operands, in_specs, scratch, collective_id):
    return pl.pallas_call(
        kernel,
        out_shape=outs,
        in_specs=in_specs,
        out_specs=out_specs,
        scratch_shapes=scratch,
        compiler_params=pltpu.CompilerParams(
            collective_id=collective_id, has_side_effects=True, vmem_limit_bytes=63 * MIB
        ),
    )(*operands)


def feed_forward(x, att_low, gain, shift, cot_cat, w_out, w_up, w_down):
    rows, width = x.shape
    wide = w_up.shape[1]
    outs = [
        struct((rows, width), BF16),
        struct((rows, width)),
        struct((rows, width)),
        struct((8, width)),
        struct((2 * rows, width), BF16),
        struct((2 * rows, wide // 2), BF16),
        struct((width, TILE)),
        *[struct((4, 4, 8, length)) for length in DOWN_WIDTHS],
    ]
    scratch = [
        pltpu.VMEM((width, width), BF16),
        pltpu.VMEM((width, wide), BF16),
        pltpu.VMEM((wide, width), BF16),
        pltpu.SemaphoreType.DMA((4,)),
        pltpu.SemaphoreType.DMA((9,)),
        pltpu.VMEM((rows, width), BF16),
        pltpu.VMEM((rows, width), F32),
        pltpu.VMEM((rows, width), F32),
        pltpu.VMEM((2 * rows, width), BF16),
        pltpu.VMEM((2 * rows, wide // 2), BF16),
        pltpu.VMEM((rows, wide), BF16),
        pltpu.VMEM((rows, wide), BF16),
        pltpu.VMEM((2 * rows, width), BF16),
        pltpu.VMEM((4, rows, TILE), F32),
        pltpu.VMEM((4, rows, TILE), F32),
        pltpu.VMEM((2, rows, TILE), F32),
        pltpu.VMEM((2, rows, TILE), F32),
        pltpu.SemaphoreType.DMA((13,)),
        pltpu.SemaphoreType.DMA((13,)),
        pltpu.SemaphoreType.REGULAR,
        *slab_shapes(DOWN_WIDTHS),
        *flatten([stream_scratch(length, (0,)) for length in DOWN_WIDTHS]),
    ]
    specs = [VMEM_SPEC] * 4 + [ANY_SPEC] * 4
    out_specs = [ANY_SPEC] * 3 + [VMEM_SPEC] + [ANY_SPEC] * 3 + [VMEM_SPEC] * 3
    operands = (x, att_low, gain, shift, cot_cat, w_out, w_up, w_down)
    return call(feed_forward_kernel, outs, out_specs, operands, specs, scratch, 1)


def last_scratch(rows, width):
    return {
        "qkv": pltpu.VMEM((3, rows, width), BF16),
        "att": pltpu.VMEM((rows, width), F32),
        "gn": pltpu.VMEM((rows, width), F32),
        "state": pltpu.VMEM((SEQ, 72, PAIR), F32),
        "x": pltpu.VMEM((rows, width), BF16),
        "grads": pltpu.VMEM((2, rows, width), F32),
        "scan": list(SCAN_SCRATCH[:3]) + [SCAN_SCRATCH[0]] + list(SCAN_SCRATCH[3:]),
        "norm_cat": pltpu.VMEM((2, 2 * rows, width // 2), BF16),
        "pre_cat": pltpu.VMEM((2 * rows, 2 * width), BF16),
        "w": pltpu.VMEM((width, 3 * width), BF16),
        "stage": pltpu.VMEM((3, rows, TILE), F32),
        "land": pltpu.VMEM((3, rows, TILE), F32),
        "swap": [pltpu.SemaphoreType.DMA((3,)), pltpu.SemaphoreType.DMA((3,))],
        "slabs": slab_shapes(UP_WIDTHS),
        "chunks": [pltpu.VMEM((4, 4, 8, length), F32) for length in DOWN_WIDTHS],
        "up_chunks": [pltpu.VMEM((4, 4, 8, length), F32) for length in UP_WIDTHS],
        "out_slabs": slab_shapes(OUT_WIDTHS),
        "vec_slab": pltpu.VMEM((4, 4, 4, 8, 128), F32),
        "sums": pltpu.VMEM((8, width), F32),
        "down": [stream_scratch(length, (1, 2), (2,)) for length in DOWN_WIDTHS],
        "up": [stream_scratch(length, (0, 1, 2), (2,)) for length in UP_WIDTHS],
        "out": [stream_scratch(length, (0, 1, 2), (1, 2)) for length in OUT_WIDTHS],
        "qkv_sems": [[pltpu.SemaphoreType.DMA((6,))] * 2 for _ in QKV_WIDTHS],
        "qkv_sum": [stream_scratch(length, (1, 2), (2,)) for length in QKV_WIDTHS],
        "vec": stream_scratch(128, (0, 1, 2), (0, 1, 2)),
        "up_rows": [pltpu.VMEM((2, 8, 2048), F32), pltpu.VMEM((8, 2048), F32)],
        "out_rows": [pltpu.VMEM((2, 8, 512), F32), pltpu.VMEM((8, 512), F32)],
        "qkv_rows": [pltpu.VMEM((2, 8, 1536), F32), pltpu.VMEM((8, 1536), F32)],
        "row_sems": pltpu.SemaphoreType.DMA((3, 2)),
        "vec_land": pltpu.VMEM((8, 128), F32),
        "vec_sems": pltpu.SemaphoreType.DMA((2,)),
        "credit": pltpu.SemaphoreType.REGULAR((3,)),
        "loads": pltpu.SemaphoreType.DMA((32,)),
    }


def last_kernel(
    block, qkv_in, att_in, den_in, state_in, gatt_in, gmixed_in, norm_one_in, norm_in, pre_in,
    down_in_a, down_in_b, down_in_c, out_in, x_in, weight, gain, sums_two,
    grad_input, grad_up, grad_out, grad_qkv, grad_down, grad_gains, *scratch,
):
    place = Place()
    core = place.core
    rows, width = att_in.shape
    like = last_scratch(rows, width)
    take = Taker(scratch)
    s = {name: take(like[name]) for name in like}
    qkv, att, gn, grads = s["qkv"], s["att"], s["gn"], s["grads"]
    slabs = s["slabs"]
    scan = Scan(*s["scan"][:4], s["scan"][4:], True)
    across = [place.neighbour(0, step) for step in (1, -1, 2)]
    others = [*across, place.partner(), *scan.others()]
    greet(others)
    loads = []

    def load(source, target):
        copy = pltpu.make_async_copy(source, target, s["loads"].at[len(loads)])
        copy.start()
        loads.append(copy)
        return copy

    down_in = (down_in_a, down_in_b, down_in_c)
    down_loads = [load(source, target) for source, target in zip(down_in, s["chunks"])]
    started = [
        load(qkv_in.at[0], qkv.at[0]),
        load(gatt_in, gn),
        load(den_in, grads.at[0]),
        load(att_in, att),
    ]
    up_loads = [load(pre_in, s["pre_cat"])]
    for which in range(2):
        for block_x in range(4):
            source = norm_in.at[:, pl.ds(block_x * 256 + which * 128, 128)]
            target = s["norm_cat"].at[which, :, pl.ds(block_x * 128, 128)]
            up_loads.append(load(source, target))
    qkv_loads = [load(qkv_in.at[pl.ds(1, 2)], qkv.at[pl.ds(1, 2)]), load(state_in, s["state"])]
    out_loads = []
    for k in range(3):
        for which, start, length, at in stream_pieces(k, OUT_WIDTHS, TILE):
            source = out_in.at[:, which, :, :, :, pl.ds(start, length)]
            target = s["out_slabs"][k].at[:, :, :, :, pl.ds(at, length)]
            out_loads.append(load(source, target))
    late_loads = [load(weight, s["w"]), load(x_in, s["x"])]

    def settle(copies):
        for copy in copies:
            copy.wait()

    first, second = head_masks()
    first_wide = first_head(block)

    def slopes(index, columns, numer):
        product = numer * att[index, columns]
        ours = jnp.sum(jnp.where(first_wide, product, 0.0), axis=1, keepdims=True)
        theirs = jnp.sum(jnp.where(first_wide, 0.0, product), axis=1, keepdims=True)
        return -ours, -theirs

    up_first = [phases[0] for phases in s["up"]]
    down = [Stream(place, s["chunks"][k], ORDERS[k][1:], s["down"][k]) for k in range(3)]
    up = [Stream(place, slabs[k], ORDERS[k], s["up"][k]) for k in range(3)]
    out = [Stream(place, s["out_slabs"][k], ORDERS[k], s["out"][k]) for k in range(3)]
    qkv_sum = [None] * 3
    vec = [Stream(place, s["vec_slab"], ORDERS[0], s["vec"])]
    begin, forward, proceed, finish = Stream.begin, Stream.forward, Stream.proceed, Stream.finish

    def go(*steps):
        for step, streams, k in steps:
            step(streams[k])

    settle(down_loads)
    met(len(others))
    for stream in down:
        stream.begin()
    settle(started)

    def local_state(unit):
        index, columns = unit_slices(unit, block)
        numer = gn[index, columns] / grads[0, index, columns]
        gn[index, columns] = numer
        one, two = slopes(index, columns, numer)
        query = features(qkv[0, index, columns].astype(F32))
        high, low = split(numer)
        wide = tn_dot(query, jnp.concatenate([high, low], axis=1))
        spread = jnp.where(first_wide, one, two)
        total = jnp.sum(query.astype(F32) * spread, axis=0, keepdims=True)
        blocks, row = pack_state(wide[:, :PAIR] + wide[:, PAIR:], total)
        scan.terms[unit, pl.ds(0, 64)] = blocks
        scan.terms[unit, pl.ds(64, 8)] = row

    for_units(local_state, 2)
    scan.start()
    go((forward, down, 0), (forward, down, 1), (forward, down, 2))
    settle(up_loads)
    for k in range(3):
        stream_product(k, s["norm_cat"], s["pre_cat"], slabs[k], UP_WIDTHS, 2048)
        if k == 0:
            up[0].begin()
    norm_load = load(norm_one_in, s["norm_cat"])
    go((proceed, down, 2))
    settle(qkv_loads)
    causal = causal_mask(block)
    causal_t = causal_mask(block, True)

    def local_part(unit):
        index, columns = unit_slices(unit, block)
        raw_query = qkv[0, index, columns].astype(F32)
        query, value = features(raw_query), qkv[2, index, columns]
        key = features(qkv[1, index, columns].astype(F32))
        numer = gn[index, columns]
        one, two = slopes(index, columns, numer)
        high, low = split(numer)
        scores = dot_nt(jnp.concatenate([key * first, key * second], axis=0), query)
        wide = jnp.concatenate([high, low], axis=1)
        values = jnp.concatenate([value, value], axis=1)
        grad_query, grad_key, grad_value = 0.0, 0.0, 0.0
        for head, (mask, slope) in enumerate(((first, one), (second, two))):
            mask_wide = jnp.concatenate([mask, mask], axis=1)
            mixing = jnp.where(causal, dot_nt(wide * mask_wide, values) + slope, 0.0).astype(BF16)
            turned = jnp.where(causal_t, scores[head * block : (head + 1) * block], 0.0)
            grad_query = grad_query + dot_nn(mixing, key * mask)
            grad_key = grad_key + tn_dot(mixing, query * mask)
            grad_value = grad_value + dot_nn(turned.astype(BF16), high * mask)
        square, total = unpack_state(s["state"][unit])
        state_high, state_low = split(square)
        grad_query = grad_query + dot_nn(wide, jnp.concatenate([state_high, state_high], axis=0))
        grad_query = grad_query + dot_nn(high, state_low)
        grad_query = grad_query + jnp.where(first_wide, one, two) * total
        qkv[0, index, columns] = (grad_query * feature_slope(raw_query)).astype(BF16)
        grads[0, index, columns] = grad_key
        grads[1, index, columns] = grad_value

    def local_parts(start, count):
        def one(index, carry):
            local_part(start + index)
            return carry

        lax.fori_loop(0, count, one, 0)

    local_parts(0, 4)
    scan.middle()
    up[1].begin()
    up[2].begin()
    go((proceed, down, 0), (proceed, down, 1))
    local_parts(4, 4)
    go((finish, down, 2))
    local_parts(8, 1)
    go((forward, up, 0))
    local_parts(9, 7)
    settle(out_loads)
    swap = Swap(place, s["stage"], *s["swap"])
    land, cat = s["land"], s["pre_cat"]
    own, other = pl.ds(0, rows), pl.ds(rows, rows)
    swap.put(0, 0, qkv[0, :, half_tile(0, 1 - core)], land.at[0])
    mixed_load = load(gmixed_in, att)
    scan.finish()

    def incoming(unit):
        index, columns = unit_slices(unit, block)
        square, total = unpack_state(scan.result[unit])
        high, low = split(square)
        raw_key = qkv[1, index, columns].astype(F32)
        key, value = features(raw_key), qkv[2, index, columns]
        grad_key = grads[0, index, columns] + total
        grad_key = grad_key + dot_nt(
            jnp.concatenate([value, value], axis=1), jnp.concatenate([high, low], axis=1)
        )
        grad_value = grads[1, index, columns] + dot_nn(
            jnp.concatenate([key, key], axis=1), jnp.concatenate([high, low], axis=0)
        )
        qkv[1, index, columns] = (grad_key * feature_slope(raw_key)).astype(BF16)
        qkv[2, index, columns] = grad_value.astype(BF16)

    for_units(incoming, 2)
    for third in (1, 2):
        swap.put(third, third, qkv[third, :, half_tile(0, 1 - core)], land.at[third])
    go((forward, up, 2))
    settle(late_loads)

    def back_norm(columns):
        total = 0.0
        for third in range(3):
            total = total + dot_nt(qkv[third], s["w"][columns, pl.ds(third * 1024, 1024)])
        gn[:, columns] = total

    for start in (0, 256, 512, 768):
        back_norm(pl.ds(start, 256))
        if start == 0:
            go((forward, up, 1), (finish, down, 1))
    for third in range(3):
        columns = pl.ds(third * TILE, TILE)
        cat[own, columns] = qkv[third, :, half_tile(0, core)]
        cat[other, columns] = swap.get(third, land.at[third])
    norm_load.wait()
    mixed_load.wait()
    def turn(k):
        up[k].finish(s["up_chunks"][k])
        up[k].drain()
        for step in (1, -1):
            pl.semaphore_signal(
                s["credit"].at[k],
                inc=1,
                device_id=place.neighbour(ORDERS[k][0], step),
                device_id_type=MESH,
            )
        narrow = (slice(None),) * 4 + (pl.ds(0, QKV_WIDTHS[k]),)
        data = slabs[k].at[narrow]
        stream_product(k, s["norm_cat"], cat, data, QKV_WIDTHS, 3 * TILE)
        pl.semaphore_wait(s["credit"].at[k], 2)
        phases = [[up_first[k][0].at[narrow], up_first[k][1].at[narrow], *s["qkv_sems"][k]]]
        qkv_sum[k] = Stream(place, data, ORDERS[k], phases + s["qkv_sum"][k])
        qkv_sum[k].begin()

    def store(index, values):
        gn[index, :] = values

    sums = s["sums"]
    norm_back_rows(s["x"], gn, att, gain, sums, store)
    leave = load(gn, grad_input)
    four = jnp.concatenate([sums[0:2, :], sums_two[0:2, :]], axis=0)
    eight = jnp.concatenate([four, four], axis=0)
    turned = jnp.transpose(jnp.concatenate([eight, jnp.zeros((120, 1024), F32)], axis=0))
    turned = turned.reshape(4, 2, 4, 4, 8, 128)
    lane = lax.broadcasted_iota(jnp.int32, (8, 128), 1)
    s["vec_slab"][...] = jnp.where(lane < 4, turned[:, 0], jnp.where(lane < 8, turned[:, 1], 0.0))
    for stream in out:
        stream.begin()
    turn(0)
    go((forward, out, 0), (finish, down, 0))
    turn(1)
    go((forward, out, 1), (forward, out, 2))
    turn(2)
    go(
        (forward, qkv_sum, 0), (proceed, out, 2), (begin, vec, 0), (forward, qkv_sum, 1), (forward, qkv_sum, 2),
        (begin, up, 0), (begin, up, 1), (begin, up, 2), (proceed, out, 0), (proceed, out, 1), (proceed, qkv_sum, 1),
        (proceed, qkv_sum, 0), (forward, up, 0), (proceed, out, 2), (proceed, qkv_sum, 2), (proceed, vec, 0),
        (forward, up, 1), (proceed, out, 0), (forward, up, 2), (forward, qkv_sum, 0), (proceed, out, 1),
        (forward, qkv_sum, 2), (forward, qkv_sum, 1), (proceed, up, 0), (proceed, up, 2), (finish, out, 2),
        (proceed, up, 1), (proceed, vec, 0), (proceed, qkv_sum, 0), (proceed, qkv_sum, 2), (proceed, qkv_sum, 1),
        (finish, out, 1), (finish, out, 0), (finish, up, 0), (finish, up, 2), (finish, up, 1), (finish, vec, 0),
    )
    for k in range(3):
        piece = down[k].data
        grad_down[pl.ds(8 * k, 8), :] = piece[:, pl.ds(0, 1024)]
        start, width_k = DOWN_CUTS[k]
        grad_down[pl.ds(24, 8), pl.ds(start, width_k)] = piece[:, pl.ds(1024, width_k)]
    swaps = []

    def swap_rows(streams, widths, columns, rows_land, slot):
        shared_rows(streams, widths, columns, rows_land[0])
        copy = row_swap(place, *rows_land, s["row_sems"].at[slot])
        copy.start()
        swaps.append(copy)

    swap_rows(up, UP_WIDTHS, 2048, s["up_rows"], 0)
    vec_tile = vec[0].data
    vec_copy = pltpu.make_async_remote_copy(
        src_ref=vec_tile,
        dst_ref=s["vec_land"],
        send_sem=s["vec_sems"].at[0],
        recv_sem=s["vec_sems"].at[1],
        device_id=place.partner(),
        device_id_type=MESH,
    )
    vec_copy.start()
    swap_rows(out, OUT_WIDTHS, TILE, s["out_rows"], 1)
    go((finish, qkv_sum, 2), (finish, qkv_sum, 0), (finish, qkv_sum, 1))
    swap_rows(qkv_sum, QKV_WIDTHS, 3 * TILE, s["qkv_rows"], 2)
    scan.drain()
    for number in range(3):
        swap.copy(number, number, land.at[number]).wait_send()
    for stream in (*down, *up, *out, *qkv_sum, *vec):
        stream.drain()
    vec_copy.wait()
    grad_gains[...] = vec_tile[...] + s["vec_land"][...]
    leave.wait()
    swaps[0].wait()
    lay_rows(place, *s["up_rows"], grad_up)
    swaps[1].wait()
    lay_rows(place, *s["out_rows"], grad_out)
    swaps[2].wait()
    lay_rows(place, *s["qkv_rows"], grad_qkv)


def last_part(qkv, att, den, state, gatt, gmixed, norm_one, norm_cat, pre_cat, down, out, x, weight, gain, sums_two, block):
    rows, width = x.shape

    def kernel(*refs):
        last_kernel(block, *refs)

    outs = [
        struct((rows, width)),
        struct((8, 4096)),
        struct((8, width)),
        struct((8, 3 * width)),
        struct((32, width)),
        struct((8, 128)),
    ]
    like = last_scratch(rows, width)
    scratch = [leaf for name in like for leaf in flatten(like[name])]
    out = out.reshape(4, 2, 4, 4, 8, TILE)
    operands = (
        qkv, att, den, state, gatt, gmixed, norm_one, norm_cat, pre_cat, *down, out, x, weight, gain, sums_two,
    )
    specs = [ANY_SPEC] * 15 + [VMEM_SPEC] * 2
    out_specs = [ANY_SPEC] + [VMEM_SPEC] * 5
    return call(kernel, outs, out_specs, operands, specs, scratch, 2)


def lay_out_kernel(output, grad_input, up, out, qkv, down, gains, output_to, grad_to, up_to, out_to, qkv_to, down_to, a, b, c, d):
    pairs = (
        (output, output_to), (grad_input, grad_to), (up, up_to), (out, out_to), (qkv, qkv_to), (down, down_to),
    )
    for source, target in pairs:
        target[...] = source[...]
    core = lax.rem(lax.axis_index("dp"), 2)
    turned = jnp.transpose(jnp.concatenate([gains[...], jnp.zeros((120, 128), F32)], axis=0))
    for k, target in enumerate((a, b, c, d)):
        target[...] = jnp.where(core == 0, turned[k : k + 1, :8], turned[4 + k : 5 + k, :8])


def lay_out(output, *grads):
    arrays = (output, *grads[:-1])
    outs = [struct(array.shape, array.dtype) for array in arrays] + [struct((1, 8))] * 4
    return pl.pallas_call(
        lay_out_kernel,
        out_shape=outs,
        in_specs=[VMEM_SPEC] * 7,
        out_specs=[VMEM_SPEC] * 10,
        compiler_params=pltpu.CompilerParams(vmem_limit_bytes=62 * MIB),
    )(output, *grads)


def body(
    inputs,
    first_gain,
    first_shift,
    qkv_weight,
    out_weight,
    second_gain,
    second_shift,
    up_weight,
    down_weight,
    cotangent,
):
    sequences, block, width = inputs.shape
    rows = sequences * block
    x = inputs.reshape(rows, width)
    cot = cotangent.reshape(rows, width)
    gain_one, gain_two = first_gain.reshape(1, width), second_gain.reshape(1, width)
    shift_two = second_shift.reshape(1, width)
    norm_one, cot_cat, qkv, att, att_low, den, state = attention_forward(
        x, first_gain, first_shift, qkv_weight, cot, block
    )
    output, gmixed, gatt, sums_two, norm_cat, pre_cat, out, *down = feed_forward(
        x, att_low, gain_two, shift_two, cot_cat, out_weight, up_weight, down_weight
    )
    grads = last_part(
        qkv, att, den, state, gatt, gmixed, norm_one, norm_cat, pre_cat, down, out, x, qkv_weight,
        gain_one, sums_two, block,
    )
    output, grad_input, grad_up, grad_out, grad_qkv, grad_down, *gains = lay_out(output, *grads)
    return (
        output.reshape(inputs.shape),
        grad_input.reshape(inputs.shape),
        grad_qkv,
        grad_out,
        grad_up,
        grad_down,
        *[gain.reshape(8) for gain in gains],
    )


def solution(mesh):
    return jax.shard_map(
        body,
        mesh=mesh,
        in_specs=(
            P("dp", "seq", None),
            P(),
            P(),
            P(),
            P(),
            P(),
            P(),
            P(),
            P(),
            P("dp", "seq", None),
        ),
        out_specs=(
            P("dp", "seq", None),
            P("dp", "seq", None),
            P(("dp", "seq"), None),
            P(("dp", "seq"), None),
            P(("dp", "seq"), None),
            P(("dp", "seq"), None),
            P(("dp", "seq")),
            P(("dp", "seq")),
            P(("dp", "seq")),
            P(("dp", "seq")),
        ),
        check_vma=False,
    )
```

time: 232 us -> 177 us (0.76)
  Pallas kernels: 224 us -> 175 us
  local copies, waits for them, and re-layouts: 6.22 us -> 0 us
    pallas_call x4, Pallas kernels: 224 us -> 175 us  [the longest x2 140 us: call(): pl.pallas_call(kernel, out_shape=outs, in_specs=in_specs, out_specs=out_s...]
    unnamed x18 -> x0, local copies, waits for them, and re-layouts: 4.61 us -> none
where the time goes in v4:
time: 177 us; the launch traced here: 176 us
  Pallas kernels  175 us (99%)
    pallas_call x2, Pallas kernels, call(): pl.pallas_call(kernel, out_shape=outs, in_specs=in_specs, out_specs=out_s...  140 us
    pallas_call x1, Pallas kernels, attention_forward(): pl.pallas_call(kernel, out_shape=[struct((2, 2 * rows, width // 2), BF16)...  31.3 us

profile of v4, /device:TPU:0, one launch (start us, length us, event | category | flops | bytes accessed | tf_op | source)
XLA Modules:
  0.0 175.6 jit_solution(3662388046253842112)
XLA Ops:
  0.6 31.3 %shard_map.177 = (bf16[2,768,512]{2,1,0:T(8,128)(2,1)}, bf16[768,1024]{1,0:T(8,128)(2,1)}, bf16[3,384,1024]{2,1,0:T(8,128)(2,1)}, f32[384,1024]{1,0:T(8,128)}, b...) custom-call(bf16[384,1024]{1,0:T(8,128)(2,1)} %bitcast.13, f32[1,1024]{1,0:T(1,128)} %bitcast.18, ...), custom_call_target="tpu_custom_call" | custom-call | tf_op jit(solution)/shard_map/pallas_call | solution.py:741
  31.9 44.5 %shard_map.178 = (bf16[384,1024]{1,0:T(8,128)(2,1)}, f32[384,1024]{1,0:T(8,128)}, f32[384,1024]{1,0:T(8,128)}, f32[8,1024]{1,0:T(8,128)}, bf16[768,1024]{1,0:T(8...) custom-call(bf16[384,1024]{1,0:T(8,128)(2,1)} %bitcast.14, ...), custom_call_target="tpu_custom_call" | custom-call | tf_op jit(solution)/shard_map/pallas_call | solution.py:983
  76.4 95.6 %shard_map.179 = (f32[384,1024]{1,0:T(8,128)}, f32[8,4096]{1,0:T(8,128)}, f32[8,1024]{1,0:T(8,128)}, f32[8,3072]{1,0:T(8,128)}, f32[32,1024]{1,0:T(8,128)}, /*index=5*/f32[8,128]{1,0:T(8,128)}) custom-call(bf16[3,384,1024]{2,1,0:T(8,128)(2,1)} %get-tuple-element.46.refs_0_, f32[384,1024]{1,0:T(8,128)} %get-tuple-element.47.refs_1_, ...), custom_call_target="tpu_custom_call" | custom-call | tf_op jit(solution)/shard_map/pallas_call | solution.py:983
  172.1 3.4 %shard_map.180 = (bf16[384,1024]{1,0:T(8,128)(2,1)}, f32[384,1024]{1,0:T(8,128)}, f32[8,4096]{1,0:T(8,128)}, f32[8,1024]{1,0:T(8,128)}, f32[8,3072]{1,0:T(8,128)...) custom-call(bf16[384,1024]{1,0:T(8,128)(2,1)} %get-tuple-element.45.output, ...), custom_call_target="tpu_custom_call" | custom-call | tf_op jit(solution)/shard_map/pallas_call | solution.py:1403

commit v5 on v4

--- a/solution.py
+++ b/solution.py
@@ -446,104 +446,106 @@
     return (row < 64) == (lane < 64)
 
 
+def head_slopes(numer, attended, first_wide):
+    product = numer * attended
+    ours = jnp.sum(jnp.where(first_wide, product, 0.0), axis=1, keepdims=True)
+    theirs = jnp.sum(jnp.where(first_wide, 0.0, product), axis=1, keepdims=True)
+    return -ours, -theirs
+
+
+def state_gradient(query, numer, attended, first_wide):
+    one, two = head_slopes(numer, attended, first_wide)
+    high, low = split(numer)
+    wide = tn_dot(query, jnp.concatenate([high, low], axis=1))
+    spread = jnp.where(first_wide, one, two)
+    total = jnp.sum(query.astype(F32) * spread, axis=0, keepdims=True)
+    return pack_state(wide[:, :PAIR] + wide[:, PAIR:], total)
+
+
+OFFSETS = sorted(
+    ((y, z) for y in range(RING) for z in range(RING) if y or z),
+    key=lambda offset: -sum(min(step, RING - step) for step in offset),
+)
+
+
 class Scan:
     def __init__(self, terms, landed, sums, result, sems, reverse):
         self.terms, self.landed, self.sums, self.result = terms, landed, sums, result
         self.sems, self.reverse = sems, reverse
         self.dp, self.me = lax.axis_index("dp"), lax.axis_index("seq")
+        self.y, self.z = lax.div(self.me, RING), lax.rem(self.me, RING)
+        self.parity = lax.rem(self.y + self.z, 2)
+        self.unit = self.unit_of(self.parity, self.me)
+
+    def unit_of(self, parity, device):
+        return parity * 8 + lax.div(device, 2)
+
+    def at(self, y, z, sign=1):
+        y = lax.rem(self.y + (sign * y + RING), RING)
+        z = lax.rem(self.z + (sign * z + RING), RING)
+        return y * RING + z
 
     def others(self):
-        return [(self.dp, lax.rem(self.me + step, SEQ)) for step in range(1, SEQ)]
-
-    def send_all(self, source, target, sent, came):
-        def one(step, carry):
-            other = lax.rem(self.me + step, SEQ)
-            pltpu.make_async_remote_copy(
-                src_ref=source.at[other],
-                dst_ref=target.at[self.me],
-                send_sem=sent.at[step],
-                recv_sem=came.at[step],
-                device_id=(self.dp, other),
-                device_id_type=MESH,
-            ).start()
-            return carry
-
-        lax.fori_loop(1, SEQ, one, 0)
-        target[self.me] = source[self.me]
-
-    def wait_all(self, source, target, sent, came):
-        def one(step, carry):
-            other = lax.rem(self.me + (SEQ - step), SEQ)
-            pltpu.make_async_remote_copy(
-                src_ref=source.at[other],
-                dst_ref=target.at[other],
-                send_sem=sent.at[step],
-                recv_sem=came.at[step],
-                device_id=(self.dp, other),
-                device_id_type=MESH,
-            ).wait_recv()
-            return carry
-
-        lax.fori_loop(1, SEQ, one, 0)
-
-    def wait_sent(self, source, target, sent, came):
-        def one(step, carry):
-            other = lax.rem(self.me + step, SEQ)
-            pltpu.make_async_remote_copy(
-                src_ref=source.at[other],
-                dst_ref=target.at[self.me],
-                send_sem=sent.at[step],
-                recv_sem=came.at[step],
-                device_id=(self.dp, other),
-                device_id_type=MESH,
-            ).wait_send()
-            return carry
-
-        lax.fori_loop(1, SEQ, one, 0)
+        return [(self.dp, self.at(*offset)) for offset in OFFSETS]
+
+    def half_offsets(self, half):
+        for y in (2, 1, 3, 0):
+            for step in (1, 0):
+                yield y, 2 * step + lax.rem(self.parity + (y + half), 2)
+
+    def copy(self, number, source, target, sems, other):
+        return pltpu.make_async_remote_copy(
+            src_ref=source,
+            dst_ref=target,
+            send_sem=sems[0].at[number],
+            recv_sem=sems[1].at[number],
+            device_id=(self.dp, other),
+            device_id_type=MESH,
+        )
 
     def start(self):
-        self.send_all(self.terms, self.landed, self.sems[0], self.sems[1])
+        for half in range(2):
+            for y, z in self.half_offsets(half):
+                other = self.at(y, z)
+                source = self.terms.at[self.unit_of(half, other)]
+                copy = self.copy(y * RING + z, source, self.landed.at[self.me], self.sems[:2], other)
+                if y:
+                    copy.start()
+                else:
+                    pl.when(z > 0)(copy.start)
+        self.landed[self.me] = self.terms[self.unit]
 
     def middle(self):
+        for y, z in OFFSETS:
+            other = self.at(y, z, -1)
+            came = self.landed.at[other]
+            self.copy(y * RING + z, came, came, self.sems[:2], other).wait_recv()
         total = jnp.zeros(self.landed.shape[1:], F32)
         for k in range(SEQ):
             at = SEQ - 1 - k if self.reverse else k
-            mine = self.me == at
-            ahead = lax.rem(at - self.me + SEQ, SEQ)
-            behind = lax.rem(self.me - at + SEQ, SEQ)
             self.sums[at] = total
-
-            @pl.when(mine)
-            def _():
-                self.result[at] = self.sums[at]
-
-            @pl.when(jnp.logical_not(mine))
-            def _():
-                pltpu.make_async_remote_copy(
-                    src_ref=self.sums.at[at],
-                    dst_ref=self.result.at[self.me],
-                    send_sem=self.sems[2].at[ahead],
-                    recv_sem=self.sems[3].at[ahead],
-                    device_id=(self.dp, at),
-                    device_id_type=MESH,
-                ).start()
-                pltpu.make_async_remote_copy(
-                    src_ref=self.terms.at[at],
-                    dst_ref=self.landed.at[at],
-                    send_sem=self.sems[0].at[behind],
-                    recv_sem=self.sems[1].at[behind],
-                    device_id=(self.dp, at),
-                    device_id_type=MESH,
-                ).wait_recv()
-
             total = total + self.landed[at]
-
-    def finish(self):
-        self.wait_all(self.sums, self.result, self.sems[2], self.sems[3])
+        for y, z in OFFSETS:
+            other = self.at(y, z)
+            target = self.result.at[self.unit]
+            self.copy(y * RING + z, self.sums.at[other], target, self.sems[2:], other).start()
+        self.result[self.unit] = self.sums[self.me]
+
+    def finish(self, half):
+        for y, z in self.half_offsets(half):
+            other = self.at(y, z, -1)
+            came = self.result.at[self.unit_of(half, other)]
+            copy = self.copy(y * RING + z, came, came, self.sems[2:], other)
+            if y:
+                copy.wait_recv()
+            else:
+                pl.when(z > 0)(copy.wait_recv)
 
     def drain(self):
-        self.wait_sent(self.terms, self.landed, self.sems[0], self.sems[1])
-        self.wait_sent(self.sums, self.result, self.sems[2], self.sems[3])
+        for y, z in OFFSETS:
+            number, other = y * RING + z, self.at(y, z)
+            self.copy(number, self.terms.at[0], self.landed.at[0], self.sems[:2], other).wait_send()
+            self.copy(number, self.sums.at[0], self.result.at[0], self.sems[2:], other).wait_send()
 
 
 SCAN_SCRATCH = [
@@ -603,8 +605,8 @@
 
 
 def attention_forward_kernel(
-    block, x, gain, shift, weight, cot_in, cat_out, cot_out, qkv_out, att_out, att_low_out, den_out, state,
-    w, cot, normed, qkv, att, att_low, den, cat, fq, fk, stage, land, terms, landed, sums, s0, s1, s2, s3,
+    block, x, gain, shift, weight, cot_in, cat_out, cot_out, qkv_out, att_out, att_low_out, den_out, state_out,
+    w, cot, normed, qkv, att, att_low, den, cat, fq, fk, stage, land, state, terms, landed, sums, s0, s1, s2, s3,
     wsem, osem, swap_sent, swap_came,
 ):
     place = Place()
@@ -688,14 +690,22 @@
         att[rows, columns] = both[:, :PAIR]
         den[rows, columns] = both[:, PAIR:]
 
-    for_units(local_part, 2)
+    def local_parts(start, count):
+        def two(index, carry):
+            local_part(start + 2 * index)
+            local_part(start + 2 * index + 1)
+            return carry
+
+        lax.fori_loop(0, count // 2, two, 0)
+
+    local_parts(0, 10)
+    scan.middle()
+    local_parts(10, 6)
     for core in range(2):
         cat[core, other, :] = swap.get(core, land.at[core])
         cot[other, pl.ds(core * TILE, TILE)] = swap.get(2 + core, land.at[2 + core])
     leave(cat, cat_out)
     leave(cot, cot_out)
-    scan.middle()
-    scan.finish()
     together = same_head()
 
     def incoming(unit):
@@ -714,6 +724,8 @@
         att_low[rows, columns] = attended.astype(BF16)
 
     for half in range(2):
+        scan.finish(half)
+        leave(state.at[pl.ds(half * 8, 8)], state_out.at[pl.ds(half * 8, 8)])
 
         def several(index, carry):
             incoming(half * 8 + 2 * index)
@@ -750,7 +762,7 @@
             struct((SEQ, 72, PAIR)),
         ],
         in_specs=[vmem, vmem, vmem, ANY_SPEC, ANY_SPEC],
-        out_specs=[ANY_SPEC] * 6 + [vmem],
+        out_specs=[ANY_SPEC] * 7,
         scratch_shapes=[
             pltpu.VMEM((3, width, width), BF16),
             pltpu.VMEM((2 * rows, width), BF16),
@@ -764,9 +776,10 @@
             pltpu.VMEM((rows, width), BF16),
             pltpu.VMEM((4, rows, TILE), F32),
             pltpu.VMEM((4, rows, TILE), F32),
+            SCAN_SCRATCH[0],
             *SCAN_SCRATCH,
             pltpu.SemaphoreType.DMA((4,)),
-            pltpu.SemaphoreType.DMA((10,)),
+            pltpu.SemaphoreType.DMA((12,)),
             pltpu.SemaphoreType.DMA((4,)),
             pltpu.SemaphoreType.DMA((4,)),
         ],
@@ -803,8 +816,8 @@
 
 
 def feed_forward_kernel(
-    x, att_low, gain, shift, cot_in, w_out, w_up, w_down,
-    output_out, gmixed_out, gatt_out, sums, norm_out, pre_out, out_out, down_a, down_b, down_c,
+    block_rows, x, att_low, gain, shift, cot_in, w_out, w_up, w_down, qkv_in, att_in, den_in,
+    output_out, gmixed_out, gn_out, sums, norm_out, pre_out, out_out, terms, down_a, down_b, down_c,
     wo, wu, wd, wsem, osem, output, gmixed, gatt, norm_cat, pre_cat, hidden, slope, cot_cat,
     stage, land, land_att, land_norm, swap_sent, swap_came, free, *scratch,
 ):
@@ -925,6 +938,8 @@
         norm_cat[other, columns] = swap.get(4 + tile, land_norm.at[tile])
         swap.put(10 + tile, tile, att_low[:, columns], land_att.at[tile], before=6 + tile)
     leave(norm_cat, norm_out)
+    query_load = pltpu.make_async_copy(qkv_in.at[0], slope.at[:, pl.ds(0, 1024)], wsem.at[4])
+    query_load.start()
     pl.semaphore_signal(free, inc=1, device_id=place.partner(), device_id_type=MESH)
     for stream in down:
         stream.forward()
@@ -947,7 +962,7 @@
         gatt[:, columns] = dot_nt(hidden[:, pl.ds(0, 1024)], wo[columns, :])
 
     for_columns(1024, TILE, back_out)
-    leave(gatt, gatt_out)
+    query_load.wait()
     ours = hidden[:, half_tile(0, core)]
     theirs = swap.get(12, land_norm.at[0])
     for tile in range(2):
@@ -957,10 +972,35 @@
             theirs_att = land_att[tile, :, pl.ds(start, width)].astype(BF16)
             land[2 * tile + part, pl.ds(0, width), :] = product + tn_dot(theirs_att, theirs)
             leave(land.at[2 * tile + part, pl.ds(0, width)], out_out.at[pl.ds(tile * TILE + start, width)])
-    for stream, out in zip(down, (down_a, down_b, down_c)):
-        stream.finish(out)
     for number, slot in ((9, 3), (10, 0), (11, 1), (12, 2)):
         swap.copy(number, slot, land_norm.at[0]).wait_send()
+    state_loads = []
+    for tile in range(2):
+        columns = pl.ds(tile * TILE, TILE)
+        for source, slot in ((att_in, tile), (den_in, 2 + tile)):
+            state_loads.append(pltpu.make_async_copy(source.at[:, columns], stage.at[slot], wsem.at[5 + slot]))
+            state_loads[-1].start()
+    for copy in state_loads:
+        copy.wait()
+    first_wide = first_head(block_rows)
+
+    def local_state(unit):
+        index, columns = unit_slices(unit, block_rows)
+        pair = lax.rem(unit, 8)
+        within = pl.ds(pl.multiple_of(lax.rem(pair, 4) * PAIR, PAIR), PAIR)
+        tile = lax.div(pair, 4)
+        numer = gatt[index, columns] / stage[2 + tile, index, within]
+        gatt[index, columns] = numer
+        query = features(slope[index, columns].astype(F32))
+        blocks, row = state_gradient(query, numer, stage[tile, index, within], first_wide)
+        terms[unit, pl.ds(0, 64)] = blocks
+        terms[unit, pl.ds(64, 8)] = row
+
+    for_units(local_state, 2)
+    leave(gatt, gn_out)
+    for stream, target in zip(down, (down_a, down_b, down_c)):
+        stream.finish()
+        leave(stream.data, target)
     for stream in down:
         stream.drain()
     for copy in outs:
@@ -992,7 +1032,7 @@
     )(*operands)
 
 
-def feed_forward(x, att_low, gain, shift, cot_cat, w_out, w_up, w_down):
+def feed_forward(x, att_low, gain, shift, cot_cat, w_out, w_up, w_down, qkv, att, den, block):
     rows, width = x.shape
     wide = w_up.shape[1]
     outs = [
@@ -1003,14 +1043,15 @@
         struct((2 * rows, width), BF16),
         struct((2 * rows, wide // 2), BF16),
         struct((width, TILE)),
+        struct((SEQ, 72, PAIR)),
         *[struct((4, 4, 8, length)) for length in DOWN_WIDTHS],
     ]
     scratch = [
         pltpu.VMEM((width, width), BF16),
         pltpu.VMEM((width, wide), BF16),
         pltpu.VMEM((wide, width), BF16),
-        pltpu.SemaphoreType.DMA((4,)),
         pltpu.SemaphoreType.DMA((9,)),
+        pltpu.SemaphoreType.DMA((12,)),
         pltpu.VMEM((rows, width), BF16),
         pltpu.VMEM((rows, width), F32),
         pltpu.VMEM((rows, width), F32),
@@ -1029,10 +1070,14 @@
         *slab_shapes(DOWN_WIDTHS),
         *flatten([stream_scratch(length, (0,)) for length in DOWN_WIDTHS]),
     ]
-    specs = [VMEM_SPEC] * 4 + [ANY_SPEC] * 4
-    out_specs = [ANY_SPEC] * 3 + [VMEM_SPEC] + [ANY_SPEC] * 3 + [VMEM_SPEC] * 3
-    operands = (x, att_low, gain, shift, cot_cat, w_out, w_up, w_down)
-    return call(feed_forward_kernel, outs, out_specs, operands, specs, scratch, 1)
+    specs = [VMEM_SPEC] * 4 + [ANY_SPEC] * 7
+    out_specs = [ANY_SPEC] * 3 + [VMEM_SPEC] + [ANY_SPEC] * 3 + [VMEM_SPEC] + [ANY_SPEC] * 3
+    operands = (x, att_low, gain, shift, cot_cat, w_out, w_up, w_down, qkv, att, den)
+
+    def kernel(*refs):
+        feed_forward_kernel(block, *refs)
+
+    return call(kernel, outs, out_specs, operands, specs, scratch, 1)
 
 
 def last_scratch(rows, width):
@@ -1074,7 +1119,7 @@
 
 
 def last_kernel(
-    block, qkv_in, att_in, den_in, state_in, gatt_in, gmixed_in, norm_one_in, norm_in, pre_in,
+    block, qkv_in, att_in, terms_in, state_in, gn_in, gmixed_in, norm_one_in, norm_in, pre_in,
     down_in_a, down_in_b, down_in_c, out_in, x_in, weight, gain, sums_two,
     grad_input, grad_up, grad_out, grad_qkv, grad_down, grad_gains, *scratch,
 ):
@@ -1098,21 +1143,16 @@
         loads.append(copy)
         return copy
 
+    started = load(terms_in, scan.terms)
     down_in = (down_in_a, down_in_b, down_in_c)
     down_loads = [load(source, target) for source, target in zip(down_in, s["chunks"])]
-    started = [
-        load(qkv_in.at[0], qkv.at[0]),
-        load(gatt_in, gn),
-        load(den_in, grads.at[0]),
-        load(att_in, att),
-    ]
     up_loads = [load(pre_in, s["pre_cat"])]
     for which in range(2):
         for block_x in range(4):
             source = norm_in.at[:, pl.ds(block_x * 256 + which * 128, 128)]
             target = s["norm_cat"].at[which, :, pl.ds(block_x * 128, 128)]
             up_loads.append(load(source, target))
-    qkv_loads = [load(qkv_in.at[pl.ds(1, 2)], qkv.at[pl.ds(1, 2)]), load(state_in, s["state"])]
+    qkv_loads = [load(qkv_in, qkv), load(state_in, s["state"]), load(gn_in, gn), load(att_in, att)]
     out_loads = []
     for k in range(3):
         for which, start, length, at in stream_pieces(k, OUT_WIDTHS, TILE):
@@ -1128,12 +1168,6 @@
     first, second = head_masks()
     first_wide = first_head(block)
 
-    def slopes(index, columns, numer):
-        product = numer * att[index, columns]
-        ours = jnp.sum(jnp.where(first_wide, product, 0.0), axis=1, keepdims=True)
-        theirs = jnp.sum(jnp.where(first_wide, 0.0, product), axis=1, keepdims=True)
-        return -ours, -theirs
-
     up_first = [phases[0] for phases in s["up"]]
     down = [Stream(place, s["chunks"][k], ORDERS[k][1:], s["down"][k]) for k in range(3)]
     up = [Stream(place, slabs[k], ORDERS[k], s["up"][k]) for k in range(3)]
@@ -1146,36 +1180,20 @@
         for step, streams, k in steps:
             step(streams[k])
 
+    started.wait()
+    met(len(others))
+    scan.start()
     settle(down_loads)
-    met(len(others))
     for stream in down:
         stream.begin()
-    settle(started)
-
-    def local_state(unit):
-        index, columns = unit_slices(unit, block)
-        numer = gn[index, columns] / grads[0, index, columns]
-        gn[index, columns] = numer
-        one, two = slopes(index, columns, numer)
-        query = features(qkv[0, index, columns].astype(F32))
-        high, low = split(numer)
-        wide = tn_dot(query, jnp.concatenate([high, low], axis=1))
-        spread = jnp.where(first_wide, one, two)
-        total = jnp.sum(query.astype(F32) * spread, axis=0, keepdims=True)
-        blocks, row = pack_state(wide[:, :PAIR] + wide[:, PAIR:], total)
-        scan.terms[unit, pl.ds(0, 64)] = blocks
-        scan.terms[unit, pl.ds(64, 8)] = row
-
-    for_units(local_state, 2)
-    scan.start()
-    go((forward, down, 0), (forward, down, 1), (forward, down, 2))
     settle(up_loads)
     for k in range(3):
         stream_product(k, s["norm_cat"], s["pre_cat"], slabs[k], UP_WIDTHS, 2048)
         if k == 0:
             up[0].begin()
+        if k == 1:
+            go((forward, down, 2))
     norm_load = load(norm_one_in, s["norm_cat"])
-    go((proceed, down, 2))
     settle(qkv_loads)
     causal = causal_mask(block)
     causal_t = causal_mask(block, True)
@@ -1186,7 +1204,7 @@
         query, value = features(raw_query), qkv[2, index, columns]
         key = features(qkv[1, index, columns].astype(F32))
         numer = gn[index, columns]
-        one, two = slopes(index, columns, numer)
+        one, two = head_slopes(numer, att[index, columns], first_wide)
         high, low = split(numer)
         scores = dot_nt(jnp.concatenate([key * first, key * second], axis=0), query)
         wide = jnp.concatenate([high, low], axis=1)
@@ -1215,23 +1233,22 @@
 
         lax.fori_loop(0, count, one, 0)
 
-    local_parts(0, 4)
+    local_parts(0, 2)
     scan.middle()
+    go((forward, down, 0), (forward, down, 1))
     up[1].begin()
     up[2].begin()
-    go((proceed, down, 0), (proceed, down, 1))
-    local_parts(4, 4)
-    go((finish, down, 2))
-    local_parts(8, 1)
+    local_parts(2, 8)
     go((forward, up, 0))
-    local_parts(9, 7)
+    local_parts(10, 6)
     settle(out_loads)
     swap = Swap(place, s["stage"], *s["swap"])
     land, cat = s["land"], s["pre_cat"]
     own, other = pl.ds(0, rows), pl.ds(rows, rows)
     swap.put(0, 0, qkv[0, :, half_tile(0, 1 - core)], land.at[0])
     mixed_load = load(gmixed_in, att)
-    scan.finish()
+    scan.finish(0)
+    scan.finish(1)
 
     def incoming(unit):
         index, columns = unit_slices(unit, block)
@@ -1252,7 +1269,7 @@
     for_units(incoming, 2)
     for third in (1, 2):
         swap.put(third, third, qkv[third, :, half_tile(0, 1 - core)], land.at[third])
-    go((forward, up, 2))
+    go((proceed, down, 2), (proceed, down, 0), (proceed, down, 1))
     settle(late_loads)
 
     def back_norm(columns):
@@ -1264,7 +1281,7 @@
     for start in (0, 256, 512, 768):
         back_norm(pl.ds(start, 256))
         if start == 0:
-            go((forward, up, 1), (finish, down, 1))
+            go((forward, up, 1), (forward, up, 2))
     for third in range(3):
         columns = pl.ds(third * TILE, TILE)
         cat[own, columns] = qkv[third, :, half_tile(0, core)]
@@ -1304,18 +1321,19 @@
     for stream in out:
         stream.begin()
     turn(0)
-    go((forward, out, 0), (finish, down, 0))
+    go((forward, out, 0))
     turn(1)
-    go((forward, out, 1), (forward, out, 2))
+    go((forward, out, 2), (forward, out, 1))
     turn(2)
     go(
-        (forward, qkv_sum, 0), (proceed, out, 2), (begin, vec, 0), (forward, qkv_sum, 1), (forward, qkv_sum, 2),
-        (begin, up, 0), (begin, up, 1), (begin, up, 2), (proceed, out, 0), (proceed, out, 1), (proceed, qkv_sum, 1),
-        (proceed, qkv_sum, 0), (forward, up, 0), (proceed, out, 2), (proceed, qkv_sum, 2), (proceed, vec, 0),
-        (forward, up, 1), (proceed, out, 0), (forward, up, 2), (forward, qkv_sum, 0), (proceed, out, 1),
-        (forward, qkv_sum, 2), (forward, qkv_sum, 1), (proceed, up, 0), (proceed, up, 2), (finish, out, 2),
-        (proceed, up, 1), (proceed, vec, 0), (proceed, qkv_sum, 0), (proceed, qkv_sum, 2), (proceed, qkv_sum, 1),
-        (finish, out, 1), (finish, out, 0), (finish, up, 0), (finish, up, 2), (finish, up, 1), (finish, vec, 0),
+        (proceed, out, 2), (finish, down, 1), (finish, down, 2), (finish, down, 0), (begin, vec, 0),
+        (forward, qkv_sum, 0), (forward, qkv_sum, 1), (forward, qkv_sum, 2), (begin, up, 0), (begin, up, 1),
+        (begin, up, 2), (proceed, out, 1), (proceed, out, 0), (proceed, vec, 0), (proceed, qkv_sum, 1),
+        (proceed, qkv_sum, 2), (proceed, qkv_sum, 0), (forward, up, 0), (forward, up, 1), (forward, up, 2),
+        (forward, qkv_sum, 1), (forward, qkv_sum, 2), (forward, qkv_sum, 0), (proceed, out, 2), (proceed, vec, 0),
+        (proceed, out, 0), (proceed, out, 1), (proceed, up, 0), (proceed, qkv_sum, 1), (proceed, qkv_sum, 2),
+        (proceed, qkv_sum, 0), (proceed, up, 1), (proceed, up, 2), (finish, out, 2), (finish, out, 0),
+        (finish, out, 1), (finish, vec, 0), (finish, up, 0), (finish, up, 1), (finish, up, 2),
     )
     for k in range(3):
         piece = down[k].data
@@ -1342,7 +1360,7 @@
     )
     vec_copy.start()
     swap_rows(out, OUT_WIDTHS, TILE, s["out_rows"], 1)
-    go((finish, qkv_sum, 2), (finish, qkv_sum, 0), (finish, qkv_sum, 1))
+    go((finish, qkv_sum, 1), (finish, qkv_sum, 0), (finish, qkv_sum, 2))
     swap_rows(qkv_sum, QKV_WIDTHS, 3 * TILE, s["qkv_rows"], 2)
     scan.drain()
     for number in range(3):
@@ -1360,7 +1378,7 @@
     lay_rows(place, *s["qkv_rows"], grad_qkv)
 
 
-def last_part(qkv, att, den, state, gatt, gmixed, norm_one, norm_cat, pre_cat, down, out, x, weight, gain, sums_two, block):
+def last_part(qkv, att, terms, state, gn, gmixed, norm_one, norm_cat, pre_cat, down, out, x, weight, gain, sums_two, block):
     rows, width = x.shape
 
     def kernel(*refs):
@@ -1378,35 +1396,31 @@
     scratch = [leaf for name in like for leaf in flatten(like[name])]
     out = out.reshape(4, 2, 4, 4, 8, TILE)
     operands = (
-        qkv, att, den, state, gatt, gmixed, norm_one, norm_cat, pre_cat, *down, out, x, weight, gain, sums_two,
+        qkv, att, terms, state, gn, gmixed, norm_one, norm_cat, pre_cat, *down, out, x, weight, gain, sums_two,
     )
     specs = [ANY_SPEC] * 15 + [VMEM_SPEC] * 2
     out_specs = [ANY_SPEC] + [VMEM_SPEC] * 5
     return call(kernel, outs, out_specs, operands, specs, scratch, 2)
 
 
-def lay_out_kernel(output, grad_input, up, out, qkv, down, gains, output_to, grad_to, up_to, out_to, qkv_to, down_to, a, b, c, d):
-    pairs = (
-        (output, output_to), (grad_input, grad_to), (up, up_to), (out, out_to), (qkv, qkv_to), (down, down_to),
-    )
-    for source, target in pairs:
-        target[...] = source[...]
+def lay_out_kernel(gains, *refs):
+    targets = refs[-4:]
     core = lax.rem(lax.axis_index("dp"), 2)
     turned = jnp.transpose(jnp.concatenate([gains[...], jnp.zeros((120, 128), F32)], axis=0))
-    for k, target in enumerate((a, b, c, d)):
+    for k, target in enumerate(targets):
         target[...] = jnp.where(core == 0, turned[k : k + 1, :8], turned[4 + k : 5 + k, :8])
 
 
-def lay_out(output, *grads):
-    arrays = (output, *grads[:-1])
-    outs = [struct(array.shape, array.dtype) for array in arrays] + [struct((1, 8))] * 4
+def lay_out(gains, *arrays):
+    count = len(arrays)
     return pl.pallas_call(
         lay_out_kernel,
-        out_shape=outs,
-        in_specs=[VMEM_SPEC] * 7,
-        out_specs=[VMEM_SPEC] * 10,
+        out_shape=[struct(array.shape, array.dtype) for array in arrays] + [struct((1, 8))] * 4,
+        in_specs=[VMEM_SPEC] + [ANY_SPEC] * count,
+        out_specs=[ANY_SPEC] * count + [VMEM_SPEC] * 4,
+        input_output_aliases={k + 1: k for k in range(count)},
         compiler_params=pltpu.CompilerParams(vmem_limit_bytes=62 * MIB),
-    )(output, *grads)
+    )(gains, *arrays)
 
 
 def body(
@@ -1430,14 +1444,15 @@
     norm_one, cot_cat, qkv, att, att_low, den, state = attention_forward(
         x, first_gain, first_shift, qkv_weight, cot, block
     )
-    output, gmixed, gatt, sums_two, norm_cat, pre_cat, out, *down = feed_forward(
-        x, att_low, gain_two, shift_two, cot_cat, out_weight, up_weight, down_weight
+    output, gmixed, gn, sums_two, norm_cat, pre_cat, out, terms, *down = feed_forward(
+        x, att_low, gain_two, shift_two, cot_cat, out_weight, up_weight, down_weight, qkv, att, den, block
     )
     grads = last_part(
-        qkv, att, den, state, gatt, gmixed, norm_one, norm_cat, pre_cat, down, out, x, qkv_weight,
+        qkv, att, terms, state, gn, gmixed, norm_one, norm_cat, pre_cat, down, out, x, qkv_weight,
         gain_one, sums_two, block,
     )
-    output, grad_input, grad_up, grad_out, grad_qkv, grad_down, *gains = lay_out(output, *grads)
+    *grads, gains = grads
+    output, grad_input, grad_up, grad_out, grad_qkv, grad_down, *gains = lay_out(gains, output, *grads)
     return (
         output.reshape(inputs.shape),
         grad_input.reshape(inputs.shape),

time: 177 us -> 181 us (1.023)
  local copies, waits for them, and re-layouts: 0 us -> 5.91 us
  Pallas kernels: 175 us -> 173 us
    unnamed x0 -> x16, local copies, waits for them, and re-layouts: none -> 5.91 us
    pallas_call x1, Pallas kernels: 3.38 us -> 1.29 us  [lay_out(): pl.pallas_call(lay_out_kernel, out_shape=[struct(array.shape, array.dtype...]
where the time goes in v5:
time: 181 us; the launch traced here: 180 us
  Pallas kernels  173 us (96%)
  local copies, waits for them, and re-layouts  5.91 us (3%)
    pallas_call x2, Pallas kernels, call(): pl.pallas_call(kernel, out_shape=outs, in_specs=in_specs, out_specs=out_s...  140 us
    pallas_call x1, Pallas kernels, attention_forward(): pl.pallas_call(kernel, out_shape=[struct((2, 2 * rows, width // 2), BF16)...  32 us
    unnamed x16, local copies, waits for them, and re-layouts  5.91 us

profile of v5, /device:TPU:0, one launch (start us, length us, event | category | flops | bytes accessed | tf_op | source)
XLA Modules:
  0.0 179.8 jit_solution(6717248579533711382)
XLA Ops:
  0.6 32.0 %shard_map.177 = (bf16[2,768,512]{2,1,0:T(8,128)(2,1)}, bf16[768,1024]{1,0:T(8,128)(2,1)}, bf16[3,384,1024]{2,1,0:T(8,128)(2,1)}, f32[384,1024]{1,0:T(8,128)}, b...) custom-call(bf16[384,1024]{1,0:T(8,128)(2,1)} %bitcast.13, f32[1,1024]{1,0:T(1,128)} %bitcast.20, ...), custom_call_target="tpu_custom_call" | custom-call | tf_op jit(solution)/shard_map/pallas_call | solution.py:753
  32.6 45.3 %shard_map.178 = (bf16[384,1024]{1,0:T(8,128)(2,1)}, f32[384,1024]{1,0:T(8,128)}, f32[384,1024]{1,0:T(8,128)}, f32[8,1024]{1,0:T(8,128)}, bf16[768,1024]{1,0:T(8...) custom-call(bf16[384,1024]{1,0:T(8,128)(2,1)} %bitcast.14, ...), custom_call_target="tpu_custom_call" | custom-call | tf_op jit(solution)/shard_map/pallas_call | solution.py:1023
  77.9 94.6 %shard_map.179 = (f32[384,1024]{1,0:T(8,128)}, f32[8,4096]{1,0:T(8,128)}, f32[8,1024]{1,0:T(8,128)}, f32[8,3072]{1,0:T(8,128)}, f32[32,1024]{1,0:T(8,128)}, /*index=5*/f32[8,128]{1,0:T(8,128)}) custom-call(bf16[3,384,1024]{2,1,0:T(8,128)(2,1)} %get-tuple-element.44.refs_8_.refs_0_, f32[384,1024]{1,0:T(8,128)} %get-tuple-element.45.refs_9_.refs_1_, ...), custom_call_target="tpu_custom_call" | custom-call | tf_op jit(solution)/shard_map/pallas_call | solution.py:1023
  172.5 1.3 shard_map.180
  173.8 0.0 copy-start
  173.8 2.2 %copy.38 = bf16[2,192,1024]{2,1,0:T(8,128)(2,1)} copy(bf16[2,192,1024]{2,1,0:T(8,128)(2,1)} %bitcast.17) | data formatting | bytes 1572864
  176.0 0.0 copy-done
  176.0 0.0 copy-start.3
  176.0 0.0 copy-start.4
  176.0 0.0 copy-start.1
  176.0 0.0 copy-start.2
  176.0 1.1 copy.39
  177.2 0.0 copy-done.3
  177.2 0.6 copy.40
  177.8 0.0 copy-done.4
  177.8 0.6 copy.41
  178.4 0.0 copy-done.1
  178.4 0.7 copy.42
  179.1 0.0 copy-done.2
  179.1 0.7 copy.43
Async XLA Ops:
  173.8 2.2 %copy-start = (f32[384,1024]{1,0:T(8,128)S(1)}, f32[384,1024]{1,0:T(8,128)}, u32[]{:S(2)}) copy-start(f32[384,1024]{1,0:T(8,128)} %get-tuple-element.69) | copy-start | bytes 4718596
  176.0 1.2 copy-start.3
  176.0 1.8 %copy-start.4 = (f32[8,1024]{1,0:T(8,128)S(1)}, f32[8,1024]{1,0:T(8,128)}, u32[]{:S(2)}) copy-start(f32[8,1024]{1,0:T(8,128)} %get-tuple-element.91) | copy-start | bytes 98308
  176.0 2.4 %copy-start.1 = (f32[8,4096]{1,0:T(8,128)S(1)}, f32[8,4096]{1,0:T(8,128)}, u32[]{:S(2)}) copy-start(f32[8,4096]{1,0:T(8,128)} %get-tuple-element.92) | copy-start | bytes 393220
  176.0 3.1 %copy-start.2 = (f32[32,1024]{1,0:T(8,128)S(1)}, f32[32,1024]{1,0:T(8,128)}, u32[]{:S(2)}) copy-start(f32[32,1024]{1,0:T(8,128)} %get-tuple-element.93) | copy-start | bytes 393220

commit v6 on v5

--- a/solution.py
+++ b/solution.py
@@ -53,7 +53,7 @@
 ORDERS = ((0, 1, 2), (1, 2, 0), (2, 0, 1))
 
 
-def phase_scratch(remaining, length):
+def phase_scratch(remaining, length, messages=6):
     if remaining:
         half = (2, 2, *[4] * (remaining - 1), 8, length)
     else:
@@ -61,8 +61,8 @@
     return [
         pltpu.VMEM((2, *[4] * remaining, 8, length), F32),
         pltpu.VMEM(half, F32),
-        pltpu.SemaphoreType.DMA((6,)),
-        pltpu.SemaphoreType.DMA((6,)),
+        pltpu.SemaphoreType.DMA((messages,)),
+        pltpu.SemaphoreType.DMA((messages,)),
     ]
 
 
@@ -122,16 +122,15 @@
             if not self.empty(way):
                 self.send(0, way, self.part(opposite, way), self.through(way))
 
-    def begin_near(self):
-        for way in range(2):
-            if self.empty(1 - way):
-                continue
+    def begin_near(self, way):
+        if not self.empty(1 - way):
             target = self.part(self.full.at[way], 1 - way)
             self.send(1, way, self.part(self.beside(way), 1 - way), target)
 
     def begin(self):
         self.begin_far()
-        self.begin_near()
+        for way in range(2):
+            self.begin_near(way)
 
     def forward(self):
         for way in range(2):
@@ -159,6 +158,67 @@
             copy.wait_send()
 
 
+HALVES = ((2, 1), (3, 0))
+
+
+class SplitPhase(Phase):
+    def block(self, way, j):
+        return self.place.ring(0, HALVES[way][j])
+
+    def copy_block(self, kind, way, j, source, target):
+        number = kind * 4 + way * 2 + j
+        return pltpu.make_async_remote_copy(
+            src_ref=source,
+            dst_ref=target,
+            send_sem=self.sent.at[number],
+            recv_sem=self.came.at[number],
+            device_id=self.place.neighbour(self.axis, 1 - 2 * way),
+            device_id_type=MESH,
+        )
+
+    def send_far(self, way, j):
+        source = self.chunk(self.place.ring(self.axis, 2)).at[self.block(way, j)]
+        self.flying.append(self.copy_block(0, way, j, source, self.half.at[way, j]))
+        self.flying[-1].start()
+
+    def send_near(self, kind, way, j):
+        block = self.block(way if kind == 2 else 1 - way, j)
+        source, target = self.beside(way).at[block], self.full.at[way, block]
+        self.flying.append(self.copy_block(kind, way, j, source, target))
+        self.flying[-1].start()
+
+    def begin_first(self):
+        for j in range(2):
+            self.send_far(0, j)
+        self.send_near(1, 1, 0)
+
+    def begin_second(self):
+        for j in range(2):
+            self.send_far(1, j)
+        self.send_near(1, 1, 1)
+        for j in range(2):
+            self.send_near(1, 0, j)
+
+    def forward(self):
+        for way in range(2):
+            for j in range(2):
+                came = self.half.at[way, j]
+                self.copy_block(0, way, j, came, came).wait_recv()
+                own = self.beside(way).at[self.block(way, j)]
+                add_into(own, own, came)
+                self.send_near(2, way, j)
+
+    def finish(self, out=None):
+        own = self.chunk(self.place.at[self.axis])
+        for way in range(2):
+            for kind, part in ((1, 1 - way), (2, way)):
+                for j in range(2):
+                    target = self.full.at[way, self.block(part, j)]
+                    self.copy_block(kind, way, j, target, target).wait_recv()
+        add_into(own if out is None else out, own, self.full.at[0], self.full.at[1])
+        return own
+
+
 class Direct:
     def __init__(self, place, data, axes, axis, scratch):
         self.place, self.data, self.axis = place, data, axis
@@ -201,16 +261,105 @@
             copy.wait_send()
 
 
+class Route:
+    def __init__(self, place, data, axis, pieces, scratch, out):
+        self.place, self.data, self.axis, self.pieces, self.out = place, data, axis, pieces, out
+        self.scratch = scratch
+
+    def send_each(self, act):
+        core = self.place.core
+        for (owner, _, width, at), (land, sent, came) in zip(self.pieces, self.scratch):
+
+            def copy(step):
+                position = list(self.place.at)
+                position[self.axis] = self.place.ring(self.axis, step)
+                return pltpu.make_async_remote_copy(
+                    src_ref=self.data.at[self.place.ring(self.axis, step), :, pl.ds(at, width)],
+                    dst_ref=land.at[core, step],
+                    send_sem=sent.at[step],
+                    recv_sem=came.at[core, step],
+                    device_id=self.place.id_of(*position, owner),
+                    device_id_type=MESH,
+                )
+
+            for step in (2, 1, 3):
+                act(copy(step))
+
+            @pl.when(core != owner)
+            def _():
+                act(copy(0))
+
+    def begin(self):
+        self.send_each(lambda copy: copy.start())
+
+    def forward(self):
+        pass
+
+    def finish(self, out=None):
+        core = self.place.core
+        mine = self.place.at[self.axis]
+        for (owner, start, width, at), (land, sent, came) in zip(self.pieces, self.scratch):
+
+            @pl.when(core == owner)
+            def _():
+                for source, steps in ((core, (1, 2, 3)), (1 - core, (0, 1, 2, 3))):
+                    for step in steps:
+                        target = land.at[source, step]
+                        pltpu.make_async_remote_copy(
+                            src_ref=target,
+                            dst_ref=target,
+                            send_sem=sent.at[step],
+                            recv_sem=came.at[source, step],
+                            device_id=self.place.partner(),
+                            device_id_type=MESH,
+                        ).wait_recv()
+                done = 0
+                while done < width:
+                    column = start + done
+                    tile, within = column // TILE, column % TILE
+                    step = min(TILE - within, width - done)
+                    part = pl.ds(done, step)
+                    ours = self.data[mine, :, pl.ds(at + done, step)]
+                    for k in (1, 2, 3):
+                        ours = ours + land[core, k, :, part]
+                    theirs = land[1 - core, 0, :, part]
+                    for k in (1, 2, 3):
+                        theirs = theirs + land[1 - core, k, :, part]
+                    for values, half in ((ours, core), (theirs, 1 - core)):
+                        place = pl.multiple_of((2 * tile + half) * TILE + within, 128)
+                        self.out[:, pl.ds(place, step)] = values
+                    done += step
+
+    def drain(self):
+        self.send_each(lambda copy: copy.wait_send())
+
+
+def route_scratch(stream, widths, columns):
+    return [
+        [
+            pltpu.VMEM((2, 4, 8, width), F32),
+            pltpu.SemaphoreType.DMA((4,)),
+            pltpu.SemaphoreType.DMA((2, 4)),
+        ]
+        for _, _, width, _ in stream_pieces(stream, widths, columns)
+    ]
+
+
 class Stream:
-    def __init__(self, place, data, order, scratch):
-        self.place, self.data, self.scratch = place, data, scratch
+    def __init__(self, place, data, order, scratch, first=None, last=None):
+        self.place, self.data, self.scratch, self.first, self.last = place, data, scratch, first, last
         self.todo, self.old = [axis for axis in order], []
         self.axes = sorted(order)
         self.phase = None
 
     def prepare(self):
         scratch = self.scratch.pop(0)
-        kind = Phase if len(scratch) == 4 else Direct
+        if self.last and len(self.todo) == 1:
+            pieces, out = self.last
+            self.phase = Route(self.place, self.data, self.todo[0], pieces, scratch, out)
+            return self.phase
+        kind = self.first or (Phase if len(scratch) == 4 else Direct)
+        self.first = None
         self.phase = kind(self.place, self.data, self.axes, self.todo[0], scratch)
         return self.phase
 
@@ -360,30 +509,6 @@
 def stream_product(stream, left, right, slab, widths, columns):
     for core, start, width, at in stream_pieces(stream, widths, columns):
         core_product(left, core, right, start, width, slab, at)
-
-
-def shared_rows(streams, widths, columns, rows):
-    for stream in range(3):
-        for core, start, width, at in stream_pieces(stream, widths, columns):
-            rows[core, :, pl.ds(start, width)] = streams[stream].data[:, pl.ds(at, width)]
-
-
-def row_swap(place, rows, land, sems):
-    return pltpu.make_async_remote_copy(
-        src_ref=rows.at[1 - place.core],
-        dst_ref=land,
-        send_sem=sems.at[0],
-        recv_sem=sems.at[1],
-        device_id=place.partner(),
-        device_id_type=MESH,
-    )
-
-
-def lay_rows(place, rows, land, out):
-    for tile in range(land.shape[1] // TILE):
-        columns = pl.ds(tile * TILE, TILE)
-        out[:, half_tile(tile, place.core)] = rows[place.core, :, columns]
-        out[:, half_tile(tile, 1 - place.core)] = land[:, columns]
 
 
 DOWN_CUTS = ((0, 384), (384, 384), (768, 256))
@@ -824,7 +949,7 @@
     take_scratch = Taker(scratch)
     slabs = take_scratch(slab_shapes(DOWN_WIDTHS))
     slab_a, slab_b, slab_c = slabs
-    phases = take_scratch([stream_scratch(length, (0,)) for length in DOWN_WIDTHS])
+    phases = take_scratch([[phase_scratch(2, length, 12)] for length in DOWN_WIDTHS])
     place = Place()
     core = place.core
     rows = x.shape[0]
@@ -866,17 +991,21 @@
         slope[:, columns] = ours_slope
         return ours
 
-    def give(block, carry):
-        theirs = up(half_columns(block, 1 - core, 1024))
-        swap.put(block, block, theirs, land.at[block])
+    def nth_block(index):
+        return lax.rem(place.at[0] + jnp.where(index == 2, 3, jnp.maximum(2 - index, 0)), RING)
+
+    def give(index, carry):
+        theirs = up(half_columns(nth_block(index), 1 - core, 1024))
+        swap.put(index, index, theirs, land.at[index])
         return carry
 
     lax.fori_loop(0, 4, give, 0)
     loads[2].wait()
 
-    def take(block, carry):
+    def take(index, carry):
+        block = nth_block(index)
         ours = up(half_columns(block, core, 1024))
-        both = jnp.concatenate([ours, swap.get(block, land.at[block])], axis=0)
+        both = jnp.concatenate([ours, swap.get(index, land.at[index])], axis=0)
         for half in range(2):
             columns = pl.ds(half * TILE, TILE)
             product = tn_dot(both, cot_cat[:, columns]).reshape(4, 4, 4, 8, TILE)
@@ -891,13 +1020,19 @@
                 slab_c[block, :, :, :, pl.ds(1024, 256)] = last[..., 256:]
         return carry
 
-    lax.fori_loop(0, 4, take, 0)
+    kinds = (None, SplitPhase, SplitPhase)
+    down = [Stream(place, slabs[k], ORDERS[k], phases[k], kinds[k]) for k in range(3)]
+    first, *split = [stream.prepare() for stream in down]
+    lax.fori_loop(0, 2, take, 0)
+    first.begin_far()
+    for phase in split:
+        phase.begin_first()
+    first.begin_near(0)
+    lax.fori_loop(2, 4, take, 0)
+    for phase in split:
+        phase.begin_second()
+    first.begin_near(1)
     pl.semaphore_signal(free, inc=1, device_id=place.partner(), device_id_type=MESH)
-    down = [Stream(place, slabs[k], ORDERS[k], phases[k]) for k in range(3)]
-    for stream in down:
-        stream.prepare().begin_far()
-    for stream in down:
-        stream.phase.begin_near()
     for tile in range(2):
         columns = pl.ds(tile * TILE, TILE)
         swap.put(4 + tile, tile, norm_cat[own, columns], land_norm.at[tile], before=tile)
@@ -925,9 +1060,22 @@
 
     lax.fori_loop(0, 4, give_back, 0)
 
+    def keep_back(block, carry):
+        columns = pl.ds(pl.multiple_of(block * TILE, TILE), TILE)
+        pre_cat[own, columns] = back(half_columns(block, core, 1024))
+        return carry
+
+    lax.fori_loop(0, 4, keep_back, 0)
+    for stream in down:
+        stream.forward()
+
+    def back_up(columns):
+        gmixed[:, columns] = dot_nt(hidden[...], wu[columns, :])
+
+    for_columns(1024, 256, back_up)
+
     def take_back(block, carry):
         columns = pl.ds(pl.multiple_of(block * TILE, TILE), TILE)
-        pre_cat[own, columns] = back(half_columns(block, core, 1024))
         pre_cat[other, columns] = swap.get(6 + block, land.at[block])
         return carry
 
@@ -941,14 +1089,6 @@
     query_load = pltpu.make_async_copy(qkv_in.at[0], slope.at[:, pl.ds(0, 1024)], wsem.at[4])
     query_load.start()
     pl.semaphore_signal(free, inc=1, device_id=place.partner(), device_id_type=MESH)
-    for stream in down:
-        stream.forward()
-
-    def back_up(columns):
-        gmixed[:, columns] = dot_nt(hidden[...], wu[columns, :])
-
-    for_columns(1024, 256, back_up)
-
     def store(index, values):
         gmixed[index, :] = values
         hidden[index, pl.ds(0, 1024)] = values.astype(BF16)
@@ -961,9 +1101,21 @@
     def back_out(columns):
         gatt[:, columns] = dot_nt(hidden[:, pl.ds(0, 1024)], wo[columns, :])
 
+    state_loads = [query_load]
+
+    def load_state(slots):
+        for slot in slots:
+            source = (att_in, den_in)[slot // 2].at[:, pl.ds(slot % 2 * TILE, TILE)]
+            state_loads.append(pltpu.make_async_copy(source, stage.at[slot], wsem.at[5 + slot]))
+            state_loads[-1].start()
+
+    for number, slot in ((9, 3), (10, 0), (11, 1)):
+        swap.copy(number, slot, land_norm.at[0]).wait_send()
+    load_state((0, 1, 3))
     for_columns(1024, TILE, back_out)
-    query_load.wait()
     ours = hidden[:, half_tile(0, core)]
+    swap.copy(12, 2, land_norm.at[0]).wait_send()
+    load_state((2,))
     theirs = swap.get(12, land_norm.at[0])
     for tile in range(2):
         swap.copy(10 + tile, tile, land_att.at[tile]).wait_recv()
@@ -972,14 +1124,6 @@
             theirs_att = land_att[tile, :, pl.ds(start, width)].astype(BF16)
             land[2 * tile + part, pl.ds(0, width), :] = product + tn_dot(theirs_att, theirs)
             leave(land.at[2 * tile + part, pl.ds(0, width)], out_out.at[pl.ds(tile * TILE + start, width)])
-    for number, slot in ((9, 3), (10, 0), (11, 1), (12, 2)):
-        swap.copy(number, slot, land_norm.at[0]).wait_send()
-    state_loads = []
-    for tile in range(2):
-        columns = pl.ds(tile * TILE, TILE)
-        for source, slot in ((att_in, tile), (den_in, 2 + tile)):
-            state_loads.append(pltpu.make_async_copy(source.at[:, columns], stage.at[slot], wsem.at[5 + slot]))
-            state_loads[-1].start()
     for copy in state_loads:
         copy.wait()
     first_wide = first_head(block_rows)
@@ -1068,7 +1212,7 @@
         pltpu.SemaphoreType.DMA((13,)),
         pltpu.SemaphoreType.REGULAR,
         *slab_shapes(DOWN_WIDTHS),
-        *flatten([stream_scratch(length, (0,)) for length in DOWN_WIDTHS]),
+        *flatten([[phase_scratch(2, length, 12)] for length in DOWN_WIDTHS]),
     ]
     specs = [VMEM_SPEC] * 4 + [ANY_SPEC] * 7
     out_specs = [ANY_SPEC] * 3 + [VMEM_SPEC] + [ANY_SPEC] * 3 + [VMEM_SPEC] + [ANY_SPEC] * 3
@@ -1102,15 +1246,19 @@
         "vec_slab": pltpu.VMEM((4, 4, 4, 8, 128), F32),
         "sums": pltpu.VMEM((8, width), F32),
         "down": [stream_scratch(length, (1, 2), (2,)) for length in DOWN_WIDTHS],
-        "up": [stream_scratch(length, (0, 1, 2), (2,)) for length in UP_WIDTHS],
-        "out": [stream_scratch(length, (0, 1, 2), (1, 2)) for length in OUT_WIDTHS],
+        "up": [
+            [*stream_scratch(length, (0, 1)), route_scratch(k, UP_WIDTHS, 2048)] for k, length in enumerate(UP_WIDTHS)
+        ],
+        "out": [
+            [*stream_scratch(length, (0, 1), (1,)), route_scratch(k, OUT_WIDTHS, TILE)]
+            for k, length in enumerate(OUT_WIDTHS)
+        ],
         "qkv_sems": [[pltpu.SemaphoreType.DMA((6,))] * 2 for _ in QKV_WIDTHS],
-        "qkv_sum": [stream_scratch(length, (1, 2), (2,)) for length in QKV_WIDTHS],
+        "qkv_sum": [
+            [*stream_scratch(length, (1,)), route_scratch(k, QKV_WIDTHS, 3 * TILE)]
+            for k, length in enumerate(QKV_WIDTHS)
+        ],
         "vec": stream_scratch(128, (0, 1, 2), (0, 1, 2)),
-        "up_rows": [pltpu.VMEM((2, 8, 2048), F32), pltpu.VMEM((8, 2048), F32)],
-        "out_rows": [pltpu.VMEM((2, 8, 512), F32), pltpu.VMEM((8, 512), F32)],
-        "qkv_rows": [pltpu.VMEM((2, 8, 1536), F32), pltpu.VMEM((8, 1536), F32)],
-        "row_sems": pltpu.SemaphoreType.DMA((3, 2)),
         "vec_land": pltpu.VMEM((8, 128), F32),
         "vec_sems": pltpu.SemaphoreType.DMA((2,)),
         "credit": pltpu.SemaphoreType.REGULAR((3,)),
@@ -1133,7 +1281,13 @@
     slabs = s["slabs"]
     scan = Scan(*s["scan"][:4], s["scan"][4:], True)
     across = [place.neighbour(0, step) for step in (1, -1, 2)]
-    others = [*across, place.partner(), *scan.others()]
+    beside = []
+    for axis in range(3):
+        for step in (1, 2, 3):
+            position = list(place.at)
+            position[axis] = place.ring(axis, step)
+            beside.append(place.id_of(*position, 1 - core))
+    others = [*across, place.partner(), *beside, *scan.others()]
     greet(others)
     loads = []
 
@@ -1144,21 +1298,21 @@
         return copy
 
     started = load(terms_in, scan.terms)
-    down_in = (down_in_a, down_in_b, down_in_c)
-    down_loads = [load(source, target) for source, target in zip(down_in, s["chunks"])]
+    out_loads = []
+    for k in (0, 2, 1):
+        for which, start, length, at in stream_pieces(k, OUT_WIDTHS, TILE):
+            source = out_in.at[:, which, :, :, :, pl.ds(start, length)]
+            target = s["out_slabs"][k].at[:, :, :, :, pl.ds(at, length)]
+            out_loads.append(load(source, target))
     up_loads = [load(pre_in, s["pre_cat"])]
     for which in range(2):
         for block_x in range(4):
             source = norm_in.at[:, pl.ds(block_x * 256 + which * 128, 128)]
             target = s["norm_cat"].at[which, :, pl.ds(block_x * 128, 128)]
             up_loads.append(load(source, target))
+    down_in = (down_in_a, down_in_b, down_in_c)
+    down_loads = [load(source, target) for source, target in zip(down_in, s["chunks"])]
     qkv_loads = [load(qkv_in, qkv), load(state_in, s["state"]), load(gn_in, gn), load(att_in, att)]
-    out_loads = []
-    for k in range(3):
-        for which, start, length, at in stream_pieces(k, OUT_WIDTHS, TILE):
-            source = out_in.at[:, which, :, :, :, pl.ds(start, length)]
-            target = s["out_slabs"][k].at[:, :, :, :, pl.ds(at, length)]
-            out_loads.append(load(source, target))
     late_loads = [load(weight, s["w"]), load(x_in, s["x"])]
 
     def settle(copies):
@@ -1170,8 +1324,14 @@
 
     up_first = [phases[0] for phases in s["up"]]
     down = [Stream(place, s["chunks"][k], ORDERS[k][1:], s["down"][k]) for k in range(3)]
-    up = [Stream(place, slabs[k], ORDERS[k], s["up"][k]) for k in range(3)]
-    out = [Stream(place, s["out_slabs"][k], ORDERS[k], s["out"][k]) for k in range(3)]
+    up = [
+        Stream(place, slabs[k], ORDERS[k], s["up"][k], None, (stream_pieces(k, UP_WIDTHS, 2048), grad_up))
+        for k in range(3)
+    ]
+    out = [
+        Stream(place, s["out_slabs"][k], ORDERS[k], s["out"][k], None, (stream_pieces(k, OUT_WIDTHS, TILE), grad_out))
+        for k in range(3)
+    ]
     qkv_sum = [None] * 3
     vec = [Stream(place, s["vec_slab"], ORDERS[0], s["vec"])]
     begin, forward, proceed, finish = Stream.begin, Stream.forward, Stream.proceed, Stream.finish
@@ -1180,19 +1340,19 @@
         for step, streams, k in steps:
             step(streams[k])
 
+    settle(out_loads)
+    met(len(others))
+    go((begin, out, 0))
     started.wait()
-    met(len(others))
     scan.start()
-    settle(down_loads)
-    for stream in down:
-        stream.begin()
+    go((begin, out, 2))
     settle(up_loads)
     for k in range(3):
         stream_product(k, s["norm_cat"], s["pre_cat"], slabs[k], UP_WIDTHS, 2048)
-        if k == 0:
-            up[0].begin()
         if k == 1:
-            go((forward, down, 2))
+            settle(down_loads)
+            go((begin, down, 0), (begin, up, 0))
+    go((begin, out, 1))
     norm_load = load(norm_one_in, s["norm_cat"])
     settle(qkv_loads)
     causal = causal_mask(block)
@@ -1235,13 +1395,15 @@
 
     local_parts(0, 2)
     scan.middle()
-    go((forward, down, 0), (forward, down, 1))
-    up[1].begin()
-    up[2].begin()
-    local_parts(2, 8)
+    local_parts(2, 1)
+    go((begin, up, 2), (forward, out, 2), (forward, out, 0))
+    local_parts(3, 2)
+    go((forward, out, 1))
+    local_parts(5, 3)
+    go((begin, up, 1))
+    local_parts(8, 7)
     go((forward, up, 0))
-    local_parts(10, 6)
-    settle(out_loads)
+    local_parts(15, 1)
     swap = Swap(place, s["stage"], *s["swap"])
     land, cat = s["land"], s["pre_cat"]
     own, other = pl.ds(0, rows), pl.ds(rows, rows)
@@ -1249,6 +1411,7 @@
     mixed_load = load(gmixed_in, att)
     scan.finish(0)
     scan.finish(1)
+    go((begin, down, 2))
 
     def incoming(unit):
         index, columns = unit_slices(unit, block)
@@ -1269,7 +1432,6 @@
     for_units(incoming, 2)
     for third in (1, 2):
         swap.put(third, third, qkv[third, :, half_tile(0, 1 - core)], land.at[third])
-    go((proceed, down, 2), (proceed, down, 0), (proceed, down, 1))
     settle(late_loads)
 
     def back_norm(columns):
@@ -1280,12 +1442,11 @@
 
     for start in (0, 256, 512, 768):
         back_norm(pl.ds(start, 256))
-        if start == 0:
-            go((forward, up, 1), (forward, up, 2))
     for third in range(3):
         columns = pl.ds(third * TILE, TILE)
         cat[own, columns] = qkv[third, :, half_tile(0, core)]
         cat[other, columns] = swap.get(third, land.at[third])
+    go((forward, up, 2), (forward, up, 1))
     norm_load.wait()
     mixed_load.wait()
     def turn(k):
@@ -1303,7 +1464,8 @@
         stream_product(k, s["norm_cat"], cat, data, QKV_WIDTHS, 3 * TILE)
         pl.semaphore_wait(s["credit"].at[k], 2)
         phases = [[up_first[k][0].at[narrow], up_first[k][1].at[narrow], *s["qkv_sems"][k]]]
-        qkv_sum[k] = Stream(place, data, ORDERS[k], phases + s["qkv_sum"][k])
+        last = (stream_pieces(k, QKV_WIDTHS, 3 * TILE), grad_qkv)
+        qkv_sum[k] = Stream(place, data, ORDERS[k], phases + s["qkv_sum"][k], None, last)
         qkv_sum[k].begin()
 
     def store(index, values):
@@ -1312,43 +1474,28 @@
     sums = s["sums"]
     norm_back_rows(s["x"], gn, att, gain, sums, store)
     leave = load(gn, grad_input)
+    go((begin, down, 1), (proceed, out, 0))
     four = jnp.concatenate([sums[0:2, :], sums_two[0:2, :]], axis=0)
     eight = jnp.concatenate([four, four], axis=0)
     turned = jnp.transpose(jnp.concatenate([eight, jnp.zeros((120, 1024), F32)], axis=0))
     turned = turned.reshape(4, 2, 4, 4, 8, 128)
     lane = lax.broadcasted_iota(jnp.int32, (8, 128), 1)
     s["vec_slab"][...] = jnp.where(lane < 4, turned[:, 0], jnp.where(lane < 8, turned[:, 1], 0.0))
-    for stream in out:
-        stream.begin()
+    go((begin, vec, 0), (proceed, out, 1))
     turn(0)
-    go((forward, out, 0))
+    turn(2)
+    go((begin, up, 0))
     turn(1)
-    go((forward, out, 2), (forward, out, 1))
-    turn(2)
     go(
-        (proceed, out, 2), (finish, down, 1), (finish, down, 2), (finish, down, 0), (begin, vec, 0),
-        (forward, qkv_sum, 0), (forward, qkv_sum, 1), (forward, qkv_sum, 2), (begin, up, 0), (begin, up, 1),
-        (begin, up, 2), (proceed, out, 1), (proceed, out, 0), (proceed, vec, 0), (proceed, qkv_sum, 1),
-        (proceed, qkv_sum, 2), (proceed, qkv_sum, 0), (forward, up, 0), (forward, up, 1), (forward, up, 2),
-        (forward, qkv_sum, 1), (forward, qkv_sum, 2), (forward, qkv_sum, 0), (proceed, out, 2), (proceed, vec, 0),
-        (proceed, out, 0), (proceed, out, 1), (proceed, up, 0), (proceed, qkv_sum, 1), (proceed, qkv_sum, 2),
-        (proceed, qkv_sum, 0), (proceed, up, 1), (proceed, up, 2), (finish, out, 2), (finish, out, 0),
-        (finish, out, 1), (finish, vec, 0), (finish, up, 0), (finish, up, 1), (finish, up, 2),
+        (forward, qkv_sum, 0), (forward, qkv_sum, 2), (begin, up, 1), (forward, down, 2), (forward, down, 1),
+        (begin, up, 2), (proceed, out, 0), (forward, qkv_sum, 1), (proceed, vec, 0), (proceed, qkv_sum, 2),
+        (proceed, qkv_sum, 0), (proceed, qkv_sum, 1), (forward, down, 0), (forward, up, 0), (forward, up, 1),
+        (proceed, out, 2), (proceed, vec, 0), (forward, qkv_sum, 2), (forward, up, 2), (proceed, down, 1),
+        (forward, qkv_sum, 0), (forward, qkv_sum, 1), (proceed, down, 2), (proceed, down, 0), (proceed, qkv_sum, 2),
+        (proceed, up, 0), (proceed, up, 1), (proceed, out, 2), (proceed, qkv_sum, 0), (proceed, up, 2),
+        (proceed, out, 1), (proceed, qkv_sum, 1), (finish, down, 2), (finish, down, 1), (finish, down, 0),
+        (finish, up, 1), (finish, vec, 0),
     )
-    for k in range(3):
-        piece = down[k].data
-        grad_down[pl.ds(8 * k, 8), :] = piece[:, pl.ds(0, 1024)]
-        start, width_k = DOWN_CUTS[k]
-        grad_down[pl.ds(24, 8), pl.ds(start, width_k)] = piece[:, pl.ds(1024, width_k)]
-    swaps = []
-
-    def swap_rows(streams, widths, columns, rows_land, slot):
-        shared_rows(streams, widths, columns, rows_land[0])
-        copy = row_swap(place, *rows_land, s["row_sems"].at[slot])
-        copy.start()
-        swaps.append(copy)
-
-    swap_rows(up, UP_WIDTHS, 2048, s["up_rows"], 0)
     vec_tile = vec[0].data
     vec_copy = pltpu.make_async_remote_copy(
         src_ref=vec_tile,
@@ -1359,9 +1506,15 @@
         device_id_type=MESH,
     )
     vec_copy.start()
-    swap_rows(out, OUT_WIDTHS, TILE, s["out_rows"], 1)
-    go((finish, qkv_sum, 1), (finish, qkv_sum, 0), (finish, qkv_sum, 2))
-    swap_rows(qkv_sum, QKV_WIDTHS, 3 * TILE, s["qkv_rows"], 2)
+    go(
+        (finish, up, 0), (finish, qkv_sum, 0), (finish, qkv_sum, 2), (finish, out, 0), (finish, qkv_sum, 1),
+        (finish, out, 2), (finish, out, 1), (finish, up, 2),
+    )
+    for k in range(3):
+        piece = down[k].data
+        grad_down[pl.ds(8 * k, 8), :] = piece[:, pl.ds(0, 1024)]
+        start, width_k = DOWN_CUTS[k]
+        grad_down[pl.ds(24, 8), pl.ds(start, width_k)] = piece[:, pl.ds(1024, width_k)]
     scan.drain()
     for number in range(3):
         swap.copy(number, number, land.at[number]).wait_send()
@@ -1370,12 +1523,6 @@
     vec_copy.wait()
     grad_gains[...] = vec_tile[...] + s["vec_land"][...]
     leave.wait()
-    swaps[0].wait()
-    lay_rows(place, *s["up_rows"], grad_up)
-    swaps[1].wait()
-    lay_rows(place, *s["out_rows"], grad_out)
-    swaps[2].wait()
-    lay_rows(place, *s["qkv_rows"], grad_qkv)
 
 
 def last_part(qkv, att, terms, state, gn, gmixed, norm_one, norm_cat, pre_cat, down, out, x, weight, gain, sums_two, block):
@@ -1403,24 +1550,28 @@
     return call(kernel, outs, out_specs, operands, specs, scratch, 2)
 
 
-def lay_out_kernel(gains, *refs):
-    targets = refs[-4:]
+def lay_out_kernel(output, grad_input, up, out, qkv, down, gains, output_to, grad_to, up_to, out_to, qkv_to, down_to, a, b, c, d):
+    pairs = (
+        (output, output_to), (grad_input, grad_to), (up, up_to), (out, out_to), (qkv, qkv_to), (down, down_to),
+    )
+    for source, target in pairs:
+        target[...] = source[...]
     core = lax.rem(lax.axis_index("dp"), 2)
     turned = jnp.transpose(jnp.concatenate([gains[...], jnp.zeros((120, 128), F32)], axis=0))
-    for k, target in enumerate(targets):
+    for k, target in enumerate((a, b, c, d)):
         target[...] = jnp.where(core == 0, turned[k : k + 1, :8], turned[4 + k : 5 + k, :8])
 
 
-def lay_out(gains, *arrays):
-    count = len(arrays)
+def lay_out(output, *grads):
+    arrays = (output, *grads[:-1])
+    outs = [struct(array.shape, array.dtype) for array in arrays] + [struct((1, 8))] * 4
     return pl.pallas_call(
         lay_out_kernel,
-        out_shape=[struct(array.shape, array.dtype) for array in arrays] + [struct((1, 8))] * 4,
-        in_specs=[VMEM_SPEC] + [ANY_SPEC] * count,
-        out_specs=[ANY_SPEC] * count + [VMEM_SPEC] * 4,
-        input_output_aliases={k + 1: k for k in range(count)},
+        out_shape=outs,
+        in_specs=[VMEM_SPEC] * 7,
+        out_specs=[VMEM_SPEC] * 10,
         compiler_params=pltpu.CompilerParams(vmem_limit_bytes=62 * MIB),
-    )(gains, *arrays)
+    )(output, *grads)
 
 
 def body(
@@ -1451,8 +1602,7 @@
         qkv, att, terms, state, gn, gmixed, norm_one, norm_cat, pre_cat, down, out, x, qkv_weight,
         gain_one, sums_two, block,
     )
-    *grads, gains = grads
-    output, grad_input, grad_up, grad_out, grad_qkv, grad_down, *gains = lay_out(gains, output, *grads)
+    output, grad_input, grad_up, grad_out, grad_qkv, grad_down, *gains = lay_out(output, *grads)
     return (
         output.reshape(inputs.shape),
         grad_input.reshape(inputs.shape),

time: 181 us -> 173 us (0.956)
  local copies, waits for them, and re-layouts: 5.91 us -> 0 us
  Pallas kernels: 173 us -> 171 us
    unnamed x16 -> x0, local copies, waits for them, and re-layouts: 5.91 us -> none
    pallas_call x2, Pallas kernels: 140 us -> 135 us  [call(): pl.pallas_call(kernel, out_shape=outs, in_specs=in_specs, out_specs=out_s...]
    pallas_call x1, Pallas kernels: 1.29 us -> 3.38 us  [lay_out(): pl.pallas_call(lay_out_kernel, out_shape=outs, in_specs=[VMEM_SPEC] * 7,...]
where the time goes in v6:
time: 173 us; the launch traced here: 171 us
  Pallas kernels  171 us (99%)
    pallas_call x2, Pallas kernels, call(): pl.pallas_call(kernel, out_shape=outs, in_specs=in_specs, out_specs=out_s...  135 us
    pallas_call x1, Pallas kernels, attention_forward(): pl.pallas_call(kernel, out_shape=[struct((2, 2 * rows, width // 2), BF16)...  32 us

profile of v6, /device:TPU:0, one launch (start us, length us, event | category | flops | bytes accessed | tf_op | source)
XLA Modules:
  0.0 171.4 jit_solution(3027636458562551727)
XLA Ops:
  0.6 32.0 %shard_map.177 = (bf16[2,768,512]{2,1,0:T(8,128)(2,1)}, bf16[768,1024]{1,0:T(8,128)(2,1)}, bf16[3,384,1024]{2,1,0:T(8,128)(2,1)}, f32[384,1024]{1,0:T(8,128)}, b...) custom-call(bf16[384,1024]{1,0:T(8,128)(2,1)} %bitcast.13, f32[1,1024]{1,0:T(1,128)} %bitcast.18, ...), custom_call_target="tpu_custom_call" | custom-call | tf_op jit(solution)/shard_map/pallas_call | solution.py:878
  32.7 42.2 %shard_map.178 = (bf16[384,1024]{1,0:T(8,128)(2,1)}, f32[384,1024]{1,0:T(8,128)}, f32[384,1024]{1,0:T(8,128)}, f32[8,1024]{1,0:T(8,128)}, bf16[768,1024]{1,0:T(8...) custom-call(bf16[384,1024]{1,0:T(8,128)(2,1)} %bitcast.14, ...), custom_call_target="tpu_custom_call" | custom-call | tf_op jit(solution)/shard_map/pallas_call | solution.py:1167
  74.9 93.0 %shard_map.179 = (f32[384,1024]{1,0:T(8,128)}, f32[8,4096]{1,0:T(8,128)}, f32[8,1024]{1,0:T(8,128)}, f32[8,3072]{1,0:T(8,128)}, f32[32,1024]{1,0:T(8,128)}, /*index=5*/f32[8,128]{1,0:T(8,128)}) custom-call(bf16[3,384,1024]{2,1,0:T(8,128)(2,1)} %get-tuple-element.46.refs_8_.refs_0_, f32[384,1024]{1,0:T(8,128)} %get-tuple-element.47.refs_9_.refs_1_, ...), custom_call_target="tpu_custom_call" | custom-call | tf_op jit(solution)/shard_map/pallas_call | solution.py:1167
  167.8 3.4 %shard_map.180 = (bf16[384,1024]{1,0:T(8,128)(2,1)}, f32[384,1024]{1,0:T(8,128)}, f32[8,4096]{1,0:T(8,128)}, f32[8,1024]{1,0:T(8,128)}, f32[8,3072]{1,0:T(8,128)...) custom-call(bf16[384,1024]{1,0:T(8,128)(2,1)} %get-tuple-element.49.output, ...), custom_call_target="tpu_custom_call" | custom-call | tf_op jit(solution)/shard_map/pallas_call | solution.py:1568

commit v7 on v6

--- a/solution.py
+++ b/solution.py
@@ -593,6 +593,24 @@
 )
 
 
+class Units:
+    def __init__(self, ref):
+        self.ref = ref
+
+    def at(self, unit):
+        rows = pl.ds(pl.multiple_of(lax.div(lax.rem(unit, 8), 4) * 72, 8), 72)
+        columns = pl.ds(pl.multiple_of(lax.rem(unit, 4) * PAIR, PAIR), PAIR)
+        return self.ref.at[lax.div(unit, 8), rows, columns]
+
+
+class Slots:
+    def __init__(self, ref):
+        self.ref = ref
+
+    def at(self, unit):
+        return self.ref.at[unit]
+
+
 class Scan:
     def __init__(self, terms, landed, sums, result, sems, reverse):
         self.terms, self.landed, self.sums, self.result = terms, landed, sums, result
@@ -632,34 +650,34 @@
         for half in range(2):
             for y, z in self.half_offsets(half):
                 other = self.at(y, z)
-                source = self.terms.at[self.unit_of(half, other)]
-                copy = self.copy(y * RING + z, source, self.landed.at[self.me], self.sems[:2], other)
+                source = self.terms.at(self.unit_of(half, other))
+                copy = self.copy(y * RING + z, source, self.landed.at(self.me), self.sems[:2], other)
                 if y:
                     copy.start()
                 else:
                     pl.when(z > 0)(copy.start)
-        self.landed[self.me] = self.terms[self.unit]
+        self.landed.at(self.me)[...] = self.terms.at(self.unit)[...]
 
     def middle(self):
         for y, z in OFFSETS:
             other = self.at(y, z, -1)
-            came = self.landed.at[other]
+            came = self.landed.at(other)
             self.copy(y * RING + z, came, came, self.sems[:2], other).wait_recv()
-        total = jnp.zeros(self.landed.shape[1:], F32)
+        total = jnp.zeros((72, PAIR), F32)
         for k in range(SEQ):
             at = SEQ - 1 - k if self.reverse else k
-            self.sums[at] = total
-            total = total + self.landed[at]
+            self.sums.at(at)[...] = total
+            total = total + self.landed.at(at)[...]
         for y, z in OFFSETS:
             other = self.at(y, z)
-            target = self.result.at[self.unit]
-            self.copy(y * RING + z, self.sums.at[other], target, self.sems[2:], other).start()
-        self.result[self.unit] = self.sums[self.me]
+            target = self.result.at(self.unit)
+            self.copy(y * RING + z, self.sums.at(other), target, self.sems[2:], other).start()
+        self.result.at(self.unit)[...] = self.sums.at(self.me)[...]
 
     def finish(self, half):
         for y, z in self.half_offsets(half):
             other = self.at(y, z, -1)
-            came = self.result.at[self.unit_of(half, other)]
+            came = self.result.at(self.unit_of(half, other))
             copy = self.copy(y * RING + z, came, came, self.sems[2:], other)
             if y:
                 copy.wait_recv()
@@ -669,8 +687,8 @@
     def drain(self):
         for y, z in OFFSETS:
             number, other = y * RING + z, self.at(y, z)
-            self.copy(number, self.terms.at[0], self.landed.at[0], self.sems[:2], other).wait_send()
-            self.copy(number, self.sums.at[0], self.result.at[0], self.sems[2:], other).wait_send()
+            self.copy(number, self.terms.at(0), self.landed.at(0), self.sems[:2], other).wait_send()
+            self.copy(number, self.sums.at(0), self.result.at(0), self.sems[2:], other).wait_send()
 
 
 SCAN_SCRATCH = [
@@ -729,195 +747,14 @@
     lax.fori_loop(0, count // width, one, 0)
 
 
-def attention_forward_kernel(
-    block, x, gain, shift, weight, cot_in, cat_out, cot_out, qkv_out, att_out, att_low_out, den_out, state_out,
-    w, cot, normed, qkv, att, att_low, den, cat, fq, fk, stage, land, state, terms, landed, sums, s0, s1, s2, s3,
-    wsem, osem, swap_sent, swap_came,
-):
-    place = Place()
-    rows_all = x.shape[0]
-    own, other = pl.ds(0, rows_all), pl.ds(rows_all, rows_all)
-    outs = []
-
-    def leave(source, target):
-        outs.append(pltpu.make_async_copy(source, target, osem.at[len(outs)]))
-        outs[-1].start()
-
-    scan = Scan(terms, landed, sums, state, (s0, s1, s2, s3), False)
-    others = [*scan.others(), place.partner()]
-    greet(others)
-    loads = []
-    cot_load = pltpu.make_async_copy(cot_in, cot.at[own], wsem.at[3])
-    for slot, third in enumerate((1, 2, 0)):
-        load = pltpu.make_async_copy(
-            weight.at[:, pl.ds(third * 1024, 1024)], w.at[slot], wsem.at[slot]
-        )
-        load.start()
-        loads.append(load)
-    cot_load.start()
-
-    def norm_step(rows):
-        scaled, _ = norm_rows(x[rows, :].astype(F32))
-        normed[rows, :] = (scaled * gain[...] + shift[...]).astype(BF16)
-
-    for_rows(x.shape[0], norm_step)
-
-    def project(slot, third, feature):
-        loads[slot].wait()
-
-        def step(columns):
-            raw = dot_nn(normed[...], w[slot, :, columns]).astype(BF16)
-            qkv[third, :, columns] = raw
-            if feature is not None:
-                feature[:, columns] = features(raw.astype(F32))
-
-        for_columns(1024, 512, step)
-
-    project(0, 1, fk)
-    project(1, 2, None)
-
-    def local_state(unit):
-        rows, columns = unit_slices(unit, block)
-        keys = fk[rows, columns]
-        square = tn_dot(qkv[2, rows, columns], keys)
-        total = jnp.sum(keys.astype(F32), axis=0, keepdims=True)
-        blocks, row = pack_state(square, total)
-        terms[unit, pl.ds(0, 64)] = blocks
-        terms[unit, pl.ds(64, 8)] = row
-
-    for_units(local_state, 4)
-    met(len(others))
-    scan.start()
-    swap = Swap(place, stage, swap_sent, swap_came)
-    for core in range(2):
-        for block_x in range(4):
-            columns = pl.ds(block_x * 256 + core * 128, 128)
-            cat[core, own, pl.ds(block_x * 128, 128)] = normed[:, columns]
-        swap.put(core, core, cat[core, own, :], land.at[core])
-    cot_load.wait()
-    for tile in range(2):
-        swap.put(2 + tile, 2 + tile, cot[own, pl.ds(tile * TILE, TILE)], land.at[2 + tile])
-    leave(qkv.at[pl.ds(1, 2)], qkv_out.at[pl.ds(1, 2)])
-    project(2, 0, fq)
-    leave(qkv.at[0], qkv_out.at[0])
-    first, second = head_masks()
-    causal = causal_mask(block)
-
-    def local_part(unit):
-        rows, columns = unit_slices(unit, block)
-        query, key, value = fq[rows, columns], fk[rows, columns], qkv[2, rows, columns]
-        scores = dot_nt(jnp.concatenate([query * first, query * second], axis=0), key)
-        both = 0.0
-        for head, mask in enumerate((first, second)):
-            own = jnp.where(causal, scores[head * block : (head + 1) * block], 0.0).astype(BF16)
-            right = jnp.concatenate([value * mask, jnp.broadcast_to(mask, value.shape)], axis=1)
-            both = both + dot_nn(own, right)
-        att[rows, columns] = both[:, :PAIR]
-        den[rows, columns] = both[:, PAIR:]
-
-    def local_parts(start, count):
-        def two(index, carry):
-            local_part(start + 2 * index)
-            local_part(start + 2 * index + 1)
-            return carry
-
-        lax.fori_loop(0, count // 2, two, 0)
-
-    local_parts(0, 10)
-    scan.middle()
-    local_parts(10, 6)
-    for core in range(2):
-        cat[core, other, :] = swap.get(core, land.at[core])
-        cot[other, pl.ds(core * TILE, TILE)] = swap.get(2 + core, land.at[2 + core])
-    leave(cat, cat_out)
-    leave(cot, cot_out)
-    together = same_head()
-
-    def incoming(unit):
-        rows, columns = unit_slices(unit, block)
-        square, total = unpack_state(state[unit])
-        totals = jnp.where(together, jnp.broadcast_to(total, (PAIR, PAIR)), 0.0)
-        high, low = split(jnp.concatenate([square, totals], axis=0))
-        query = fq[rows, columns]
-        both = dot_nt(
-            jnp.concatenate([query, query], axis=1), jnp.concatenate([high, low], axis=1)
-        )
-        denom = den[rows, columns] + both[:, PAIR:]
-        den[rows, columns] = denom
-        attended = (att[rows, columns] + both[:, :PAIR]) / denom
-        att[rows, columns] = attended
-        att_low[rows, columns] = attended.astype(BF16)
-
-    for half in range(2):
-        scan.finish(half)
-        leave(state.at[pl.ds(half * 8, 8)], state_out.at[pl.ds(half * 8, 8)])
-
-        def several(index, carry):
-            incoming(half * 8 + 2 * index)
-            incoming(half * 8 + 2 * index + 1)
-            return carry
-
-        lax.fori_loop(0, 4, several, 0)
-        part = pl.ds(half * block, block)
-        leave(att.at[part], att_out.at[part])
-        leave(den.at[part], den_out.at[part])
-        leave(att_low.at[part], att_low_out.at[part])
-    scan.drain()
-    swap.drain(range(4), land.at[0])
-    for copy in outs:
-        copy.wait()
-
-
-def attention_forward(x, gain, shift, weight, cot, block):
-    rows, width = x.shape
-    vmem = pl.BlockSpec(memory_space=pltpu.VMEM)
-
-    def kernel(*refs):
-        attention_forward_kernel(block, *refs)
-
-    return pl.pallas_call(
-        kernel,
-        out_shape=[
-            struct((2, 2 * rows, width // 2), BF16),
-            struct((2 * rows, width), BF16),
-            struct((3, rows, width), BF16),
-            struct((rows, width)),
-            struct((rows, width), BF16),
-            struct((rows, width)),
-            struct((SEQ, 72, PAIR)),
-        ],
-        in_specs=[vmem, vmem, vmem, ANY_SPEC, ANY_SPEC],
-        out_specs=[ANY_SPEC] * 7,
-        scratch_shapes=[
-            pltpu.VMEM((3, width, width), BF16),
-            pltpu.VMEM((2 * rows, width), BF16),
-            pltpu.VMEM((rows, width), BF16),
-            pltpu.VMEM((3, rows, width), BF16),
-            pltpu.VMEM((rows, width), F32),
-            pltpu.VMEM((rows, width), BF16),
-            pltpu.VMEM((rows, width), F32),
-            pltpu.VMEM((2, 2 * rows, width // 2), BF16),
-            pltpu.VMEM((rows, width), BF16),
-            pltpu.VMEM((rows, width), BF16),
-            pltpu.VMEM((4, rows, TILE), F32),
-            pltpu.VMEM((4, rows, TILE), F32),
-            SCAN_SCRATCH[0],
-            *SCAN_SCRATCH,
-            pltpu.SemaphoreType.DMA((4,)),
-            pltpu.SemaphoreType.DMA((12,)),
-            pltpu.SemaphoreType.DMA((4,)),
-            pltpu.SemaphoreType.DMA((4,)),
-        ],
-        compiler_params=pltpu.CompilerParams(
-            collective_id=5, has_side_effects=True, vmem_limit_bytes=62 * MIB
-        ),
-    )(x, gain.reshape(1, width), shift.reshape(1, width), weight, cot)
+SLOPE_SCALE = 28000.0
 
 
 def gelu_both(pre):
     cumulative = 0.5 * (1.0 + lax.erf(pre * (1.0 / math.sqrt(2.0))))
     density = jnp.exp(-0.5 * pre * pre) * (1.0 / math.sqrt(2.0 * math.pi))
-    return (pre * cumulative).astype(BF16), (cumulative + pre * density).astype(BF16)
+    slope = (cumulative + pre * density) * SLOPE_SCALE
+    return (pre * cumulative).astype(BF16), jnp.round(slope).astype(jnp.int32).astype(jnp.int16)
 
 
 def norm_back(grad, gain, scaled, inverse):
@@ -940,11 +777,12 @@
     for_rows(grad.shape[0], step)
 
 
-def feed_forward_kernel(
-    block_rows, x, att_low, gain, shift, cot_in, w_out, w_up, w_down, qkv_in, att_in, den_in,
-    output_out, gmixed_out, gn_out, sums, norm_out, pre_out, out_out, terms, down_a, down_b, down_c,
-    wo, wu, wd, wsem, osem, output, gmixed, gatt, norm_cat, pre_cat, hidden, slope, cot_cat,
-    stage, land, land_att, land_norm, swap_sent, swap_came, free, *scratch,
+def front_kernel(
+    block, x, gain_one, shift_one, gain, shift, w_qkv, cot_in, w_out, w_up, w_down,
+    norm_one_out, qkv_out, att_out, den_out, state_out, output_out, gmixed_out, gn_out, sums, norm_out, pre_out,
+    out_out, terms, down_a, down_b, down_c,
+    wo, wu, wd, wsem, osem, att_low, state, output, gmixed, gatt, norm_cat, pre_cat, hidden, slope, cot_cat,
+    stage, land, land_att, land_norm, swap_sent, swap_came, free, s0, s1, s2, s3, *scratch,
 ):
     take_scratch = Taker(scratch)
     slabs = take_scratch(slab_shapes(DOWN_WIDTHS))
@@ -953,90 +791,234 @@
     place = Place()
     core = place.core
     rows = x.shape[0]
-    others = link_neighbours(place)
+    scan = Scan(Slots(terms), Units(land_att), Units(land_norm), Slots(state), (s0, s1, s2, s3), False)
+    others = [place.neighbour(0, 1), place.neighbour(0, -1), place.partner(), *scan.others()]
     greet(others)
     own, other = pl.ds(0, rows), pl.ds(rows, rows)
+
+    def load(source, target, slot):
+        copy = pltpu.make_async_copy(source, target, wsem.at[slot])
+        copy.start()
+        return copy
+
+    outs = []
+
+    def leave(source, target):
+        copy = pltpu.make_async_copy(source, target, osem.at[len(outs)])
+        copy.start()
+        outs.append(copy)
+        return copy
+
+    def settle(copies):
+        for copy in copies:
+            copy.wait()
+            settled.append(id(copy))
+
+    settled = []
+    thirds = [
+        load(w_qkv.at[:, pl.ds(third * 1024, 1024)], wu.at[:, pl.ds(slot * 1024, 1024)], slot)
+        for slot, third in enumerate((1, 2, 0))
+    ]
+    cot_load = load(cot_in, cot_cat.at[own], 3)
+    out_load = load(w_out, wo, 4)
+
+    def norm_step(index):
+        scaled, _ = norm_rows(x[index, :].astype(F32))
+        hidden[index, pl.ds(0, 1024)] = (scaled * gain_one[...] + shift_one[...]).astype(BF16)
+
+    for_rows(rows, norm_step)
+
+    def shifted(columns, offset):
+        return pl.ds(pl.multiple_of(columns.start + offset, PAIR), columns.size)
+
+    def later_rows(index, offset):
+        return pl.ds(pl.multiple_of(index.start + offset, 64), index.size)
+
+    def project(slot, third, feature):
+        thirds[slot].wait()
+
+        def step(columns):
+            raw = dot_nn(hidden[:, pl.ds(0, 1024)], wu[:, shifted(columns, slot * 1024)]).astype(BF16)
+            hidden[:, shifted(columns, 1024 + third * 1024)] = raw
+            if feature is not None:
+                wd[pl.ds(feature * rows, rows), columns] = features(raw.astype(F32))
+
+        for_columns(1024, TILE, step)
+
+    project(0, 1, 1)
+    project(1, 2, None)
+
+    def local_state(unit):
+        index, columns = unit_slices(unit, block)
+        keys = wd[later_rows(index, rows), columns]
+        square = tn_dot(hidden[index, shifted(columns, 3072)], keys)
+        total = jnp.sum(keys.astype(F32), axis=0, keepdims=True)
+        blocks, row = pack_state(square, total)
+        terms[unit, pl.ds(0, 64)] = blocks
+        terms[unit, pl.ds(64, 8)] = row
+
+    for_units(local_state, 4)
+    met(len(others))
+    scan.start()
+    swap = Swap(place, stage, swap_sent, swap_came)
+    for which in range(2):
+        for block_x in range(4):
+            columns = pl.ds(block_x * 256 + which * 128, 128)
+            pre_cat[own, pl.ds(which * TILE + block_x * 128, 128)] = hidden[:, columns]
+        swap.put(which, which, pre_cat[own, pl.ds(which * TILE, TILE)], land.at[which])
+    cot_load.wait()
+    for tile in range(2):
+        swap.put(2 + tile, 2 + tile, cot_cat[own, pl.ds(tile * TILE, TILE)], land.at[2 + tile])
+    qkv_leaves = [leave(hidden.at[:, pl.ds(third * 1024 + 1024, 1024)], qkv_out.at[third]) for third in (1, 2)]
+    project(2, 0, 0)
+    qkv_leaves.append(leave(hidden.at[:, pl.ds(1024, 1024)], qkv_out.at[0]))
+    up_load = load(w_up, wu, 6)
+    first, second = head_masks()
+    causal = causal_mask(block)
+
+    def local_part(unit):
+        index, columns = unit_slices(unit, block)
+        query, key = wd[index, columns], wd[later_rows(index, rows), columns]
+        value = hidden[index, shifted(columns, 3072)]
+        scores = dot_nt(jnp.concatenate([query * first, query * second], axis=0), key)
+        both = 0.0
+        for head, mask in enumerate((first, second)):
+            kept = jnp.where(causal, scores[head * block : (head + 1) * block], 0.0).astype(BF16)
+            right = jnp.concatenate([value * mask, jnp.broadcast_to(mask, value.shape)], axis=1)
+            both = both + dot_nn(kept, right)
+        gmixed[index, columns] = both[:, :PAIR]
+        gatt[index, columns] = both[:, PAIR:]
+
+    def local_parts(start, count):
+        def two(index, carry):
+            local_part(start + 2 * index)
+            local_part(start + 2 * index + 1)
+            return carry
+
+        lax.fori_loop(0, count // 2, two, 0)
+
+    local_parts(0, 10)
+    scan.middle()
+    local_parts(10, 6)
+    for which in range(2):
+        pre_cat[other, pl.ds(which * TILE, TILE)] = swap.get(which, land.at[which])
+        cot_cat[other, pl.ds(which * TILE, TILE)] = swap.get(2 + which, land.at[2 + which])
+    cat_leaves = [leave(pre_cat.at[:, pl.ds(which * TILE, TILE)], norm_one_out.at[which]) for which in range(2)]
+    together = same_head()
+
+    def incoming(unit):
+        index, columns = unit_slices(unit, block)
+        square, total = unpack_state(state[unit])
+        totals = jnp.where(together, jnp.broadcast_to(total, (PAIR, PAIR)), 0.0)
+        high, low = split(jnp.concatenate([square, totals], axis=0))
+        query = wd[index, columns]
+        both = dot_nt(
+            jnp.concatenate([query, query], axis=1), jnp.concatenate([high, low], axis=1)
+        )
+        denom = gatt[index, columns] + both[:, PAIR:]
+        attended = (gmixed[index, columns] + both[:, :PAIR]) / denom
+        tile, within = stage_place(unit)
+        stage[tile, index, within] = attended
+        stage[2 + tile, index, within] = denom
+        att_low[index, columns] = attended.astype(BF16)
+
+    def stage_place(unit):
+        pair = lax.rem(unit, 8)
+        return lax.div(pair, 4), pl.ds(pl.multiple_of(lax.rem(pair, 4) * PAIR, PAIR), PAIR)
+
     mixed = gatt
-    loads = []
-    moves = ((w_out, wo), (w_up, wu), (w_down, wd), (cot_in, cot_cat))
-    for slot in (0, 1, 3, 2):
-        loads.append(pltpu.make_async_copy(*moves[slot], wsem.at[slot]))
-        loads[-1].start()
-    outs = []
-
-    def leave(source, target):
-        outs.append(pltpu.make_async_copy(source, target, osem.at[len(outs)]))
-        outs[-1].start()
-
-    cot = cot_cat.at[own]
-    swap = Swap(place, stage, swap_sent, swap_came)
-    loads[0].wait()
-
-    def mix(columns):
-        mixed[:, columns] = x[:, columns].astype(F32) + dot_nn(att_low[...], wo[:, columns])
-
-    for_columns(1024, TILE, mix)
-
-    def norm_step(index):
-        scaled, _ = norm_rows(mixed[index, :])
-        norm_cat[index, :] = (scaled * gain[...] + shift[...]).astype(BF16)
-
-    for_rows(rows, norm_step)
-    met(len(others))
-    loads[1].wait()
-
-    def up(columns):
-        ours, ours_slope = gelu_both(dot_nn(norm_cat[own, :], wu[:, columns]))
-        hidden[:, columns] = ours
-        slope[:, columns] = ours_slope
-        return ours
+
+    def up(columns, index):
+        ours, ours_slope = gelu_both(dot_nn(norm_cat[index, :], wu[:, columns]))
+        hidden[index, columns] = ours
+        slope[index, columns] = ours_slope
+
+    settle(qkv_leaves)
+    swap.drain(range(4), land.at[0])
+    att_leaves = []
+    for half in range(2):
+        scan.finish(half)
+        leave(state.at[pl.ds(half * 8, 8)], state_out.at[pl.ds(half * 8, 8)])
+
+        def several(index, carry):
+            incoming(half * 8 + 2 * index)
+            incoming(half * 8 + 2 * index + 1)
+            return carry
+
+        lax.fori_loop(0, 4, several, 0)
+        part = pl.ds(half * block, block)
+        for slot in range(4):
+            target = (att_out, den_out)[slot // 2].at[part, pl.ds(slot % 2 * TILE, TILE)]
+            att_leaves.append(leave(stage.at[slot, part], target))
+        if half == 0:
+            out_load.wait()
+
+        def mix(columns):
+            mixed[part, columns] = x[part, columns].astype(F32) + dot_nn(att_low[part, :], wo[:, columns])
+
+        mix(pl.ds(0, 1024))
+        for start in range(0, block, ROWS):
+            index = pl.ds(half * block + start, ROWS)
+            scaled, _ = norm_rows(mixed[index, :])
+            norm_cat[index, :] = (scaled * gain[...] + shift[...]).astype(BF16)
+        if half == 0:
+            up_load.wait()
+            for_columns(4096, 1024, lambda columns: up(columns, part))
+    down_load = load(w_down, wd, 5)
+    late = pl.ds(block, block)
+    scan.drain()
+    pl.semaphore_signal(free, inc=1, device_id=place.partner(), device_id_type=MESH)
+    settle(att_leaves)
+    pl.semaphore_wait(free, 1)
 
     def nth_block(index):
         return lax.rem(place.at[0] + jnp.where(index == 2, 3, jnp.maximum(2 - index, 0)), RING)
 
     def give(index, carry):
-        theirs = up(half_columns(nth_block(index), 1 - core, 1024))
-        swap.put(index, index, theirs, land.at[index])
+        columns = half_columns(nth_block(index), 1 - core, 1024)
+        up(columns, late)
+        swap.put(4 + index, index, hidden[:, columns], land.at[index])
         return carry
 
     lax.fori_loop(0, 4, give, 0)
-    loads[2].wait()
 
     def take(index, carry):
-        block = nth_block(index)
-        ours = up(half_columns(block, core, 1024))
-        both = jnp.concatenate([ours, swap.get(index, land.at[index])], axis=0)
+        block_x = nth_block(index)
+        columns = half_columns(block_x, core, 1024)
+        up(columns, late)
+        both = jnp.concatenate([hidden[:, columns], swap.get(4 + index, land.at[index])], axis=0)
         for half in range(2):
             columns = pl.ds(half * TILE, TILE)
             product = tn_dot(both, cot_cat[:, columns]).reshape(4, 4, 4, 8, TILE)
             for stream in range(3):
-                slabs[stream][block, :, :, :, columns] = product[:, :, stream]
+                slabs[stream][block_x, :, :, :, columns] = product[:, :, stream]
             last = product[:, :, 3]
             if half == 0:
-                slab_a[block, :, :, :, pl.ds(1024, 384)] = last[..., :384]
-                slab_b[block, :, :, :, pl.ds(1024, 128)] = last[..., 384:]
+                slab_a[block_x, :, :, :, pl.ds(1024, 384)] = last[..., :384]
+                slab_b[block_x, :, :, :, pl.ds(1024, 128)] = last[..., 384:]
             else:
-                slab_b[block, :, :, :, pl.ds(1152, 256)] = last[..., :256]
-                slab_c[block, :, :, :, pl.ds(1024, 256)] = last[..., 256:]
+                slab_b[block_x, :, :, :, pl.ds(1152, 256)] = last[..., :256]
+                slab_c[block_x, :, :, :, pl.ds(1024, 256)] = last[..., 256:]
         return carry
 
     kinds = (None, SplitPhase, SplitPhase)
     down = [Stream(place, slabs[k], ORDERS[k], phases[k], kinds[k]) for k in range(3)]
-    first, *split = [stream.prepare() for stream in down]
+    lead, *others_two = [stream.prepare() for stream in down]
     lax.fori_loop(0, 2, take, 0)
-    first.begin_far()
-    for phase in split:
+    lead.begin_far()
+    for phase in others_two:
         phase.begin_first()
-    first.begin_near(0)
+    lead.begin_near(0)
     lax.fori_loop(2, 4, take, 0)
-    for phase in split:
+    for phase in others_two:
         phase.begin_second()
-    first.begin_near(1)
+    lead.begin_near(1)
     pl.semaphore_signal(free, inc=1, device_id=place.partner(), device_id_type=MESH)
     for tile in range(2):
         columns = pl.ds(tile * TILE, TILE)
-        swap.put(4 + tile, tile, norm_cat[own, columns], land_norm.at[tile], before=tile)
-    loads[3].wait()
+        swap.put(8 + tile, tile, norm_cat[own, columns], land_norm.at[tile], before=4 + tile)
+    down_load.wait()
+    cot = cot_cat.at[own]
 
     def finish_forward(columns):
         output[:, columns] = (mixed[:, columns] + dot_nn(hidden[...], wd[:, columns])).astype(BF16)
@@ -1045,7 +1027,8 @@
     leave(output, output_out)
 
     def back(columns):
-        grad = dot_nt(cot[...], wd[columns, :]) * slope[:, columns].astype(F32)
+        held = slope[:, columns].astype(jnp.int32).astype(F32) * (1.0 / SLOPE_SCALE)
+        grad = dot_nt(cot[...], wd[columns, :]) * held
         low = grad.astype(BF16)
         hidden[:, columns] = low
         return low
@@ -1054,8 +1037,8 @@
 
     def give_back(block, carry):
         theirs = back(half_columns(block, 1 - core, 1024))
-        before = jnp.where(block < 2, 4 + block, block)
-        swap.put(6 + block, block, theirs, land.at[block], before=before)
+        before = jnp.where(block < 2, 8 + block, 4 + block)
+        swap.put(10 + block, block, theirs, land.at[block], before=before)
         return carry
 
     lax.fori_loop(0, 4, give_back, 0)
@@ -1065,6 +1048,7 @@
         pre_cat[own, columns] = back(half_columns(block, core, 1024))
         return carry
 
+    settle(cat_leaves)
     lax.fori_loop(0, 4, keep_back, 0)
     for stream in down:
         stream.forward()
@@ -1076,18 +1060,17 @@
 
     def take_back(block, carry):
         columns = pl.ds(pl.multiple_of(block * TILE, TILE), TILE)
-        pre_cat[other, columns] = swap.get(6 + block, land.at[block])
+        pre_cat[other, columns] = swap.get(10 + block, land.at[block])
         return carry
 
     lax.fori_loop(0, 4, take_back, 0)
     leave(pre_cat, pre_out)
     for tile in range(2):
         columns = pl.ds(tile * TILE, TILE)
-        norm_cat[other, columns] = swap.get(4 + tile, land_norm.at[tile])
-        swap.put(10 + tile, tile, att_low[:, columns], land_att.at[tile], before=6 + tile)
+        norm_cat[other, columns] = swap.get(8 + tile, land_norm.at[tile])
+        swap.put(14 + tile, tile, att_low[:, columns], land_att.at[tile], before=10 + tile)
     leave(norm_cat, norm_out)
-    query_load = pltpu.make_async_copy(qkv_in.at[0], slope.at[:, pl.ds(0, 1024)], wsem.at[4])
-    query_load.start()
+    query_load = load(qkv_out.at[0], wd.at[own], 7)
     pl.semaphore_signal(free, inc=1, device_id=place.partner(), device_id_type=MESH)
     def store(index, values):
         gmixed[index, :] = values
@@ -1096,7 +1079,7 @@
     norm_back_rows(mixed, gmixed, cot, gain, sums, store)
     leave(gmixed, gmixed_out)
     pl.semaphore_wait(free, 1)
-    swap.put(12, 2, hidden[:, half_tile(0, 1 - core)], land_norm.at[0], before=8)
+    swap.put(16, 2, hidden[:, half_tile(0, 1 - core)], land_norm.at[0], before=12)
 
     def back_out(columns):
         gatt[:, columns] = dot_nt(hidden[:, pl.ds(0, 1024)], wo[columns, :])
@@ -1105,20 +1088,19 @@
 
     def load_state(slots):
         for slot in slots:
-            source = (att_in, den_in)[slot // 2].at[:, pl.ds(slot % 2 * TILE, TILE)]
-            state_loads.append(pltpu.make_async_copy(source, stage.at[slot], wsem.at[5 + slot]))
-            state_loads[-1].start()
-
-    for number, slot in ((9, 3), (10, 0), (11, 1)):
+            source = (att_out, den_out)[slot // 2].at[:, pl.ds(slot % 2 * TILE, TILE)]
+            state_loads.append(load(source, stage.at[slot], 8 + slot))
+
+    for number, slot in ((13, 3), (14, 0), (15, 1)):
         swap.copy(number, slot, land_norm.at[0]).wait_send()
     load_state((0, 1, 3))
     for_columns(1024, TILE, back_out)
     ours = hidden[:, half_tile(0, core)]
-    swap.copy(12, 2, land_norm.at[0]).wait_send()
+    swap.copy(16, 2, land_norm.at[0]).wait_send()
     load_state((2,))
-    theirs = swap.get(12, land_norm.at[0])
+    theirs = swap.get(16, land_norm.at[0])
     for tile in range(2):
-        swap.copy(10 + tile, tile, land_att.at[tile]).wait_recv()
+        swap.copy(14 + tile, tile, land_att.at[tile]).wait_recv()
         for part, (start, width) in enumerate(((0, 384), (384, 128))):
             product = tn_dot(att_low[:, pl.ds(tile * TILE + start, width)], ours)
             theirs_att = land_att[tile, :, pl.ds(start, width)].astype(BF16)
@@ -1126,21 +1108,19 @@
             leave(land.at[2 * tile + part, pl.ds(0, width)], out_out.at[pl.ds(tile * TILE + start, width)])
     for copy in state_loads:
         copy.wait()
-    first_wide = first_head(block_rows)
-
-    def local_state(unit):
-        index, columns = unit_slices(unit, block_rows)
-        pair = lax.rem(unit, 8)
-        within = pl.ds(pl.multiple_of(lax.rem(pair, 4) * PAIR, PAIR), PAIR)
-        tile = lax.div(pair, 4)
+    first_wide = first_head(block)
+
+    def state_back(unit):
+        index, columns = unit_slices(unit, block)
+        tile, within = stage_place(unit)
         numer = gatt[index, columns] / stage[2 + tile, index, within]
         gatt[index, columns] = numer
-        query = features(slope[index, columns].astype(F32))
+        query = features(wd[index, columns].astype(F32))
         blocks, row = state_gradient(query, numer, stage[tile, index, within], first_wide)
         terms[unit, pl.ds(0, 64)] = blocks
         terms[unit, pl.ds(64, 8)] = row
 
-    for_units(local_state, 2)
+    for_units(state_back, 2)
     leave(gatt, gn_out)
     for stream, target in zip(down, (down_a, down_b, down_c)):
         stream.finish()
@@ -1148,7 +1128,8 @@
     for stream in down:
         stream.drain()
     for copy in outs:
-        copy.wait()
+        if id(copy) not in settled:
+            copy.wait()
 
 
 def slab_shapes(widths):
@@ -1176,10 +1157,15 @@
     )(*operands)
 
 
-def feed_forward(x, att_low, gain, shift, cot_cat, w_out, w_up, w_down, qkv, att, den, block):
+def front(x, gain_one, shift_one, gain, shift, w_qkv, cot, w_out, w_up, w_down, block):
     rows, width = x.shape
     wide = w_up.shape[1]
     outs = [
+        struct((2, 2 * rows, width // 2), BF16),
+        struct((3, rows, width), BF16),
+        struct((rows, width)),
+        struct((rows, width)),
+        struct((SEQ, 72, PAIR)),
         struct((rows, width), BF16),
         struct((rows, width)),
         struct((rows, width)),
@@ -1194,32 +1180,35 @@
         pltpu.VMEM((width, width), BF16),
         pltpu.VMEM((width, wide), BF16),
         pltpu.VMEM((wide, width), BF16),
-        pltpu.SemaphoreType.DMA((9,)),
         pltpu.SemaphoreType.DMA((12,)),
+        pltpu.SemaphoreType.DMA((28,)),
+        pltpu.VMEM((rows, width), BF16),
+        SCAN_SCRATCH[0],
         pltpu.VMEM((rows, width), BF16),
         pltpu.VMEM((rows, width), F32),
         pltpu.VMEM((rows, width), F32),
         pltpu.VMEM((2 * rows, width), BF16),
         pltpu.VMEM((2 * rows, wide // 2), BF16),
         pltpu.VMEM((rows, wide), BF16),
-        pltpu.VMEM((rows, wide), BF16),
+        pltpu.VMEM((rows, wide), jnp.int16),
         pltpu.VMEM((2 * rows, width), BF16),
         pltpu.VMEM((4, rows, TILE), F32),
         pltpu.VMEM((4, rows, TILE), F32),
         pltpu.VMEM((2, rows, TILE), F32),
         pltpu.VMEM((2, rows, TILE), F32),
-        pltpu.SemaphoreType.DMA((13,)),
-        pltpu.SemaphoreType.DMA((13,)),
+        pltpu.SemaphoreType.DMA((17,)),
+        pltpu.SemaphoreType.DMA((17,)),
         pltpu.SemaphoreType.REGULAR,
+        *SCAN_SCRATCH[3:],
         *slab_shapes(DOWN_WIDTHS),
         *flatten([[phase_scratch(2, length, 12)] for length in DOWN_WIDTHS]),
     ]
-    specs = [VMEM_SPEC] * 4 + [ANY_SPEC] * 7
-    out_specs = [ANY_SPEC] * 3 + [VMEM_SPEC] + [ANY_SPEC] * 3 + [VMEM_SPEC] + [ANY_SPEC] * 3
-    operands = (x, att_low, gain, shift, cot_cat, w_out, w_up, w_down, qkv, att, den)
+    specs = [VMEM_SPEC] * 5 + [ANY_SPEC] * 5
+    out_specs = [ANY_SPEC] * 8 + [VMEM_SPEC] + [ANY_SPEC] * 3 + [VMEM_SPEC] + [ANY_SPEC] * 3
+    operands = (x, gain_one, shift_one, gain, shift, w_qkv, cot, w_out, w_up, w_down)
 
     def kernel(*refs):
-        feed_forward_kernel(block, *refs)
+        front_kernel(block, *refs)
 
     return call(kernel, outs, out_specs, operands, specs, scratch, 1)
 
@@ -1279,7 +1268,7 @@
     s = {name: take(like[name]) for name in like}
     qkv, att, gn, grads = s["qkv"], s["att"], s["gn"], s["grads"]
     slabs = s["slabs"]
-    scan = Scan(*s["scan"][:4], s["scan"][4:], True)
+    scan = Scan(*[Slots(ref) for ref in s["scan"][:4]], s["scan"][4:], True)
     across = [place.neighbour(0, step) for step in (1, -1, 2)]
     beside = []
     for axis in range(3):
@@ -1297,7 +1286,7 @@
         loads.append(copy)
         return copy
 
-    started = load(terms_in, scan.terms)
+    started = load(terms_in, scan.terms.ref)
     out_loads = []
     for k in (0, 2, 1):
         for which, start, length, at in stream_pieces(k, OUT_WIDTHS, TILE):
@@ -1415,7 +1404,7 @@
 
     def incoming(unit):
         index, columns = unit_slices(unit, block)
-        square, total = unpack_state(scan.result[unit])
+        square, total = unpack_state(scan.result.ref[unit])
         high, low = split(square)
         raw_key = qkv[1, index, columns].astype(F32)
         key, value = features(raw_key), qkv[2, index, columns]
@@ -1592,11 +1581,9 @@
     cot = cotangent.reshape(rows, width)
     gain_one, gain_two = first_gain.reshape(1, width), second_gain.reshape(1, width)
     shift_two = second_shift.reshape(1, width)
-    norm_one, cot_cat, qkv, att, att_low, den, state = attention_forward(
-        x, first_gain, first_shift, qkv_weight, cot, block
-    )
-    output, gmixed, gn, sums_two, norm_cat, pre_cat, out, terms, *down = feed_forward(
-        x, att_low, gain_two, shift_two, cot_cat, out_weight, up_weight, down_weight, qkv, att, den, block
+    shift_one = first_shift.reshape(1, width)
+    norm_one, qkv, att, _, state, output, gmixed, gn, sums_two, norm_cat, pre_cat, out, terms, *down = front(
+        x, gain_one, shift_one, gain_two, shift_two, qkv_weight, cot, out_weight, up_weight, down_weight, block
     )
     grads = last_part(
         qkv, att, terms, state, gn, gmixed, norm_one, norm_cat, pre_cat, down, out, x, qkv_weight,

time: 173 us -> 170 us (0.983)
  Pallas kernels: 171 us -> 167 us
    pallas_call x1 -> x0, Pallas kernels: 32 us -> none  [attention_forward(): pl.pallas_call(kernel, out_shape=[struct((2, 2 * rows, width // 2), BF16)...]
    pallas_call x2, Pallas kernels: 135 us -> 163 us  [call(): pl.pallas_call(kernel, out_shape=outs, in_specs=in_specs, out_specs=out_s...]
where the time goes in v7:
time: 170 us; the launch traced here: 168 us
  Pallas kernels  167 us (98%)
    pallas_call x2, Pallas kernels, call(): pl.pallas_call(kernel, out_shape=outs, in_specs=in_specs, out_specs=out_s...  163 us

profile of v7, /device:TPU:0, one launch (start us, length us, event | category | flops | bytes accessed | tf_op | source)
XLA Modules:
  0.0 167.6 jit_solution(6693768396243653632)
XLA Ops:
  0.6 72.1 %shard_map.177 = (bf16[2,768,512]{2,1,0:T(8,128)(2,1)}, bf16[3,384,1024]{2,1,0:T(8,128)(2,1)}, f32[384,1024]{1,0:T(8,128)}, f32[384,1024]{1,0:T(8,128)}, f32[16,...) custom-call(bf16[384,1024]{1,0:T(8,128)(2,1)} %bitcast.13, ...), custom_call_target="tpu_custom_call" | custom-call | tf_op jit(solution)/shard_map/pallas_call | solution.py:1148
  72.8 91.2 %shard_map.178 = (f32[384,1024]{1,0:T(8,128)}, f32[8,4096]{1,0:T(8,128)}, f32[8,1024]{1,0:T(8,128)}, f32[8,3072]{1,0:T(8,128)}, f32[32,1024]{1,0:T(8,128)}, /*index=5*/f32[8,128]{1,0:T(8,128)}) custom-call(bf16[3,384,1024]{2,1,0:T(8,128)(2,1)} %get-tuple-element.42.refs_0_, f32[384,1024]{1,0:T(8,128)} %get-tuple-element.43.refs_1_, ...), custom_call_target="tpu_custom_call" | custom-call | tf_op jit(solution)/shard_map/pallas_call | solution.py:1148
  164.0 3.4 %shard_map.179 = (bf16[384,1024]{1,0:T(8,128)(2,1)}, f32[384,1024]{1,0:T(8,128)}, f32[8,4096]{1,0:T(8,128)}, f32[8,1024]{1,0:T(8,128)}, f32[8,3072]{1,0:T(8,128)...) custom-call(bf16[384,1024]{1,0:T(8,128)(2,1)} %get-tuple-element.41.output, ...), custom_call_target="tpu_custom_call" | custom-call | tf_op jit(solution)/shard_map/pallas_call | solution.py:1557

commit v8 on v7

--- a/solution.py
+++ b/solution.py
@@ -646,23 +646,22 @@
             device_id_type=MESH,
         )
 
-    def start(self):
-        for half in range(2):
-            for y, z in self.half_offsets(half):
-                other = self.at(y, z)
-                source = self.terms.at(self.unit_of(half, other))
-                copy = self.copy(y * RING + z, source, self.landed.at(self.me), self.sems[:2], other)
-                if y:
-                    copy.start()
-                else:
-                    pl.when(z > 0)(copy.start)
-        self.landed.at(self.me)[...] = self.terms.at(self.unit)[...]
+    def start(self, half):
+        for y, z in self.half_offsets(half):
+            other = self.at(y, z)
+            source = self.terms.at(self.unit_of(half, other))
+            copy = self.copy(y * RING + z, source, self.landed.at(self.me), self.sems[:2], other)
+            if y:
+                copy.start()
+            else:
+                pl.when(z > 0)(copy.start)
 
     def middle(self):
         for y, z in OFFSETS:
             other = self.at(y, z, -1)
             came = self.landed.at(other)
             self.copy(y * RING + z, came, came, self.sems[:2], other).wait_recv()
+        self.landed.at(self.me)[...] = self.terms.at(self.unit)[...]
         total = jnp.zeros((72, PAIR), F32)
         for k in range(SEQ):
             at = SEQ - 1 - k if self.reverse else k
@@ -857,9 +856,19 @@
         terms[unit, pl.ds(0, 64)] = blocks
         terms[unit, pl.ds(64, 8)] = row
 
-    for_units(local_state, 4)
+    def local_states(half):
+        def four(index, carry):
+            for offset in range(4):
+                local_state(half * 8 + index * 4 + offset)
+            return carry
+
+        lax.fori_loop(0, 2, four, 0)
+
+    local_states(0)
     met(len(others))
-    scan.start()
+    scan.start(0)
+    local_states(1)
+    scan.start(1)
     swap = Swap(place, stage, swap_sent, swap_came)
     for which in range(2):
         for block_x in range(4):
@@ -963,9 +972,7 @@
             norm_cat[index, :] = (scaled * gain[...] + shift[...]).astype(BF16)
         if half == 0:
             up_load.wait()
-            for_columns(4096, 1024, lambda columns: up(columns, part))
     down_load = load(w_down, wd, 5)
-    late = pl.ds(block, block)
     scan.drain()
     pl.semaphore_signal(free, inc=1, device_id=place.partner(), device_id_type=MESH)
     settle(att_leaves)
@@ -976,7 +983,7 @@
 
     def give(index, carry):
         columns = half_columns(nth_block(index), 1 - core, 1024)
-        up(columns, late)
+        up(columns, own)
         swap.put(4 + index, index, hidden[:, columns], land.at[index])
         return carry
 
@@ -985,7 +992,7 @@
     def take(index, carry):
         block_x = nth_block(index)
         columns = half_columns(block_x, core, 1024)
-        up(columns, late)
+        up(columns, own)
         both = jnp.concatenate([hidden[:, columns], swap.get(4 + index, land.at[index])], axis=0)
         for half in range(2):
             columns = pl.ds(half * TILE, TILE)
@@ -1333,7 +1340,8 @@
     met(len(others))
     go((begin, out, 0))
     started.wait()
-    scan.start()
+    scan.start(0)
+    scan.start(1)
     go((begin, out, 2))
     settle(up_loads)
     for k in range(3):
@@ -1361,11 +1369,13 @@
         grad_query, grad_key, grad_value = 0.0, 0.0, 0.0
         for head, (mask, slope) in enumerate(((first, one), (second, two))):
             mask_wide = jnp.concatenate([mask, mask], axis=1)
-            mixing = jnp.where(causal, dot_nt(wide * mask_wide, values) + slope, 0.0).astype(BF16)
+            mixing = split(jnp.where(causal, dot_nt(wide * mask_wide, values) + slope, 0.0))
             turned = jnp.where(causal_t, scores[head * block : (head + 1) * block], 0.0)
-            grad_query = grad_query + dot_nn(mixing, key * mask)
-            grad_key = grad_key + tn_dot(mixing, query * mask)
-            grad_value = grad_value + dot_nn(turned.astype(BF16), high * mask)
+            for part in mixing:
+                grad_query = grad_query + dot_nn(part, key * mask)
+                grad_key = grad_key + tn_dot(part, query * mask)
+            both = dot_nn(turned.astype(BF16), wide * mask_wide)
+            grad_value = grad_value + both[:, :PAIR] + both[:, PAIR:]
         square, total = unpack_state(s["state"][unit])
         state_high, state_low = split(square)
         grad_query = grad_query + dot_nn(wide, jnp.concatenate([state_high, state_high], axis=0))

time: 170 us -> 168 us (0.988)
  Pallas kernels: 167 us -> 165 us
    pallas_call x2, Pallas kernels: 163 us -> 162 us  [call(): pl.pallas_call(kernel, out_shape=outs, in_specs=in_specs, out_specs=out_s...]
where the time goes in v8:
time: 168 us; the launch traced here: 166 us
  Pallas kernels  165 us (98%)
    pallas_call x2, Pallas kernels, call(): pl.pallas_call(kernel, out_shape=outs, in_specs=in_specs, out_specs=out_s...  162 us
    pallas_call x1, Pallas kernels, lay_out(): pl.pallas_call(lay_out_kernel, out_shape=outs, in_specs=[VMEM_SPEC] * 7,...  3.38 us

profile of v8, /device:TPU:0, one launch (start us, length us, event | category | flops | bytes accessed | tf_op | source)
XLA Modules:
  0.0 165.8 jit_solution(15535335233982868812)
XLA Ops:
  0.6 69.8 %shard_map.177 = (bf16[2,768,512]{2,1,0:T(8,128)(2,1)}, bf16[3,384,1024]{2,1,0:T(8,128)(2,1)}, f32[384,1024]{1,0:T(8,128)}, f32[384,1024]{1,0:T(8,128)}, f32[16,...) custom-call(bf16[384,1024]{1,0:T(8,128)(2,1)} %bitcast.13, ...), custom_call_target="tpu_custom_call" | custom-call | tf_op jit(solution)/shard_map/pallas_call | solution.py:1155
  70.5 91.8 %shard_map.178 = (f32[384,1024]{1,0:T(8,128)}, f32[8,4096]{1,0:T(8,128)}, f32[8,1024]{1,0:T(8,128)}, f32[8,3072]{1,0:T(8,128)}, f32[32,1024]{1,0:T(8,128)}, /*index=5*/f32[8,128]{1,0:T(8,128)}) custom-call(bf16[3,384,1024]{2,1,0:T(8,128)(2,1)} %get-tuple-element.42.refs_0_, f32[384,1024]{1,0:T(8,128)} %get-tuple-element.43.refs_1_, ...), custom_call_target="tpu_custom_call" | custom-call | tf_op jit(solution)/shard_map/pallas_call | solution.py:1155
  162.2 3.4 %shard_map.179 = (bf16[384,1024]{1,0:T(8,128)(2,1)}, f32[384,1024]{1,0:T(8,128)}, f32[8,4096]{1,0:T(8,128)}, f32[8,1024]{1,0:T(8,128)}, f32[8,3072]{1,0:T(8,128)...) custom-call(bf16[384,1024]{1,0:T(8,128)(2,1)} %get-tuple-element.41.output, ...), custom_call_target="tpu_custom_call" | custom-call | tf_op jit(solution)/shard_map/pallas_call | solution.py:1567

commit v9 on v8

--- a/solution.py
+++ b/solution.py
@@ -753,7 +753,7 @@
     cumulative = 0.5 * (1.0 + lax.erf(pre * (1.0 / math.sqrt(2.0))))
     density = jnp.exp(-0.5 * pre * pre) * (1.0 / math.sqrt(2.0 * math.pi))
     slope = (cumulative + pre * density) * SLOPE_SCALE
-    return (pre * cumulative).astype(BF16), jnp.round(slope).astype(jnp.int32).astype(jnp.int16)
+    return (pre * cumulative).astype(BF16), slope.astype(jnp.int32).astype(jnp.int16)
 
 
 def norm_back(grad, gain, scaled, inverse):
@@ -950,11 +950,11 @@
         leave(state.at[pl.ds(half * 8, 8)], state_out.at[pl.ds(half * 8, 8)])
 
         def several(index, carry):
-            incoming(half * 8 + 2 * index)
-            incoming(half * 8 + 2 * index + 1)
+            for offset in range(4):
+                incoming(half * 8 + 4 * index + offset)
             return carry
 
-        lax.fori_loop(0, 4, several, 0)
+        lax.fori_loop(0, 2, several, 0)
         part = pl.ds(half * block, block)
         for slot in range(4):
             target = (att_out, den_out)[slot // 2].at[part, pl.ds(slot % 2 * TILE, TILE)]
@@ -1549,28 +1549,46 @@
     return call(kernel, outs, out_specs, operands, specs, scratch, 2)
 
 
-def lay_out_kernel(output, grad_input, up, out, qkv, down, gains, output_to, grad_to, up_to, out_to, qkv_to, down_to, a, b, c, d):
-    pairs = (
-        (output, output_to), (grad_input, grad_to), (up, up_to), (out, out_to), (qkv, qkv_to), (down, down_to),
-    )
-    for source, target in pairs:
-        target[...] = source[...]
+PARTS = (4, 4, 1, 1, 1, 1)
+
+
+def lay_out_kernel(core_gains, *refs):
+    count = len(PARTS)
+    sources, targets, gains = refs[:count], refs[count : 2 * count], refs[2 * count : 2 * count + 4]
+    held, (into, out_of) = refs[2 * count + 4 : 3 * count + 4], refs[3 * count + 4 :]
+    moves = []
+    for k in (1, 0, 2, 3, 4, 5):
+        rows = sources[k].shape[0] // PARTS[k]
+        for part in range(PARTS[k]):
+            index, number = pl.ds(part * rows, rows), len(moves)
+            load = pltpu.make_async_copy(sources[k].at[index], held[k].at[index], into.at[number])
+            leave = pltpu.make_async_copy(held[k].at[index], targets[k].at[index], out_of.at[number])
+            load.start()
+            moves.append((load, leave))
+    for load, leave in moves:
+        load.wait()
+        leave.start()
     core = lax.rem(lax.axis_index("dp"), 2)
-    turned = jnp.transpose(jnp.concatenate([gains[...], jnp.zeros((120, 128), F32)], axis=0))
-    for k, target in enumerate((a, b, c, d)):
+    turned = jnp.transpose(jnp.concatenate([core_gains[...], jnp.zeros((120, 128), F32)], axis=0))
+    for k, target in enumerate(gains):
         target[...] = jnp.where(core == 0, turned[k : k + 1, :8], turned[4 + k : 5 + k, :8])
-
-
-def lay_out(output, *grads):
-    arrays = (output, *grads[:-1])
-    outs = [struct(array.shape, array.dtype) for array in arrays] + [struct((1, 8))] * 4
+    for _, leave in moves:
+        leave.wait()
+
+
+def lay_out(gains, *arrays):
     return pl.pallas_call(
         lay_out_kernel,
-        out_shape=outs,
-        in_specs=[VMEM_SPEC] * 7,
-        out_specs=[VMEM_SPEC] * 10,
+        out_shape=[struct(array.shape, array.dtype) for array in arrays] + [struct((1, 8))] * 4,
+        in_specs=[VMEM_SPEC] + [ANY_SPEC] * len(PARTS),
+        out_specs=[ANY_SPEC] * len(PARTS) + [VMEM_SPEC] * 4,
+        scratch_shapes=[
+            *[pltpu.VMEM(array.shape, array.dtype) for array in arrays],
+            pltpu.SemaphoreType.DMA((sum(PARTS),)),
+            pltpu.SemaphoreType.DMA((sum(PARTS),)),
+        ],
         compiler_params=pltpu.CompilerParams(vmem_limit_bytes=62 * MIB),
-    )(output, *grads)
+    )(gains, *arrays)
 
 
 def body(
@@ -1599,7 +1617,8 @@
         qkv, att, terms, state, gn, gmixed, norm_one, norm_cat, pre_cat, down, out, x, qkv_weight,
         gain_one, sums_two, block,
     )
-    output, grad_input, grad_up, grad_out, grad_qkv, grad_down, *gains = lay_out(output, *grads)
+    *grads, gains = grads
+    output, grad_input, grad_up, grad_out, grad_qkv, grad_down, *gains = lay_out(gains, output, *grads)
     return (
         output.reshape(inputs.shape),
         grad_input.reshape(inputs.shape),

time: 168 us -> 168 us (level)
  no operation moved by 1% of the time
where the time goes in v9:
time: 168 us; the launch traced here: 166 us
  Pallas kernels  165 us (98%)
    pallas_call x2, Pallas kernels, call(): pl.pallas_call(kernel, out_shape=outs, in_specs=in_specs, out_specs=out_s...  161 us
    pallas_call x1, Pallas kernels, lay_out(): pl.pallas_call(lay_out_kernel, out_shape=[struct(array.shape, array.dtype...  3.92 us

profile of v9, /device:TPU:0, one launch (start us, length us, event | category | flops | bytes accessed | tf_op | source)
XLA Modules:
  0.0 165.9 jit_solution(4430018858499469125)
XLA Ops:
  0.6 69.2 %shard_map.177 = (bf16[2,768,512]{2,1,0:T(8,128)(2,1)}, bf16[3,384,1024]{2,1,0:T(8,128)(2,1)}, f32[384,1024]{1,0:T(8,128)}, f32[384,1024]{1,0:T(8,128)}, f32[16,...) custom-call(bf16[384,1024]{1,0:T(8,128)(2,1)} %bitcast.13, ...), custom_call_target="tpu_custom_call" | custom-call | tf_op jit(solution)/shard_map/pallas_call | solution.py:1155
  69.9 92.0 %shard_map.178 = (f32[384,1024]{1,0:T(8,128)}, f32[8,4096]{1,0:T(8,128)}, f32[8,1024]{1,0:T(8,128)}, f32[8,3072]{1,0:T(8,128)}, f32[32,1024]{1,0:T(8,128)}, /*index=5*/f32[8,128]{1,0:T(8,128)}) custom-call(bf16[3,384,1024]{2,1,0:T(8,128)(2,1)} %get-tuple-element.41.refs_0_, f32[384,1024]{1,0:T(8,128)} %get-tuple-element.42.refs_1_, ...), custom_call_target="tpu_custom_call" | custom-call | tf_op jit(solution)/shard_map/pallas_call | solution.py:1155
  161.8 3.9 %shard_map.179 = (bf16[384,1024]{1,0:T(8,128)(2,1)}, f32[384,1024]{1,0:T(8,128)}, f32[8,4096]{1,0:T(8,128)}, f32[8,1024]{1,0:T(8,128)}, f32[8,3072]{1,0:T(8,128)...) custom-call(f32[8,128]{1,0:T(8,128)} %get-tuple-element.55.core_gains, ...), custom_call_target="tpu_custom_call" | custom-call | tf_op jit(solution)/shard_map/pallas_call | solution.py:1580

commit v10 on v8

--- a/solution.py
+++ b/solution.py
@@ -753,7 +753,7 @@
     cumulative = 0.5 * (1.0 + lax.erf(pre * (1.0 / math.sqrt(2.0))))
     density = jnp.exp(-0.5 * pre * pre) * (1.0 / math.sqrt(2.0 * math.pi))
     slope = (cumulative + pre * density) * SLOPE_SCALE
-    return (pre * cumulative).astype(BF16), jnp.round(slope).astype(jnp.int32).astype(jnp.int16)
+    return (pre * cumulative).astype(BF16), slope.astype(jnp.int32).astype(jnp.int16)
 
 
 def norm_back(grad, gain, scaled, inverse):
@@ -950,11 +950,11 @@
         leave(state.at[pl.ds(half * 8, 8)], state_out.at[pl.ds(half * 8, 8)])
 
         def several(index, carry):
-            incoming(half * 8 + 2 * index)
-            incoming(half * 8 + 2 * index + 1)
+            for offset in range(4):
+                incoming(half * 8 + 4 * index + offset)
             return carry
 
-        lax.fori_loop(0, 4, several, 0)
+        lax.fori_loop(0, 2, several, 0)
         part = pl.ds(half * block, block)
         for slot in range(4):
             target = (att_out, den_out)[slot // 2].at[part, pl.ds(slot % 2 * TILE, TILE)]

time: 168 us -> 167 us (level)
  no operation moved by 1% of the time
where the time goes in v10:
time: 167 us; the launch traced here: 165 us
  Pallas kernels  165 us (99%)
    pallas_call x2, Pallas kernels, call(): pl.pallas_call(kernel, out_shape=outs, in_specs=in_specs, out_specs=out_s...  161 us
    pallas_call x1, Pallas kernels, lay_out(): pl.pallas_call(lay_out_kernel, out_shape=outs, in_specs=[VMEM_SPEC] * 7,...  3.38 us

profile of v10, /device:TPU:0, one launch (start us, length us, event | category | flops | bytes accessed | tf_op | source)
XLA Modules:
  0.0 165.4 jit_solution(11308233391892650803)
XLA Ops:
  0.6 69.2 %shard_map.177 = (bf16[2,768,512]{2,1,0:T(8,128)(2,1)}, bf16[3,384,1024]{2,1,0:T(8,128)(2,1)}, f32[384,1024]{1,0:T(8,128)}, f32[384,1024]{1,0:T(8,128)}, f32[16,...) custom-call(bf16[384,1024]{1,0:T(8,128)(2,1)} %bitcast.13, ...), custom_call_target="tpu_custom_call" | custom-call | tf_op jit(solution)/shard_map/pallas_call | solution.py:1155
  69.9 92.0 %shard_map.178 = (f32[384,1024]{1,0:T(8,128)}, f32[8,4096]{1,0:T(8,128)}, f32[8,1024]{1,0:T(8,128)}, f32[8,3072]{1,0:T(8,128)}, f32[32,1024]{1,0:T(8,128)}, /*index=5*/f32[8,128]{1,0:T(8,128)}) custom-call(bf16[3,384,1024]{2,1,0:T(8,128)(2,1)} %get-tuple-element.42.refs_0_, f32[384,1024]{1,0:T(8,128)} %get-tuple-element.43.refs_1_, ...), custom_call_target="tpu_custom_call" | custom-call | tf_op jit(solution)/shard_map/pallas_call | solution.py:1155
  161.8 3.4 %shard_map.179 = (bf16[384,1024]{1,0:T(8,128)(2,1)}, f32[384,1024]{1,0:T(8,128)}, f32[8,4096]{1,0:T(8,128)}, f32[8,1024]{1,0:T(8,128)}, f32[8,3072]{1,0:T(8,128)...) custom-call(bf16[384,1024]{1,0:T(8,128)(2,1)} %get-tuple-element.41.output, ...), custom_call_target="tpu_custom_call" | custom-call | tf_op jit(solution)/shard_map/pallas_call | solution.py:1567
